TPU v7x, 1024 devices: a whole 4x4x32 slice. The times are simulated.
1024 devices in a mesh: row: 32 (over y, z_hi, core), col: 32 (over z_lo, x).
Axes of the slice: x: 4, y: 4, z: 32 (z_hi: 4, z_lo: 8; z = z_hi * 8 + z_lo), core: 2. Of those that a mesh axis runs over, the one named last changes fastest.
Arguments:
- left_tiles: bfloat16 [32, 32, 3, 128, 128], P('col', 'row'), may hold values from -0.5 to 0.5
- left_index: int32 [32, 32, 2, 3], P('col', 'row'), may hold values from -1 to 511, as said below
- right_tiles: bfloat16 [32, 32, 4, 128, 128], P('row', 'col'), may hold values from -6 to 6
- right_index: int32 [32, 32, 2, 4], P('row', 'col'), may hold values from -1 to 511, as said below
- keep_mask: int32 [32, 128], P('col', 'row'), may hold values 0 or 1
Outputs:
- product: bfloat16 [4096, 16384], P('col', 'row')
Inputs may be any that keep to these rules, and one draw needn't show every extreme that they name: `left_index`: A slot is empty when both entries are -1, else its block-row lies in 0 to 0 and its block-column k satisfies k % 32 = (c + r) % 32 for the slot held at [c, r]. No two slots of one panel name the same block. Panels hold 1 or 3 tiles in their first slots; panel [0, 0] and some others are full. `right_index`: A slot is empty when both entries are -1, else its block-column lies in 0 to 3 and its block-row k satisfies k % 32 = (c + r) % 32 for the slot held at [r, c]. No two slots of one panel name the same block. Panels hold 1 or 4 tiles in their first slots; panel [0, 0] and some others are full.
All inputs are finite; a program needn't handle non-finite values. No bound on the sum of `keep_mask` on one device may be relied on, other than what follows from the above.
Results may differ from a plain program's by a relative error of at most 0.001.
Values may be sent and summed in bfloat16 or wider, within the bound.
No kernel may reach another device: no remote copies, remote signals or barrier semaphores. Data moves between devices by JAX's collectives and lax.ppermute only.
A program may use at most 32 MiB of HBM per device.

v0:
```python
import jax
import jax.numpy as jnp
from jax import lax
from jax.sharding import PartitionSpec as P


def shortened(shard):
    return jax.tree.map(lambda a: a.astype(jnp.bfloat16) if a.dtype == jnp.float32 else a, shard)


def passed_along(block, axis, distance):
    devices = range(lax.axis_size(axis))
    route = [((i - distance) % len(devices), i) for i in devices]
    return lax.ppermute(block, axis, route)


def on_device(left_tiles, left_index, right_tiles, right_index, keep_mask):
    rows_dev = keep_mask.shape[0]
    cols_dev = keep_mask.shape[1]
    tile_size = left_tiles.shape[-1]
    left_slots = left_tiles.shape[2]
    col_count = lax.axis_size("col")
    half_turns = col_count // 2

    def multiply(summed, left_part, left_ids, right_part, right_ids):
        left_block = left_part[0, 0]
        right_block = right_part[0, 0]
        left_rows = left_ids[0, 0, 0]
        left_keys = left_ids[0, 0, 1]
        right_keys = right_ids[0, 0, 0]
        right_cols = right_ids[0, 0, 1]
        matched = ((left_keys[:, None] == right_keys[None, :]) & (left_keys[:, None] >= 0)).astype(
            jnp.bfloat16
        )
        placed = (right_cols[:, None] == jnp.arange(cols_dev, dtype=jnp.int32)[None, :]).astype(
            jnp.bfloat16
        )
        strips = jnp.einsum(
            "ab,bj,bxy->axjy", matched, placed, right_block, preferred_element_type=jnp.float32
        )
        strips = strips.astype(jnp.bfloat16).reshape(left_slots * tile_size, cols_dev * tile_size)
        chosen = (left_rows[:, None] == jnp.arange(rows_dev, dtype=jnp.int32)[None, :]).astype(
            jnp.bfloat16
        )
        stacked = jnp.einsum("ai,axy->ixay", chosen, left_block, preferred_element_type=jnp.float32)
        stacked = stacked.astype(jnp.bfloat16).reshape(rows_dev, tile_size, left_slots * tile_size)
        return summed + jnp.einsum(
            "ixk,kz->ixz", stacked, strips, preferred_element_type=jnp.float32
        )

    def advance(panels, offset):
        left_part, left_ids, right_part, right_ids = panels
        left_part, left_ids = (
            passed_along(left_part, "row", offset),
            passed_along(shortened(left_ids), "row", offset).astype(left_ids.dtype),
        )
        right_part, right_ids = (
            passed_along(right_part, "col", offset),
            passed_along(shortened(right_ids), "col", offset).astype(right_ids.dtype),
        )
        return (left_part, left_ids, right_part, right_ids)

    initial = (left_tiles, left_index, right_tiles, right_index)
    summed = jnp.zeros((rows_dev, tile_size, cols_dev * tile_size), jnp.float32)
    summed = multiply(summed, *initial)

    def two_steps(step_index, carry_state):
        summed, panels = carry_state
        panels = advance(panels, 1)
        summed = multiply(summed, *panels)
        panels = advance(panels, 1)
        summed = multiply(summed, *panels)
        return (summed, panels)

    summed, panels = lax.fori_loop(0, half_turns - 1, two_steps, (summed, initial))
    panels = advance(panels, 1)
    summed = multiply(summed, *panels)
    summed = summed.reshape(rows_dev, tile_size, cols_dev, tile_size)
    summed = summed * keep_mask[:, None, :, None].astype(jnp.float32)
    return summed.reshape(rows_dev * tile_size, cols_dev * tile_size).astype(jnp.bfloat16)


def solution(mesh):
    in_specs = (
        P("col", "row", None, None, None),
        P("col", "row", None, None),
        P("row", "col", None, None, None),
        P("row", "col", None, None),
        P("col", "row"),
    )
    out_specs = P("col", "row")
    return jax.shard_map(
        on_device, mesh=mesh, in_specs=in_specs, out_specs=out_specs, check_vma=False
    )
```

profile of v0, /device:TPU:1, one launch (start us, length us, event | category | flops | bytes accessed | tf_op | source)
XLA Modules:
  0.0 860.7 jit_solution(18106289245779109622)
XLA Ops:
  3.3 831.6 %while.18 = (s32[]{:T(128)}, f32[1,128,512]{2,1,0:T(8,128)S(1)}, bf16[1,1,3,128,128]{3,4,2,1,0:T(8,128)(2,1)S(1)}, s32[1,1,2,3]{3,2,1,0:T(2,128)S(1)}, bf16[1,1,...) while((s32[]{:T(128)}, f32[1,128,512]{2,1,0:T(8,128)S(1)}, ...), condition=%wide.region_1.0_spmd, body=%wide.region_0.0_spmd.sunk | while | flops 104628480 | bytes 5310081 | solution.py:75
  3.3 16.8 %collective-permute-start.2 = (s32[1,1,2,3]{3,2,1,0:T(2,128)S(1)}, s32[1,1,2,3]{3,2,1,0:T(2,128)S(1)}, u32[]{:S(2)}, u32[]{:S(2)}) collective-permute-start(s32[1,1,2,3]{3,2,1,0:T(2,128)S(1)} %get-tuple-element.133), channel_id=1, source_target_pairs={{992,0},{0,32},{32,64},{64,96},{96,128},{128,160},{160,192},{192,2... | collective-permute-start | bytes 80 | tf_op jit(solution)/shard_map/while/body/eval_jaxpr/ppermute | solution.py:14
  28.9 15.3 %collective-permute-start.3 = (s32[1,1,2,3]{3,2,1,0:T(2,128)S(1)}, s32[1,1,2,3]{3,2,1,0:T(2,128)S(1)}, u32[]{:S(2)}, u32[]{:S(2)}) collective-permute-start(s32[1,1,2,3]{3,2,1,0:T(2,128)S(1)} %collective-permute-done.2), channel_id=1, source_target_pairs={{992,0},{0,32},{32,64},{64,96},{96,128},{128,160},{160,192},{192,2... | collective-permute-start | bytes 80 | tf_op jit(solution)/shard_map/while/body/eval_jaxpr/ppermute | solution.py:14
  47.2 10.1 %collective-permute-done.7 = s32[1,1,2,4]{3,2,1,0:T(2,128)S(1)} collective-permute-done((s32[1,1,2,4]{3,2,1,0:T(2,128)S(1)}, s32[1,1,2,4]{3,2,1,0:T(2,128)S(1)}, u32[]{:S(2)}, u32[]{:S(2)}) %collective-permute-start.7) | collective-permute-done | bytes 64 | tf_op jit(solution)/shard_map/while/body/eval_jaxpr/ppermute | solution.py:14
  66.8 9.4 %collective-permute-done.5 = bf16[1,1,4,128,128]{4,2,3,1,0:T(4,128)(2,1)S(1)} collective-permute-done((bf16[1,1,4,128,128]{4,2,3,1,0:T(4,128)(2,1)S(1)}, bf16[1,1,4,128,128]{4,2,3,1,0:T(4,128)(2,1)S(1)}, u32[]{:S(2)}, u32[]{:S(2)}) %collective-permute-start.5) | collective-permute-done | bytes 131104 | tf_op jit(solution)/shard_map/while/body/eval_jaxpr/ppermute | solution.py:14
  77.1 5.7 collective-permute-start.2
  89.1 7.3 collective-permute-start.3
  98.5 11.1 %collective-permute-done.7 = s32[1,1,2,4]{3,2,1,0:T(2,128)S(1)} collective-permute-done((s32[1,1,2,4]{3,2,1,0:T(2,128)S(1)}, s32[1,1,2,4]{3,2,1,0:T(2,128)S(1)}, u32[]{:S(2)}, u32[]{:S(2)}) %collective-permute-start.7) | collective-permute-done | bytes 64 | tf_op jit(solution)/shard_map/while/body/eval_jaxpr/ppermute | solution.py:14
  116.2 12.3 %collective-permute-done.5 = bf16[1,1,4,128,128]{4,2,3,1,0:T(4,128)(2,1)S(1)} collective-permute-done((bf16[1,1,4,128,128]{4,2,3,1,0:T(4,128)(2,1)S(1)}, bf16[1,1,4,128,128]{4,2,3,1,0:T(4,128)(2,1)S(1)}, u32[]{:S(2)}, u32[]{:S(2)}) %collective-permute-start.5) | collective-permute-done | bytes 131104 | tf_op jit(solution)/shard_map/while/body/eval_jaxpr/ppermute | solution.py:14
  129.3 5.5 collective-permute-start.2
  141.1 10.1 %collective-permute-start.3 = (s32[1,1,2,3]{3,2,1,0:T(2,128)S(1)}, s32[1,1,2,3]{3,2,1,0:T(2,128)S(1)}, u32[]{:S(2)}, u32[]{:S(2)}) collective-permute-start(s32[1,1,2,3]{3,2,1,0:T(2,128)S(1)} %collective-permute-done.2), channel_id=1, source_target_pairs={{992,0},{0,32},{32,64},{64,96},{96,128},{128,160},{160,192},{192,2... | collective-permute-start | bytes 80 | tf_op jit(solution)/shard_map/while/body/eval_jaxpr/ppermute | solution.py:14
  153.3 11.1 %collective-permute-done.7 = s32[1,1,2,4]{3,2,1,0:T(2,128)S(1)} collective-permute-done((s32[1,1,2,4]{3,2,1,0:T(2,128)S(1)}, s32[1,1,2,4]{3,2,1,0:T(2,128)S(1)}, u32[]{:S(2)}, u32[]{:S(2)}) %collective-permute-start.7) | collective-permute-done | bytes 64 | tf_op jit(solution)/shard_map/while/body/eval_jaxpr/ppermute | solution.py:14
  170.5 12.7 %collective-permute-done.5 = bf16[1,1,4,128,128]{4,2,3,1,0:T(4,128)(2,1)S(1)} collective-permute-done((bf16[1,1,4,128,128]{4,2,3,1,0:T(4,128)(2,1)S(1)}, bf16[1,1,4,128,128]{4,2,3,1,0:T(4,128)(2,1)S(1)}, u32[]{:S(2)}, u32[]{:S(2)}) %collective-permute-start.5) | collective-permute-done | bytes 131104 | tf_op jit(solution)/shard_map/while/body/eval_jaxpr/ppermute | solution.py:14
  184.1 9.1 %collective-permute-start.2 = (s32[1,1,2,3]{3,2,1,0:T(2,128)S(1)}, s32[1,1,2,3]{3,2,1,0:T(2,128)S(1)}, u32[]{:S(2)}, u32[]{:S(2)}) collective-permute-start(s32[1,1,2,3]{3,2,1,0:T(2,128)S(1)} %get-tuple-element.133), channel_id=1, source_target_pairs={{992,0},{0,32},{32,64},{64,96},{96,128},{128,160},{160,192},{192,2... | collective-permute-start | bytes 80 | tf_op jit(solution)/shard_map/while/body/eval_jaxpr/ppermute | solution.py:14
  199.1 7.8 collective-permute-start.3
  209.0 11.1 %collective-permute-done.7 = s32[1,1,2,4]{3,2,1,0:T(2,128)S(1)} collective-permute-done((s32[1,1,2,4]{3,2,1,0:T(2,128)S(1)}, s32[1,1,2,4]{3,2,1,0:T(2,128)S(1)}, u32[]{:S(2)}, u32[]{:S(2)}) %collective-permute-start.7) | collective-permute-done | bytes 64 | tf_op jit(solution)/shard_map/while/body/eval_jaxpr/ppermute | solution.py:14
  226.2 12.8 %collective-permute-done.5 = bf16[1,1,4,128,128]{4,2,3,1,0:T(4,128)(2,1)S(1)} collective-permute-done((bf16[1,1,4,128,128]{4,2,3,1,0:T(4,128)(2,1)S(1)}, bf16[1,1,4,128,128]{4,2,3,1,0:T(4,128)(2,1)S(1)}, u32[]{:S(2)}, u32[]{:S(2)}) %collective-permute-start.5) | collective-permute-done | bytes 131104 | tf_op jit(solution)/shard_map/while/body/eval_jaxpr/ppermute | solution.py:14
  239.8 6.3 collective-permute-start.2
  253.0 6.7 collective-permute-start.3
  261.8 11.1 %collective-permute-done.7 = s32[1,1,2,4]{3,2,1,0:T(2,128)S(1)} collective-permute-done((s32[1,1,2,4]{3,2,1,0:T(2,128)S(1)}, s32[1,1,2,4]{3,2,1,0:T(2,128)S(1)}, u32[]{:S(2)}, u32[]{:S(2)}) %collective-permute-start.7) | collective-permute-done | bytes 64 | tf_op jit(solution)/shard_map/while/body/eval_jaxpr/ppermute | solution.py:14
  272.9 4.7 collective-permute-start.1
  280.0 12.1 %collective-permute-done.5 = bf16[1,1,4,128,128]{4,2,3,1,0:T(4,128)(2,1)S(1)} collective-permute-done((bf16[1,1,4,128,128]{4,2,3,1,0:T(4,128)(2,1)S(1)}, bf16[1,1,4,128,128]{4,2,3,1,0:T(4,128)(2,1)S(1)}, u32[]{:S(2)}, u32[]{:S(2)}) %collective-permute-start.5) | collective-permute-done | bytes 131104 | tf_op jit(solution)/shard_map/while/body/eval_jaxpr/ppermute | solution.py:14
  293.0 7.9 collective-permute-start.2
  306.8 7.8 collective-permute-start.3
  316.7 11.1 %collective-permute-done.7 = s32[1,1,2,4]{3,2,1,0:T(2,128)S(1)} collective-permute-done((s32[1,1,2,4]{3,2,1,0:T(2,128)S(1)}, s32[1,1,2,4]{3,2,1,0:T(2,128)S(1)}, u32[]{:S(2)}, u32[]{:S(2)}) %collective-permute-start.7) | collective-permute-done | bytes 64 | tf_op jit(solution)/shard_map/while/body/eval_jaxpr/ppermute | solution.py:14
  333.9 12.8 %collective-permute-done.5 = bf16[1,1,4,128,128]{4,2,3,1,0:T(4,128)(2,1)S(1)} collective-permute-done((bf16[1,1,4,128,128]{4,2,3,1,0:T(4,128)(2,1)S(1)}, bf16[1,1,4,128,128]{4,2,3,1,0:T(4,128)(2,1)S(1)}, u32[]{:S(2)}, u32[]{:S(2)}) %collective-permute-start.5) | collective-permute-done | bytes 131104 | tf_op jit(solution)/shard_map/while/body/eval_jaxpr/ppermute | solution.py:14
  347.5 8.2 collective-permute-start.2
  361.7 7.7 collective-permute-start.3
  371.5 11.1 %collective-permute-done.7 = s32[1,1,2,4]{3,2,1,0:T(2,128)S(1)} collective-permute-done((s32[1,1,2,4]{3,2,1,0:T(2,128)S(1)}, s32[1,1,2,4]{3,2,1,0:T(2,128)S(1)}, u32[]{:S(2)}, u32[]{:S(2)}) %collective-permute-start.7) | collective-permute-done | bytes 64 | tf_op jit(solution)/shard_map/while/body/eval_jaxpr/ppermute | solution.py:14
  389.2 12.2 %collective-permute-done.5 = bf16[1,1,4,128,128]{4,2,3,1,0:T(4,128)(2,1)S(1)} collective-permute-done((bf16[1,1,4,128,128]{4,2,3,1,0:T(4,128)(2,1)S(1)}, bf16[1,1,4,128,128]{4,2,3,1,0:T(4,128)(2,1)S(1)}, u32[]{:S(2)}, u32[]{:S(2)}) %collective-permute-start.5) | collective-permute-done | bytes 131104 | tf_op jit(solution)/shard_map/while/body/eval_jaxpr/ppermute | solution.py:14
  402.3 6.7 collective-permute-start.2
  415.7 6.9 collective-permute-start.3
  424.6 11.1 %collective-permute-done.7 = s32[1,1,2,4]{3,2,1,0:T(2,128)S(1)} collective-permute-done((s32[1,1,2,4]{3,2,1,0:T(2,128)S(1)}, s32[1,1,2,4]{3,2,1,0:T(2,128)S(1)}, u32[]{:S(2)}, u32[]{:S(2)}) %collective-permute-start.7) | collective-permute-done | bytes 64 | tf_op jit(solution)/shard_map/while/body/eval_jaxpr/ppermute | solution.py:14
  442.7 12.1 %collective-permute-done.5 = bf16[1,1,4,128,128]{4,2,3,1,0:T(4,128)(2,1)S(1)} collective-permute-done((bf16[1,1,4,128,128]{4,2,3,1,0:T(4,128)(2,1)S(1)}, bf16[1,1,4,128,128]{4,2,3,1,0:T(4,128)(2,1)S(1)}, u32[]{:S(2)}, u32[]{:S(2)}) %collective-permute-start.5) | collective-permute-done | bytes 131104 | tf_op jit(solution)/shard_map/while/body/eval_jaxpr/ppermute | solution.py:14
  455.7 7.6 collective-permute-start.2
  469.2 7.7 collective-permute-start.3
  479.0 11.1 %collective-permute-done.7 = s32[1,1,2,4]{3,2,1,0:T(2,128)S(1)} collective-permute-done((s32[1,1,2,4]{3,2,1,0:T(2,128)S(1)}, s32[1,1,2,4]{3,2,1,0:T(2,128)S(1)}, u32[]{:S(2)}, u32[]{:S(2)}) %collective-permute-start.7) | collective-permute-done | bytes 64 | tf_op jit(solution)/shard_map/while/body/eval_jaxpr/ppermute | solution.py:14
  496.2 12.7 %collective-permute-done.5 = bf16[1,1,4,128,128]{4,2,3,1,0:T(4,128)(2,1)S(1)} collective-permute-done((bf16[1,1,4,128,128]{4,2,3,1,0:T(4,128)(2,1)S(1)}, bf16[1,1,4,128,128]{4,2,3,1,0:T(4,128)(2,1)S(1)}, u32[]{:S(2)}, u32[]{:S(2)}) %collective-permute-start.5) | collective-permute-done | bytes 131104 | tf_op jit(solution)/shard_map/while/body/eval_jaxpr/ppermute | solution.py:14
  509.8 7.4 collective-permute-start.2
  523.4 7.3 collective-permute-start.3
  532.8 11.1 %collective-permute-done.7 = s32[1,1,2,4]{3,2,1,0:T(2,128)S(1)} collective-permute-done((s32[1,1,2,4]{3,2,1,0:T(2,128)S(1)}, s32[1,1,2,4]{3,2,1,0:T(2,128)S(1)}, u32[]{:S(2)}, u32[]{:S(2)}) %collective-permute-start.7) | collective-permute-done | bytes 64 | tf_op jit(solution)/shard_map/while/body/eval_jaxpr/ppermute | solution.py:14
  550.5 12.3 %collective-permute-done.5 = bf16[1,1,4,128,128]{4,2,3,1,0:T(4,128)(2,1)S(1)} collective-permute-done((bf16[1,1,4,128,128]{4,2,3,1,0:T(4,128)(2,1)S(1)}, bf16[1,1,4,128,128]{4,2,3,1,0:T(4,128)(2,1)S(1)}, u32[]{:S(2)}, u32[]{:S(2)}) %collective-permute-start.5) | collective-permute-done | bytes 131104 | tf_op jit(solution)/shard_map/while/body/eval_jaxpr/ppermute | solution.py:14
  563.6 6.6 collective-permute-start.2
  577.2 6.7 collective-permute-start.3
  586.1 11.1 %collective-permute-done.7 = s32[1,1,2,4]{3,2,1,0:T(2,128)S(1)} collective-permute-done((s32[1,1,2,4]{3,2,1,0:T(2,128)S(1)}, s32[1,1,2,4]{3,2,1,0:T(2,128)S(1)}, u32[]{:S(2)}, u32[]{:S(2)}) %collective-permute-start.7) | collective-permute-done | bytes 64 | tf_op jit(solution)/shard_map/while/body/eval_jaxpr/ppermute | solution.py:14
  604.7 11.7 %collective-permute-done.5 = bf16[1,1,4,128,128]{4,2,3,1,0:T(4,128)(2,1)S(1)} collective-permute-done((bf16[1,1,4,128,128]{4,2,3,1,0:T(4,128)(2,1)S(1)}, bf16[1,1,4,128,128]{4,2,3,1,0:T(4,128)(2,1)S(1)}, u32[]{:S(2)}, u32[]{:S(2)}) %collective-permute-start.5) | collective-permute-done | bytes 131104 | tf_op jit(solution)/shard_map/while/body/eval_jaxpr/ppermute | solution.py:14
  617.2 8.1 collective-permute-start.2
  631.2 7.8 collective-permute-start.3
  641.1 11.1 %collective-permute-done.7 = s32[1,1,2,4]{3,2,1,0:T(2,128)S(1)} collective-permute-done((s32[1,1,2,4]{3,2,1,0:T(2,128)S(1)}, s32[1,1,2,4]{3,2,1,0:T(2,128)S(1)}, u32[]{:S(2)}, u32[]{:S(2)}) %collective-permute-start.7) | collective-permute-done | bytes 64 | tf_op jit(solution)/shard_map/while/body/eval_jaxpr/ppermute | solution.py:14
  658.3 12.8 %collective-permute-done.5 = bf16[1,1,4,128,128]{4,2,3,1,0:T(4,128)(2,1)S(1)} collective-permute-done((bf16[1,1,4,128,128]{4,2,3,1,0:T(4,128)(2,1)S(1)}, bf16[1,1,4,128,128]{4,2,3,1,0:T(4,128)(2,1)S(1)}, u32[]{:S(2)}, u32[]{:S(2)}) %collective-permute-start.5) | collective-permute-done | bytes 131104 | tf_op jit(solution)/shard_map/while/body/eval_jaxpr/ppermute | solution.py:14
  671.9 6.9 collective-permute-start.2
  685.4 7.1 collective-permute-start.3
  694.6 11.1 %collective-permute-done.7 = s32[1,1,2,4]{3,2,1,0:T(2,128)S(1)} collective-permute-done((s32[1,1,2,4]{3,2,1,0:T(2,128)S(1)}, s32[1,1,2,4]{3,2,1,0:T(2,128)S(1)}, u32[]{:S(2)}, u32[]{:S(2)}) %collective-permute-start.7) | collective-permute-done | bytes 64 | tf_op jit(solution)/shard_map/while/body/eval_jaxpr/ppermute | solution.py:14
  712.5 12.1 %collective-permute-done.5 = bf16[1,1,4,128,128]{4,2,3,1,0:T(4,128)(2,1)S(1)} collective-permute-done((bf16[1,1,4,128,128]{4,2,3,1,0:T(4,128)(2,1)S(1)}, bf16[1,1,4,128,128]{4,2,3,1,0:T(4,128)(2,1)S(1)}, u32[]{:S(2)}, u32[]{:S(2)}) %collective-permute-start.5) | collective-permute-done | bytes 131104 | tf_op jit(solution)/shard_map/while/body/eval_jaxpr/ppermute | solution.py:14
  725.4 7.5 collective-permute-start.2
  739.5 7.1 collective-permute-start.3
  748.7 11.1 %collective-permute-done.7 = s32[1,1,2,4]{3,2,1,0:T(2,128)S(1)} collective-permute-done((s32[1,1,2,4]{3,2,1,0:T(2,128)S(1)}, s32[1,1,2,4]{3,2,1,0:T(2,128)S(1)}, u32[]{:S(2)}, u32[]{:S(2)}) %collective-permute-start.7) | collective-permute-done | bytes 64 | tf_op jit(solution)/shard_map/while/body/eval_jaxpr/ppermute | solution.py:14
  766.5 12.1 %collective-permute-done.5 = bf16[1,1,4,128,128]{4,2,3,1,0:T(4,128)(2,1)S(1)} collective-permute-done((bf16[1,1,4,128,128]{4,2,3,1,0:T(4,128)(2,1)S(1)}, bf16[1,1,4,128,128]{4,2,3,1,0:T(4,128)(2,1)S(1)}, u32[]{:S(2)}, u32[]{:S(2)}) %collective-permute-start.5) | collective-permute-done | bytes 131104 | tf_op jit(solution)/shard_map/while/body/eval_jaxpr/ppermute | solution.py:14
  779.5 8.8 %collective-permute-start.2 = (s32[1,1,2,3]{3,2,1,0:T(2,128)S(1)}, s32[1,1,2,3]{3,2,1,0:T(2,128)S(1)}, u32[]{:S(2)}, u32[]{:S(2)}) collective-permute-start(s32[1,1,2,3]{3,2,1,0:T(2,128)S(1)} %get-tuple-element.133), channel_id=1, source_target_pairs={{992,0},{0,32},{32,64},{64,96},{96,128},{128,160},{160,192},{192,2... | collective-permute-start | bytes 80 | tf_op jit(solution)/shard_map/while/body/eval_jaxpr/ppermute | solution.py:14
  794.3 7.7 collective-permute-start.3
  804.1 11.1 %collective-permute-done.7 = s32[1,1,2,4]{3,2,1,0:T(2,128)S(1)} collective-permute-done((s32[1,1,2,4]{3,2,1,0:T(2,128)S(1)}, s32[1,1,2,4]{3,2,1,0:T(2,128)S(1)}, u32[]{:S(2)}, u32[]{:S(2)}) %collective-permute-start.7) | collective-permute-done | bytes 64 | tf_op jit(solution)/shard_map/while/body/eval_jaxpr/ppermute | solution.py:14
  822.4 11.7 %collective-permute-done.5 = bf16[1,1,4,128,128]{4,2,3,1,0:T(4,128)(2,1)S(1)} collective-permute-done((bf16[1,1,4,128,128]{4,2,3,1,0:T(4,128)(2,1)S(1)}, bf16[1,1,4,128,128]{4,2,3,1,0:T(4,128)(2,1)S(1)}, u32[]{:S(2)}, u32[]{:S(2)}) %collective-permute-start.5) | collective-permute-done | bytes 131104 | tf_op jit(solution)/shard_map/while/body/eval_jaxpr/ppermute | solution.py:14
  834.9 8.2 collective-permute-start.9
  849.2 7.0 collective-permute-done.10
  (483 shorter events, 250.9 us)
Async XLA Ops:
  3.3 25.6 %collective-permute-start.2 = (s32[1,1,2,3]{3,2,1,0:T(2,128)S(1)}, s32[1,1,2,3]{3,2,1,0:T(2,128)S(1)}, u32[]{:S(2)}, u32[]{:S(2)}) collective-permute-start(s32[1,1,2,3]{3,2,1,0:T(2,128)S(1)} %get-tuple-element.133), channel_id=1, source_target_pairs={{992,0},{0,32},{32,64},{64,96},{96,128},{128,160},{160,192},{192,2... | collective-permute-start | bytes 80 | tf_op jit(solution)/shard_map/while/body/eval_jaxpr/ppermute | solution.py:14
  20.2 24.1 %collective-permute-start.6 = (s32[1,1,2,4]{3,2,1,0:T(2,128)S(1)}, s32[1,1,2,4]{3,2,1,0:T(2,128)S(1)}, u32[]{:S(2)}, u32[]{:S(2)}) collective-permute-start(s32[1,1,2,4]{3,2,1,0:T(2,128)S(1)} %get-tuple-element.135), channel_id=1, source_target_pairs={{31,0},{0,1},{1,2},{2,3},{3,4},{4,5},{5,6},{6,7},{7,8},{8,9},{9,10... | collective-permute-start | bytes 104 | tf_op jit(solution)/shard_map/while/body/eval_jaxpr/ppermute | solution.py:14
  23.3 37.9 %collective-permute-start.4 = (bf16[1,1,4,128,128]{4,2,3,1,0:T(4,128)(2,1)S(1)}, bf16[1,1,4,128,128]{4,2,3,1,0:T(4,128)(2,1)S(1)}, u32[]{:S(2)}, u32[]{:S(2)}) collective-permute-start(bf16[1,1,4,128,128]{4,2,3,1,0:T(4,128)(2,1)S(1)} %get-tuple-element.134), channel_id=1, source_target_pairs={{31,0},{0,1},{1,2},{2,3},{3,4},{4,5},{5,6},{6,7},{7,8},{8,9},{9,10... | collective-permute-start | bytes 393224 | tf_op jit(solution)/shard_map/while/body/eval_jaxpr/ppermute | solution.py:14
  26.4 31.0 %collective-permute-start = (bf16[1,1,3,128,128]{3,4,2,1,0:T(8,128)(2,1)S(1)}, bf16[1,1,3,128,128]{3,4,2,1,0:T(8,128)(2,1)S(1)}, u32[]{:S(2)}, u32[]{:S(2)}) collective-permute-start(bf16[1,1,3,128,128]{3,4,2,1,0:T(8,128)(2,1)S(1)} %get-tuple-element.132), channel_id=1, source_target_pairs={{992,0},{0,32},{32,64},{64,96},{96,128},{128,160},{160,192},{192,2... | collective-permute-start | bytes 294920 | tf_op jit(solution)/shard_map/while/body/eval_jaxpr/ppermute | solution.py:14
  28.9 18.3 %collective-permute-start.3 = (s32[1,1,2,3]{3,2,1,0:T(2,128)S(1)}, s32[1,1,2,3]{3,2,1,0:T(2,128)S(1)}, u32[]{:S(2)}, u32[]{:S(2)}) collective-permute-start(s32[1,1,2,3]{3,2,1,0:T(2,128)S(1)} %collective-permute-done.2), channel_id=1, source_target_pairs={{992,0},{0,32},{32,64},{64,96},{96,128},{128,160},{160,192},{192,2... | collective-permute-start | bytes 80 | tf_op jit(solution)/shard_map/while/body/eval_jaxpr/ppermute | solution.py:14
  61.2 15.1 %collective-permute-start.5 = (bf16[1,1,4,128,128]{4,2,3,1,0:T(4,128)(2,1)S(1)}, bf16[1,1,4,128,128]{4,2,3,1,0:T(4,128)(2,1)S(1)}, u32[]{:S(2)}, u32[]{:S(2)}) collective-permute-start(bf16[1,1,4,128,128]{4,2,3,1,0:T(4,128)(2,1)S(1)} %collective-permute-done.4), channel_id=1, source_target_pairs={{31,0},{0,1},{1,2},{2,3},{3,4},{4,5},{5,6},{6,7},{7,8},{8,9},{9,10... | collective-permute-start | bytes 393224 | tf_op jit(solution)/shard_map/while/body/eval_jaxpr/ppermute | solution.py:14
  84.7 29.1 %collective-permute-start.4 = (bf16[1,1,4,128,128]{4,2,3,1,0:T(4,128)(2,1)S(1)}, bf16[1,1,4,128,128]{4,2,3,1,0:T(4,128)(2,1)S(1)}, u32[]{:S(2)}, u32[]{:S(2)}) collective-permute-start(bf16[1,1,4,128,128]{4,2,3,1,0:T(4,128)(2,1)S(1)} %get-tuple-element.134), channel_id=1, source_target_pairs={{31,0},{0,1},{1,2},{2,3},{3,4},{4,5},{5,6},{6,7},{7,8},{8,9},{9,10... | collective-permute-start | bytes 393224 | tf_op jit(solution)/shard_map/while/body/eval_jaxpr/ppermute | solution.py:14
  86.6 23.0 %collective-permute-start = (bf16[1,1,3,128,128]{3,4,2,1,0:T(8,128)(2,1)S(1)}, bf16[1,1,3,128,128]{3,4,2,1,0:T(8,128)(2,1)S(1)}, u32[]{:S(2)}, u32[]{:S(2)}) collective-permute-start(bf16[1,1,3,128,128]{3,4,2,1,0:T(8,128)(2,1)S(1)} %get-tuple-element.132), channel_id=1, source_target_pairs={{992,0},{0,32},{32,64},{64,96},{96,128},{128,160},{160,192},{192,2... | collective-permute-start | bytes 294920 | tf_op jit(solution)/shard_map/while/body/eval_jaxpr/ppermute | solution.py:14
  113.8 14.6 %collective-permute-start.5 = (bf16[1,1,4,128,128]{4,2,3,1,0:T(4,128)(2,1)S(1)}, bf16[1,1,4,128,128]{4,2,3,1,0:T(4,128)(2,1)S(1)}, u32[]{:S(2)}, u32[]{:S(2)}) collective-permute-start(bf16[1,1,4,128,128]{4,2,3,1,0:T(4,128)(2,1)S(1)} %collective-permute-done.4), channel_id=1, source_target_pairs={{31,0},{0,1},{1,2},{2,3},{3,4},{4,5},{5,6},{6,7},{7,8},{8,9},{9,10... | collective-permute-start | bytes 393224 | tf_op jit(solution)/shard_map/while/body/eval_jaxpr/ppermute | solution.py:14
  134.8 16.4 %collective-permute-start.6 = (s32[1,1,2,4]{3,2,1,0:T(2,128)S(1)}, s32[1,1,2,4]{3,2,1,0:T(2,128)S(1)}, u32[]{:S(2)}, u32[]{:S(2)}) collective-permute-start(s32[1,1,2,4]{3,2,1,0:T(2,128)S(1)} %get-tuple-element.135), channel_id=1, source_target_pairs={{31,0},{0,1},{1,2},{2,3},{3,4},{4,5},{5,6},{6,7},{7,8},{8,9},{9,10... | collective-permute-start | bytes 104 | tf_op jit(solution)/shard_map/while/body/eval_jaxpr/ppermute | solution.py:14
  136.7 31.3 %collective-permute-start.4 = (bf16[1,1,4,128,128]{4,2,3,1,0:T(4,128)(2,1)S(1)}, bf16[1,1,4,128,128]{4,2,3,1,0:T(4,128)(2,1)S(1)}, u32[]{:S(2)}, u32[]{:S(2)}) collective-permute-start(bf16[1,1,4,128,128]{4,2,3,1,0:T(4,128)(2,1)S(1)} %get-tuple-element.134), channel_id=1, source_target_pairs={{31,0},{0,1},{1,2},{2,3},{3,4},{4,5},{5,6},{6,7},{7,8},{8,9},{9,10... | collective-permute-start | bytes 393224 | tf_op jit(solution)/shard_map/while/body/eval_jaxpr/ppermute | solution.py:14
  138.7 25.7 %collective-permute-start = (bf16[1,1,3,128,128]{3,4,2,1,0:T(8,128)(2,1)S(1)}, bf16[1,1,3,128,128]{3,4,2,1,0:T(8,128)(2,1)S(1)}, u32[]{:S(2)}, u32[]{:S(2)}) collective-permute-start(bf16[1,1,3,128,128]{3,4,2,1,0:T(8,128)(2,1)S(1)} %get-tuple-element.132), channel_id=1, source_target_pairs={{992,0},{0,32},{32,64},{64,96},{96,128},{128,160},{160,192},{192,2... | collective-permute-start | bytes 294920 | tf_op jit(solution)/shard_map/while/body/eval_jaxpr/ppermute | solution.py:14
  168.1 15.2 %collective-permute-start.5 = (bf16[1,1,4,128,128]{4,2,3,1,0:T(4,128)(2,1)S(1)}, bf16[1,1,4,128,128]{4,2,3,1,0:T(4,128)(2,1)S(1)}, u32[]{:S(2)}, u32[]{:S(2)}) collective-permute-start(bf16[1,1,4,128,128]{4,2,3,1,0:T(4,128)(2,1)S(1)} %collective-permute-done.4), channel_id=1, source_target_pairs={{31,0},{0,1},{1,2},{2,3},{3,4},{4,5},{5,6},{6,7},{7,8},{8,9},{9,10... | collective-permute-start | bytes 393224 | tf_op jit(solution)/shard_map/while/body/eval_jaxpr/ppermute | solution.py:14
  184.1 15.0 %collective-permute-start.2 = (s32[1,1,2,3]{3,2,1,0:T(2,128)S(1)}, s32[1,1,2,3]{3,2,1,0:T(2,128)S(1)}, u32[]{:S(2)}, u32[]{:S(2)}) collective-permute-start(s32[1,1,2,3]{3,2,1,0:T(2,128)S(1)} %get-tuple-element.133), channel_id=1, source_target_pairs={{992,0},{0,32},{32,64},{64,96},{96,128},{128,160},{160,192},{192,2... | collective-permute-start | bytes 80 | tf_op jit(solution)/shard_map/while/body/eval_jaxpr/ppermute | solution.py:14
  193.2 13.7 %collective-permute-start.6 = (s32[1,1,2,4]{3,2,1,0:T(2,128)S(1)}, s32[1,1,2,4]{3,2,1,0:T(2,128)S(1)}, u32[]{:S(2)}, u32[]{:S(2)}) collective-permute-start(s32[1,1,2,4]{3,2,1,0:T(2,128)S(1)} %get-tuple-element.135), channel_id=1, source_target_pairs={{31,0},{0,1},{1,2},{2,3},{3,4},{4,5},{5,6},{6,7},{7,8},{8,9},{9,10... | collective-permute-start | bytes 104 | tf_op jit(solution)/shard_map/while/body/eval_jaxpr/ppermute | solution.py:14
  195.1 28.7 %collective-permute-start.4 = (bf16[1,1,4,128,128]{4,2,3,1,0:T(4,128)(2,1)S(1)}, bf16[1,1,4,128,128]{4,2,3,1,0:T(4,128)(2,1)S(1)}, u32[]{:S(2)}, u32[]{:S(2)}) collective-permute-start(bf16[1,1,4,128,128]{4,2,3,1,0:T(4,128)(2,1)S(1)} %get-tuple-element.134), channel_id=1, source_target_pairs={{31,0},{0,1},{1,2},{2,3},{3,4},{4,5},{5,6},{6,7},{7,8},{8,9},{9,10... | collective-permute-start | bytes 393224 | tf_op jit(solution)/shard_map/while/body/eval_jaxpr/ppermute | solution.py:14
  197.0 23.1 %collective-permute-start = (bf16[1,1,3,128,128]{3,4,2,1,0:T(8,128)(2,1)S(1)}, bf16[1,1,3,128,128]{3,4,2,1,0:T(8,128)(2,1)S(1)}, u32[]{:S(2)}, u32[]{:S(2)}) collective-permute-start(bf16[1,1,3,128,128]{3,4,2,1,0:T(8,128)(2,1)S(1)} %get-tuple-element.132), channel_id=1, source_target_pairs={{992,0},{0,32},{32,64},{64,96},{96,128},{128,160},{160,192},{192,2... | collective-permute-start | bytes 294920 | tf_op jit(solution)/shard_map/while/body/eval_jaxpr/ppermute | solution.py:14
  223.8 15.1 %collective-permute-start.5 = (bf16[1,1,4,128,128]{4,2,3,1,0:T(4,128)(2,1)S(1)}, bf16[1,1,4,128,128]{4,2,3,1,0:T(4,128)(2,1)S(1)}, u32[]{:S(2)}, u32[]{:S(2)}) collective-permute-start(bf16[1,1,4,128,128]{4,2,3,1,0:T(4,128)(2,1)S(1)} %collective-permute-done.4), channel_id=1, source_target_pairs={{31,0},{0,1},{1,2},{2,3},{3,4},{4,5},{5,6},{6,7},{7,8},{8,9},{9,10... | collective-permute-start | bytes 393224 | tf_op jit(solution)/shard_map/while/body/eval_jaxpr/ppermute | solution.py:14
  248.0 29.7 %collective-permute-start.4 = (bf16[1,1,4,128,128]{4,2,3,1,0:T(4,128)(2,1)S(1)}, bf16[1,1,4,128,128]{4,2,3,1,0:T(4,128)(2,1)S(1)}, u32[]{:S(2)}, u32[]{:S(2)}) collective-permute-start(bf16[1,1,4,128,128]{4,2,3,1,0:T(4,128)(2,1)S(1)} %get-tuple-element.134), channel_id=1, source_target_pairs={{31,0},{0,1},{1,2},{2,3},{3,4},{4,5},{5,6},{6,7},{7,8},{8,9},{9,10... | collective-permute-start | bytes 393224 | tf_op jit(solution)/shard_map/while/body/eval_jaxpr/ppermute | solution.py:14
  249.9 23.0 %collective-permute-start = (bf16[1,1,3,128,128]{3,4,2,1,0:T(8,128)(2,1)S(1)}, bf16[1,1,3,128,128]{3,4,2,1,0:T(8,128)(2,1)S(1)}, u32[]{:S(2)}, u32[]{:S(2)}) collective-permute-start(bf16[1,1,3,128,128]{3,4,2,1,0:T(8,128)(2,1)S(1)} %get-tuple-element.132), channel_id=1, source_target_pairs={{992,0},{0,32},{32,64},{64,96},{96,128},{128,160},{160,192},{192,2... | collective-permute-start | bytes 294920 | tf_op jit(solution)/shard_map/while/body/eval_jaxpr/ppermute | solution.py:14
  277.7 14.4 %collective-permute-start.5 = (bf16[1,1,4,128,128]{4,2,3,1,0:T(4,128)(2,1)S(1)}, bf16[1,1,4,128,128]{4,2,3,1,0:T(4,128)(2,1)S(1)}, u32[]{:S(2)}, u32[]{:S(2)}) collective-permute-start(bf16[1,1,4,128,128]{4,2,3,1,0:T(4,128)(2,1)S(1)} %collective-permute-done.4), channel_id=1, source_target_pairs={{31,0},{0,1},{1,2},{2,3},{3,4},{4,5},{5,6},{6,7},{7,8},{8,9},{9,10... | collective-permute-start | bytes 393224 | tf_op jit(solution)/shard_map/while/body/eval_jaxpr/ppermute | solution.py:14
  293.0 13.9 %collective-permute-start.2 = (s32[1,1,2,3]{3,2,1,0:T(2,128)S(1)}, s32[1,1,2,3]{3,2,1,0:T(2,128)S(1)}, u32[]{:S(2)}, u32[]{:S(2)}) collective-permute-start(s32[1,1,2,3]{3,2,1,0:T(2,128)S(1)} %get-tuple-element.133), channel_id=1, source_target_pairs={{992,0},{0,32},{32,64},{64,96},{96,128},{128,160},{160,192},{192,2... | collective-permute-start | bytes 80 | tf_op jit(solution)/shard_map/while/body/eval_jaxpr/ppermute | solution.py:14
  300.9 13.7 %collective-permute-start.6 = (s32[1,1,2,4]{3,2,1,0:T(2,128)S(1)}, s32[1,1,2,4]{3,2,1,0:T(2,128)S(1)}, u32[]{:S(2)}, u32[]{:S(2)}) collective-permute-start(s32[1,1,2,4]{3,2,1,0:T(2,128)S(1)} %get-tuple-element.135), channel_id=1, source_target_pairs={{31,0},{0,1},{1,2},{2,3},{3,4},{4,5},{5,6},{6,7},{7,8},{8,9},{9,10... | collective-permute-start | bytes 104 | tf_op jit(solution)/shard_map/while/body/eval_jaxpr/ppermute | solution.py:14
  302.8 28.7 %collective-permute-start.4 = (bf16[1,1,4,128,128]{4,2,3,1,0:T(4,128)(2,1)S(1)}, bf16[1,1,4,128,128]{4,2,3,1,0:T(4,128)(2,1)S(1)}, u32[]{:S(2)}, u32[]{:S(2)}) collective-permute-start(bf16[1,1,4,128,128]{4,2,3,1,0:T(4,128)(2,1)S(1)} %get-tuple-element.134), channel_id=1, source_target_pairs={{31,0},{0,1},{1,2},{2,3},{3,4},{4,5},{5,6},{6,7},{7,8},{8,9},{9,10... | collective-permute-start | bytes 393224 | tf_op jit(solution)/shard_map/while/body/eval_jaxpr/ppermute | solution.py:14
  304.8 23.1 %collective-permute-start = (bf16[1,1,3,128,128]{3,4,2,1,0:T(8,128)(2,1)S(1)}, bf16[1,1,3,128,128]{3,4,2,1,0:T(8,128)(2,1)S(1)}, u32[]{:S(2)}, u32[]{:S(2)}) collective-permute-start(bf16[1,1,3,128,128]{3,4,2,1,0:T(8,128)(2,1)S(1)} %get-tuple-element.132), channel_id=1, source_target_pairs={{992,0},{0,32},{32,64},{64,96},{96,128},{128,160},{160,192},{192,2... | collective-permute-start | bytes 294920 | tf_op jit(solution)/shard_map/while/body/eval_jaxpr/ppermute | solution.py:14
  331.6 15.1 %collective-permute-start.5 = (bf16[1,1,4,128,128]{4,2,3,1,0:T(4,128)(2,1)S(1)}, bf16[1,1,4,128,128]{4,2,3,1,0:T(4,128)(2,1)S(1)}, u32[]{:S(2)}, u32[]{:S(2)}) collective-permute-start(bf16[1,1,4,128,128]{4,2,3,1,0:T(4,128)(2,1)S(1)} %collective-permute-done.4), channel_id=1, source_target_pairs={{31,0},{0,1},{1,2},{2,3},{3,4},{4,5},{5,6},{6,7},{7,8},{8,9},{9,10... | collective-permute-start | bytes 393224 | tf_op jit(solution)/shard_map/while/body/eval_jaxpr/ppermute | solution.py:14
  347.5 14.2 %collective-permute-start.2 = (s32[1,1,2,3]{3,2,1,0:T(2,128)S(1)}, s32[1,1,2,3]{3,2,1,0:T(2,128)S(1)}, u32[]{:S(2)}, u32[]{:S(2)}) collective-permute-start(s32[1,1,2,3]{3,2,1,0:T(2,128)S(1)} %get-tuple-element.133), channel_id=1, source_target_pairs={{992,0},{0,32},{32,64},{64,96},{96,128},{128,160},{160,192},{192,2... | collective-permute-start | bytes 80 | tf_op jit(solution)/shard_map/while/body/eval_jaxpr/ppermute | solution.py:14
  357.7 28.7 %collective-permute-start.4 = (bf16[1,1,4,128,128]{4,2,3,1,0:T(4,128)(2,1)S(1)}, bf16[1,1,4,128,128]{4,2,3,1,0:T(4,128)(2,1)S(1)}, u32[]{:S(2)}, u32[]{:S(2)}) collective-permute-start(bf16[1,1,4,128,128]{4,2,3,1,0:T(4,128)(2,1)S(1)} %get-tuple-element.134), channel_id=1, source_target_pairs={{31,0},{0,1},{1,2},{2,3},{3,4},{4,5},{5,6},{6,7},{7,8},{8,9},{9,10... | collective-permute-start | bytes 393224 | tf_op jit(solution)/shard_map/while/body/eval_jaxpr/ppermute | solution.py:14
  359.6 23.0 %collective-permute-start = (bf16[1,1,3,128,128]{3,4,2,1,0:T(8,128)(2,1)S(1)}, bf16[1,1,3,128,128]{3,4,2,1,0:T(8,128)(2,1)S(1)}, u32[]{:S(2)}, u32[]{:S(2)}) collective-permute-start(bf16[1,1,3,128,128]{3,4,2,1,0:T(8,128)(2,1)S(1)} %get-tuple-element.132), channel_id=1, source_target_pairs={{992,0},{0,32},{32,64},{64,96},{96,128},{128,160},{160,192},{192,2... | collective-permute-start | bytes 294920 | tf_op jit(solution)/shard_map/while/body/eval_jaxpr/ppermute | solution.py:14
  386.4 15.0 %collective-permute-start.5 = (bf16[1,1,4,128,128]{4,2,3,1,0:T(4,128)(2,1)S(1)}, bf16[1,1,4,128,128]{4,2,3,1,0:T(4,128)(2,1)S(1)}, u32[]{:S(2)}, u32[]{:S(2)}) collective-permute-start(bf16[1,1,4,128,128]{4,2,3,1,0:T(4,128)(2,1)S(1)} %collective-permute-done.4), channel_id=1, source_target_pairs={{31,0},{0,1},{1,2},{2,3},{3,4},{4,5},{5,6},{6,7},{7,8},{8,9},{9,10... | collective-permute-start | bytes 393224 | tf_op jit(solution)/shard_map/while/body/eval_jaxpr/ppermute | solution.py:14
  410.9 29.5 %collective-permute-start.4 = (bf16[1,1,4,128,128]{4,2,3,1,0:T(4,128)(2,1)S(1)}, bf16[1,1,4,128,128]{4,2,3,1,0:T(4,128)(2,1)S(1)}, u32[]{:S(2)}, u32[]{:S(2)}) collective-permute-start(bf16[1,1,4,128,128]{4,2,3,1,0:T(4,128)(2,1)S(1)} %get-tuple-element.134), channel_id=1, source_target_pairs={{31,0},{0,1},{1,2},{2,3},{3,4},{4,5},{5,6},{6,7},{7,8},{8,9},{9,10... | collective-permute-start | bytes 393224 | tf_op jit(solution)/shard_map/while/body/eval_jaxpr/ppermute | solution.py:14
  412.8 23.0 %collective-permute-start = (bf16[1,1,3,128,128]{3,4,2,1,0:T(8,128)(2,1)S(1)}, bf16[1,1,3,128,128]{3,4,2,1,0:T(8,128)(2,1)S(1)}, u32[]{:S(2)}, u32[]{:S(2)}) collective-permute-start(bf16[1,1,3,128,128]{3,4,2,1,0:T(8,128)(2,1)S(1)} %get-tuple-element.132), channel_id=1, source_target_pairs={{992,0},{0,32},{32,64},{64,96},{96,128},{128,160},{160,192},{192,2... | collective-permute-start | bytes 294920 | tf_op jit(solution)/shard_map/while/body/eval_jaxpr/ppermute | solution.py:14
  440.4 14.4 %collective-permute-start.5 = (bf16[1,1,4,128,128]{4,2,3,1,0:T(4,128)(2,1)S(1)}, bf16[1,1,4,128,128]{4,2,3,1,0:T(4,128)(2,1)S(1)}, u32[]{:S(2)}, u32[]{:S(2)}) collective-permute-start(bf16[1,1,4,128,128]{4,2,3,1,0:T(4,128)(2,1)S(1)} %collective-permute-done.4), channel_id=1, source_target_pairs={{31,0},{0,1},{1,2},{2,3},{3,4},{4,5},{5,6},{6,7},{7,8},{8,9},{9,10... | collective-permute-start | bytes 393224 | tf_op jit(solution)/shard_map/while/body/eval_jaxpr/ppermute | solution.py:14
  465.2 28.7 %collective-permute-start.4 = (bf16[1,1,4,128,128]{4,2,3,1,0:T(4,128)(2,1)S(1)}, bf16[1,1,4,128,128]{4,2,3,1,0:T(4,128)(2,1)S(1)}, u32[]{:S(2)}, u32[]{:S(2)}) collective-permute-start(bf16[1,1,4,128,128]{4,2,3,1,0:T(4,128)(2,1)S(1)} %get-tuple-element.134), channel_id=1, source_target_pairs={{31,0},{0,1},{1,2},{2,3},{3,4},{4,5},{5,6},{6,7},{7,8},{8,9},{9,10... | collective-permute-start | bytes 393224 | tf_op jit(solution)/shard_map/while/body/eval_jaxpr/ppermute | solution.py:14
  467.1 23.0 %collective-permute-start = (bf16[1,1,3,128,128]{3,4,2,1,0:T(8,128)(2,1)S(1)}, bf16[1,1,3,128,128]{3,4,2,1,0:T(8,128)(2,1)S(1)}, u32[]{:S(2)}, u32[]{:S(2)}) collective-permute-start(bf16[1,1,3,128,128]{3,4,2,1,0:T(8,128)(2,1)S(1)} %get-tuple-element.132), channel_id=1, source_target_pairs={{992,0},{0,32},{32,64},{64,96},{96,128},{128,160},{160,192},{192,2... | collective-permute-start | bytes 294920 | tf_op jit(solution)/shard_map/while/body/eval_jaxpr/ppermute | solution.py:14
  493.9 15.0 %collective-permute-start.5 = (bf16[1,1,4,128,128]{4,2,3,1,0:T(4,128)(2,1)S(1)}, bf16[1,1,4,128,128]{4,2,3,1,0:T(4,128)(2,1)S(1)}, u32[]{:S(2)}, u32[]{:S(2)}) collective-permute-start(bf16[1,1,4,128,128]{4,2,3,1,0:T(4,128)(2,1)S(1)} %collective-permute-done.4), channel_id=1, source_target_pairs={{31,0},{0,1},{1,2},{2,3},{3,4},{4,5},{5,6},{6,7},{7,8},{8,9},{9,10... | collective-permute-start | bytes 393224 | tf_op jit(solution)/shard_map/while/body/eval_jaxpr/ppermute | solution.py:14
  519.0 29.1 %collective-permute-start.4 = (bf16[1,1,4,128,128]{4,2,3,1,0:T(4,128)(2,1)S(1)}, bf16[1,1,4,128,128]{4,2,3,1,0:T(4,128)(2,1)S(1)}, u32[]{:S(2)}, u32[]{:S(2)}) collective-permute-start(bf16[1,1,4,128,128]{4,2,3,1,0:T(4,128)(2,1)S(1)} %get-tuple-element.134), channel_id=1, source_target_pairs={{31,0},{0,1},{1,2},{2,3},{3,4},{4,5},{5,6},{6,7},{7,8},{8,9},{9,10... | collective-permute-start | bytes 393224 | tf_op jit(solution)/shard_map/while/body/eval_jaxpr/ppermute | solution.py:14
  521.0 23.0 %collective-permute-start = (bf16[1,1,3,128,128]{3,4,2,1,0:T(8,128)(2,1)S(1)}, bf16[1,1,3,128,128]{3,4,2,1,0:T(8,128)(2,1)S(1)}, u32[]{:S(2)}, u32[]{:S(2)}) collective-permute-start(bf16[1,1,3,128,128]{3,4,2,1,0:T(8,128)(2,1)S(1)} %get-tuple-element.132), channel_id=1, source_target_pairs={{992,0},{0,32},{32,64},{64,96},{96,128},{128,160},{160,192},{192,2... | collective-permute-start | bytes 294920 | tf_op jit(solution)/shard_map/while/body/eval_jaxpr/ppermute | solution.py:14
  548.2 14.6 %collective-permute-start.5 = (bf16[1,1,4,128,128]{4,2,3,1,0:T(4,128)(2,1)S(1)}, bf16[1,1,4,128,128]{4,2,3,1,0:T(4,128)(2,1)S(1)}, u32[]{:S(2)}, u32[]{:S(2)}) collective-permute-start(bf16[1,1,4,128,128]{4,2,3,1,0:T(4,128)(2,1)S(1)} %collective-permute-done.4), channel_id=1, source_target_pairs={{31,0},{0,1},{1,2},{2,3},{3,4},{4,5},{5,6},{6,7},{7,8},{8,9},{9,10... | collective-permute-start | bytes 393224 | tf_op jit(solution)/shard_map/while/body/eval_jaxpr/ppermute | solution.py:14
  570.3 13.7 %collective-permute-start.6 = (s32[1,1,2,4]{3,2,1,0:T(2,128)S(1)}, s32[1,1,2,4]{3,2,1,0:T(2,128)S(1)}, u32[]{:S(2)}, u32[]{:S(2)}) collective-permute-start(s32[1,1,2,4]{3,2,1,0:T(2,128)S(1)} %get-tuple-element.135), channel_id=1, source_target_pairs={{31,0},{0,1},{1,2},{2,3},{3,4},{4,5},{5,6},{6,7},{7,8},{8,9},{9,10... | collective-permute-start | bytes 104 | tf_op jit(solution)/shard_map/while/body/eval_jaxpr/ppermute | solution.py:14
  572.2 29.8 %collective-permute-start.4 = (bf16[1,1,4,128,128]{4,2,3,1,0:T(4,128)(2,1)S(1)}, bf16[1,1,4,128,128]{4,2,3,1,0:T(4,128)(2,1)S(1)}, u32[]{:S(2)}, u32[]{:S(2)}) collective-permute-start(bf16[1,1,4,128,128]{4,2,3,1,0:T(4,128)(2,1)S(1)} %get-tuple-element.134), channel_id=1, source_target_pairs={{31,0},{0,1},{1,2},{2,3},{3,4},{4,5},{5,6},{6,7},{7,8},{8,9},{9,10... | collective-permute-start | bytes 393224 | tf_op jit(solution)/shard_map/while/body/eval_jaxpr/ppermute | solution.py:14
  574.1 23.1 %collective-permute-start = (bf16[1,1,3,128,128]{3,4,2,1,0:T(8,128)(2,1)S(1)}, bf16[1,1,3,128,128]{3,4,2,1,0:T(8,128)(2,1)S(1)}, u32[]{:S(2)}, u32[]{:S(2)}) collective-permute-start(bf16[1,1,3,128,128]{3,4,2,1,0:T(8,128)(2,1)S(1)} %get-tuple-element.132), channel_id=1, source_target_pairs={{992,0},{0,32},{32,64},{64,96},{96,128},{128,160},{160,192},{192,2... | collective-permute-start | bytes 294920 | tf_op jit(solution)/shard_map/while/body/eval_jaxpr/ppermute | solution.py:14
  602.0 14.4 %collective-permute-start.5 = (bf16[1,1,4,128,128]{4,2,3,1,0:T(4,128)(2,1)S(1)}, bf16[1,1,4,128,128]{4,2,3,1,0:T(4,128)(2,1)S(1)}, u32[]{:S(2)}, u32[]{:S(2)}) collective-permute-start(bf16[1,1,4,128,128]{4,2,3,1,0:T(4,128)(2,1)S(1)} %collective-permute-done.4), channel_id=1, source_target_pairs={{31,0},{0,1},{1,2},{2,3},{3,4},{4,5},{5,6},{6,7},{7,8},{8,9},{9,10... | collective-permute-start | bytes 393224 | tf_op jit(solution)/shard_map/while/body/eval_jaxpr/ppermute | solution.py:14
  617.2 14.0 %collective-permute-start.2 = (s32[1,1,2,3]{3,2,1,0:T(2,128)S(1)}, s32[1,1,2,3]{3,2,1,0:T(2,128)S(1)}, u32[]{:S(2)}, u32[]{:S(2)}) collective-permute-start(s32[1,1,2,3]{3,2,1,0:T(2,128)S(1)} %get-tuple-element.133), channel_id=1, source_target_pairs={{992,0},{0,32},{32,64},{64,96},{96,128},{128,160},{160,192},{192,2... | collective-permute-start | bytes 80 | tf_op jit(solution)/shard_map/while/body/eval_jaxpr/ppermute | solution.py:14
  625.3 13.7 %collective-permute-start.6 = (s32[1,1,2,4]{3,2,1,0:T(2,128)S(1)}, s32[1,1,2,4]{3,2,1,0:T(2,128)S(1)}, u32[]{:S(2)}, u32[]{:S(2)}) collective-permute-start(s32[1,1,2,4]{3,2,1,0:T(2,128)S(1)} %get-tuple-element.135), channel_id=1, source_target_pairs={{31,0},{0,1},{1,2},{2,3},{3,4},{4,5},{5,6},{6,7},{7,8},{8,9},{9,10... | collective-permute-start | bytes 104 | tf_op jit(solution)/shard_map/while/body/eval_jaxpr/ppermute | solution.py:14
  627.3 28.7 %collective-permute-start.4 = (bf16[1,1,4,128,128]{4,2,3,1,0:T(4,128)(2,1)S(1)}, bf16[1,1,4,128,128]{4,2,3,1,0:T(4,128)(2,1)S(1)}, u32[]{:S(2)}, u32[]{:S(2)}) collective-permute-start(bf16[1,1,4,128,128]{4,2,3,1,0:T(4,128)(2,1)S(1)} %get-tuple-element.134), channel_id=1, source_target_pairs={{31,0},{0,1},{1,2},{2,3},{3,4},{4,5},{5,6},{6,7},{7,8},{8,9},{9,10... | collective-permute-start | bytes 393224 | tf_op jit(solution)/shard_map/while/body/eval_jaxpr/ppermute | solution.py:14
  629.2 23.1 %collective-permute-start = (bf16[1,1,3,128,128]{3,4,2,1,0:T(8,128)(2,1)S(1)}, bf16[1,1,3,128,128]{3,4,2,1,0:T(8,128)(2,1)S(1)}, u32[]{:S(2)}, u32[]{:S(2)}) collective-permute-start(bf16[1,1,3,128,128]{3,4,2,1,0:T(8,128)(2,1)S(1)} %get-tuple-element.132), channel_id=1, source_target_pairs={{992,0},{0,32},{32,64},{64,96},{96,128},{128,160},{160,192},{192,2... | collective-permute-start | bytes 294920 | tf_op jit(solution)/shard_map/while/body/eval_jaxpr/ppermute | solution.py:14
  656.0 15.1 %collective-permute-start.5 = (bf16[1,1,4,128,128]{4,2,3,1,0:T(4,128)(2,1)S(1)}, bf16[1,1,4,128,128]{4,2,3,1,0:T(4,128)(2,1)S(1)}, u32[]{:S(2)}, u32[]{:S(2)}) collective-permute-start(bf16[1,1,4,128,128]{4,2,3,1,0:T(4,128)(2,1)S(1)} %collective-permute-done.4), channel_id=1, source_target_pairs={{31,0},{0,1},{1,2},{2,3},{3,4},{4,5},{5,6},{6,7},{7,8},{8,9},{9,10... | collective-permute-start | bytes 393224 | tf_op jit(solution)/shard_map/while/body/eval_jaxpr/ppermute | solution.py:14
  678.8 13.7 %collective-permute-start.6 = (s32[1,1,2,4]{3,2,1,0:T(2,128)S(1)}, s32[1,1,2,4]{3,2,1,0:T(2,128)S(1)}, u32[]{:S(2)}, u32[]{:S(2)}) collective-permute-start(s32[1,1,2,4]{3,2,1,0:T(2,128)S(1)} %get-tuple-element.135), channel_id=1, source_target_pairs={{31,0},{0,1},{1,2},{2,3},{3,4},{4,5},{5,6},{6,7},{7,8},{8,9},{9,10... | collective-permute-start | bytes 104 | tf_op jit(solution)/shard_map/while/body/eval_jaxpr/ppermute | solution.py:14
  680.8 29.4 %collective-permute-start.4 = (bf16[1,1,4,128,128]{4,2,3,1,0:T(4,128)(2,1)S(1)}, bf16[1,1,4,128,128]{4,2,3,1,0:T(4,128)(2,1)S(1)}, u32[]{:S(2)}, u32[]{:S(2)}) collective-permute-start(bf16[1,1,4,128,128]{4,2,3,1,0:T(4,128)(2,1)S(1)} %get-tuple-element.134), channel_id=1, source_target_pairs={{31,0},{0,1},{1,2},{2,3},{3,4},{4,5},{5,6},{6,7},{7,8},{8,9},{9,10... | collective-permute-start | bytes 393224 | tf_op jit(solution)/shard_map/while/body/eval_jaxpr/ppermute | solution.py:14
  682.7 23.1 %collective-permute-start = (bf16[1,1,3,128,128]{3,4,2,1,0:T(8,128)(2,1)S(1)}, bf16[1,1,3,128,128]{3,4,2,1,0:T(8,128)(2,1)S(1)}, u32[]{:S(2)}, u32[]{:S(2)}) collective-permute-start(bf16[1,1,3,128,128]{3,4,2,1,0:T(8,128)(2,1)S(1)} %get-tuple-element.132), channel_id=1, source_target_pairs={{992,0},{0,32},{32,64},{64,96},{96,128},{128,160},{160,192},{192,2... | collective-permute-start | bytes 294920 | tf_op jit(solution)/shard_map/while/body/eval_jaxpr/ppermute | solution.py:14
  710.1 14.5 %collective-permute-start.5 = (bf16[1,1,4,128,128]{4,2,3,1,0:T(4,128)(2,1)S(1)}, bf16[1,1,4,128,128]{4,2,3,1,0:T(4,128)(2,1)S(1)}, u32[]{:S(2)}, u32[]{:S(2)}) collective-permute-start(bf16[1,1,4,128,128]{4,2,3,1,0:T(4,128)(2,1)S(1)} %collective-permute-done.4), channel_id=1, source_target_pairs={{31,0},{0,1},{1,2},{2,3},{3,4},{4,5},{5,6},{6,7},{7,8},{8,9},{9,10... | collective-permute-start | bytes 393224 | tf_op jit(solution)/shard_map/while/body/eval_jaxpr/ppermute | solution.py:14
  725.4 14.0 %collective-permute-start.2 = (s32[1,1,2,3]{3,2,1,0:T(2,128)S(1)}, s32[1,1,2,3]{3,2,1,0:T(2,128)S(1)}, u32[]{:S(2)}, u32[]{:S(2)}) collective-permute-start(s32[1,1,2,3]{3,2,1,0:T(2,128)S(1)} %get-tuple-element.133), channel_id=1, source_target_pairs={{992,0},{0,32},{32,64},{64,96},{96,128},{128,160},{160,192},{192,2... | collective-permute-start | bytes 80 | tf_op jit(solution)/shard_map/while/body/eval_jaxpr/ppermute | solution.py:14
  732.9 13.7 %collective-permute-start.6 = (s32[1,1,2,4]{3,2,1,0:T(2,128)S(1)}, s32[1,1,2,4]{3,2,1,0:T(2,128)S(1)}, u32[]{:S(2)}, u32[]{:S(2)}) collective-permute-start(s32[1,1,2,4]{3,2,1,0:T(2,128)S(1)} %get-tuple-element.135), channel_id=1, source_target_pairs={{31,0},{0,1},{1,2},{2,3},{3,4},{4,5},{5,6},{6,7},{7,8},{8,9},{9,10... | collective-permute-start | bytes 104 | tf_op jit(solution)/shard_map/while/body/eval_jaxpr/ppermute | solution.py:14
  734.8 29.4 %collective-permute-start.4 = (bf16[1,1,4,128,128]{4,2,3,1,0:T(4,128)(2,1)S(1)}, bf16[1,1,4,128,128]{4,2,3,1,0:T(4,128)(2,1)S(1)}, u32[]{:S(2)}, u32[]{:S(2)}) collective-permute-start(bf16[1,1,4,128,128]{4,2,3,1,0:T(4,128)(2,1)S(1)} %get-tuple-element.134), channel_id=1, source_target_pairs={{31,0},{0,1},{1,2},{2,3},{3,4},{4,5},{5,6},{6,7},{7,8},{8,9},{9,10... | collective-permute-start | bytes 393224 | tf_op jit(solution)/shard_map/while/body/eval_jaxpr/ppermute | solution.py:14
  736.8 23.1 %collective-permute-start = (bf16[1,1,3,128,128]{3,4,2,1,0:T(8,128)(2,1)S(1)}, bf16[1,1,3,128,128]{3,4,2,1,0:T(8,128)(2,1)S(1)}, u32[]{:S(2)}, u32[]{:S(2)}) collective-permute-start(bf16[1,1,3,128,128]{3,4,2,1,0:T(8,128)(2,1)S(1)} %get-tuple-element.132), channel_id=1, source_target_pairs={{992,0},{0,32},{32,64},{64,96},{96,128},{128,160},{160,192},{192,2... | collective-permute-start | bytes 294920 | tf_op jit(solution)/shard_map/while/body/eval_jaxpr/ppermute | solution.py:14
  764.2 14.5 %collective-permute-start.5 = (bf16[1,1,4,128,128]{4,2,3,1,0:T(4,128)(2,1)S(1)}, bf16[1,1,4,128,128]{4,2,3,1,0:T(4,128)(2,1)S(1)}, u32[]{:S(2)}, u32[]{:S(2)}) collective-permute-start(bf16[1,1,4,128,128]{4,2,3,1,0:T(4,128)(2,1)S(1)} %collective-permute-done.4), channel_id=1, source_target_pairs={{31,0},{0,1},{1,2},{2,3},{3,4},{4,5},{5,6},{6,7},{7,8},{8,9},{9,10... | collective-permute-start | bytes 393224 | tf_op jit(solution)/shard_map/while/body/eval_jaxpr/ppermute | solution.py:14
  779.5 14.7 %collective-permute-start.2 = (s32[1,1,2,3]{3,2,1,0:T(2,128)S(1)}, s32[1,1,2,3]{3,2,1,0:T(2,128)S(1)}, u32[]{:S(2)}, u32[]{:S(2)}) collective-permute-start(s32[1,1,2,3]{3,2,1,0:T(2,128)S(1)} %get-tuple-element.133), channel_id=1, source_target_pairs={{992,0},{0,32},{32,64},{64,96},{96,128},{128,160},{160,192},{192,2... | collective-permute-start | bytes 80 | tf_op jit(solution)/shard_map/while/body/eval_jaxpr/ppermute | solution.py:14
  788.3 13.7 %collective-permute-start.6 = (s32[1,1,2,4]{3,2,1,0:T(2,128)S(1)}, s32[1,1,2,4]{3,2,1,0:T(2,128)S(1)}, u32[]{:S(2)}, u32[]{:S(2)}) collective-permute-start(s32[1,1,2,4]{3,2,1,0:T(2,128)S(1)} %get-tuple-element.135), channel_id=1, source_target_pairs={{31,0},{0,1},{1,2},{2,3},{3,4},{4,5},{5,6},{6,7},{7,8},{8,9},{9,10... | collective-permute-start | bytes 104 | tf_op jit(solution)/shard_map/while/body/eval_jaxpr/ppermute | solution.py:14
  790.3 28.8 %collective-permute-start.4 = (bf16[1,1,4,128,128]{4,2,3,1,0:T(4,128)(2,1)S(1)}, bf16[1,1,4,128,128]{4,2,3,1,0:T(4,128)(2,1)S(1)}, u32[]{:S(2)}, u32[]{:S(2)}) collective-permute-start(bf16[1,1,4,128,128]{4,2,3,1,0:T(4,128)(2,1)S(1)} %get-tuple-element.134), channel_id=1, source_target_pairs={{31,0},{0,1},{1,2},{2,3},{3,4},{4,5},{5,6},{6,7},{7,8},{8,9},{9,10... | collective-permute-start | bytes 393224 | tf_op jit(solution)/shard_map/while/body/eval_jaxpr/ppermute | solution.py:14
  792.2 23.1 %collective-permute-start = (bf16[1,1,3,128,128]{3,4,2,1,0:T(8,128)(2,1)S(1)}, bf16[1,1,3,128,128]{3,4,2,1,0:T(8,128)(2,1)S(1)}, u32[]{:S(2)}, u32[]{:S(2)}) collective-permute-start(bf16[1,1,3,128,128]{3,4,2,1,0:T(8,128)(2,1)S(1)} %get-tuple-element.132), channel_id=1, source_target_pairs={{992,0},{0,32},{32,64},{64,96},{96,128},{128,160},{160,192},{192,2... | collective-permute-start | bytes 294920 | tf_op jit(solution)/shard_map/while/body/eval_jaxpr/ppermute | solution.py:14
  819.0 15.1 %collective-permute-start.5 = (bf16[1,1,4,128,128]{4,2,3,1,0:T(4,128)(2,1)S(1)}, bf16[1,1,4,128,128]{4,2,3,1,0:T(4,128)(2,1)S(1)}, u32[]{:S(2)}, u32[]{:S(2)}) collective-permute-start(bf16[1,1,4,128,128]{4,2,3,1,0:T(4,128)(2,1)S(1)} %collective-permute-done.4), channel_id=1, source_target_pairs={{31,0},{0,1},{1,2},{2,3},{3,4},{4,5},{5,6},{6,7},{7,8},{8,9},{9,10... | collective-permute-start | bytes 393224 | tf_op jit(solution)/shard_map/while/body/eval_jaxpr/ppermute | solution.py:14
  834.9 14.2 %collective-permute-start.9 = (s32[1,1,2,3]{3,2,1,0:T(2,128)S(1)}, s32[1,1,2,3]{3,2,1,0:T(2,128)S(1)}, u32[]{:S(2)}, u32[]{:S(2)}) collective-permute-start(s32[1,1,2,3]{3,2,1,0:T(2,128)S(1)} %get-tuple-element.43), channel_id=1, source_target_pairs={{992,0},{0,32},{32,64},{64,96},{96,128},{128,160},{160,192},{192,2... | collective-permute-start | bytes 80 | tf_op jit(solution)/shard_map/ppermute | solution.py:14
  845.0 14.4 %collective-permute-start.11 = (bf16[1,1,4,128,128]{4,2,3,1,0:T(4,128)(2,1)S(1)}, bf16[1,1,4,128,128]{4,2,3,1,0:T(4,128)(2,1)S(1)}, u32[]{:S(2)}, u32[]{:S(2)}) collective-permute-start(bf16[1,1,4,128,128]{4,2,3,1,0:T(4,128)(2,1)S(1)} %get-tuple-element.45), channel_id=1, source_target_pairs={{31,0},{0,1},{1,2},{2,3},{3,4},{4,5},{5,6},{6,7},{7,8},{8,9},{9,10... | collective-permute-start | bytes 393224 | tf_op jit(solution)/shard_map/ppermute | solution.py:14
  (62 other events, 645.0 us)
where the time goes:
time: 864 us; the launch traced here: 861 us
  starting transfers between devices  468 us (54%)
  waiting for transfers between devices  362 us (42%)
  matrix products  18 us (2%)
    ppermute x124, starting transfers between devices, passed_along(): return lax.ppermute(block, axis, route)  468 us
    ppermute x124, waiting for transfers between devices, passed_along(): return lax.ppermute(block, axis, route)  362 us
  transfers between devices with their start and end apart: 124, of which 37 were waited for; matrix products, arithmetic and copies ran while one was open for 1% of the time, Pallas kernels for 0%

commit v1 on v0

v1 whole, which is shorter than its diff:
```python
import functools

import jax
import jax.numpy as jnp
from jax import lax
from jax.experimental import pallas as pl
from jax.experimental.pallas import tpu as pltpu
from jax.sharding import Mesh, PartitionSpec as P

ROW = ("y", "zh", "core")
COL = ("zl", "x")
GROUP = 32
TILE = 128
LEFT = 3
RIGHT = 4
PLACES = 16
PIECE = 2
MSG = RIGHT * PIECE
PANEL = LEFT * TILE
F32, BF16, I32 = jnp.float32, jnp.bfloat16, jnp.int32
VMEM_LIMIT = 48 * 1024 * 1024


def iota(shape, dim):
    return lax.broadcasted_iota(I32, shape, dim)


def scatter_kernel(place, left_ids, right_ids, keep, right, message, rows):
    row, col = place[0], place[1]
    for b in range(RIGHT):
        for u in range(4):
            strip = right[b, 32 * u : 32 * u + 32, :].astype(F32)
            rows[u % 2, pl.ds(PIECE * b + u // 2, GROUP, stride=MSG), :] = strip
    for v in range(2):
        message[:, :, v * TILE : (v + 1) * TILE] = rows[v].reshape(GROUP, MSG, TILE).astype(BF16)
    sub, lane = iota((MSG, TILE), 0), iota((MSG, TILE), 1)
    facts = jnp.zeros((MSG, TILE), I32)
    for b in range(RIGHT):
        key, block = right_ids[0, b], right_ids[1, b]
        here = lane == col * RIGHT + b
        facts = jnp.where((sub == 0) & here, jnp.where(key >= 0, lax.shift_right_logical(key, 5) + 1, 0), facts)
        facts = jnp.where((sub == 1) & here, block + 1, facts)
        facts = jnp.where((sub == 3) & (lane == b), keep[0, b], facts)
    for a in range(LEFT):
        key = left_ids[1, a]
        here = lane == row * LEFT + a
        facts = jnp.where((sub == 2) & here, jnp.where(key >= 0, lax.shift_right_logical(key, 5) + 1, 0), facts)
    facts = facts.astype(F32)
    message[:, :, 2 * TILE :] = jnp.broadcast_to(facts[None], (GROUP, MSG, TILE)).astype(BF16)


def left_kernel(left, pieces, payload, facts):
    facts[...] = pieces[:, :, 2 * TILE :].astype(F32).reshape(GROUP * MSG, TILE)
    ids = facts[pl.ds(2, GROUP, stride=MSG), :].astype(BF16)
    for n in range(payload.shape[0]):
        for a in range(LEFT):
            payload[n, a * TILE : (a + 1) * TILE, :] = left[a]
        payload[n, PANEL:, :] = ids


def select_kernel(place, pieces, left_facts, message, wanted, facts):
    row, col, base = place[0], place[1], place[2]
    facts[...] = pieces[:, :, 2 * TILE :].astype(F32).reshape(GROUP * MSG, TILE)
    right_q = jnp.sum(facts[pl.ds(0, GROUP, stride=MSG), :], axis=0, keepdims=True)
    right_j = jnp.sum(facts[pl.ds(1, GROUP, stride=MSG), :], axis=0, keepdims=True)
    keep = facts[pl.ds(3, GROUP, stride=MSG), :]
    left_q = jnp.sum(left_facts[...].astype(F32), axis=0)
    lane = iota((1, TILE), 1)
    right_class = ((lane >> 2) + row) & (GROUP - 1)
    right_key = jnp.where(right_q > 0, (right_q - 1) * GROUP + right_class.astype(F32), -2.0)
    slot = iota((GROUP, TILE), 1)
    left_class = (iota((GROUP, TILE), 0) + ((slot * 43) >> 7)) & (GROUP - 1)
    left_key = jnp.where(left_q > 0, (left_q - 1) * GROUP + left_class.astype(F32), -1.0)
    partner = jnp.full((GROUP, TILE), -1.0, F32)
    for t in range(GROUP * LEFT):
        partner = jnp.where(left_key[:, t : t + 1] == right_key, float(t), partner)
    kept = jnp.zeros((GROUP, TILE), F32)
    for j in range(RIGHT):
        kept = kept + jnp.where(right_j == j + 1, keep[:, j : j + 1], 0.0)
    needed = jnp.where((partner >= 0) & (kept > 0), 1.0, 0.0)
    before = (iota((TILE, TILE), 0) < iota((TILE, TILE), 1)).astype(F32).astype(BF16)
    order = jnp.dot(needed.astype(BF16), before, preferred_element_type=F32)
    spread = (iota((TILE, 2 * TILE), 0) == (iota((TILE, 2 * TILE), 1) >> 1)).astype(F32).astype(BF16)
    needed2 = jnp.dot(needed.astype(BF16), spread, preferred_element_type=F32)
    order2 = jnp.dot(order.astype(BF16), spread, preferred_element_type=F32)
    half = (iota((GROUP, 2 * TILE), 1) & 1).astype(F32)
    base_f = base.astype(F32)
    line = jnp.where(needed2 > 0, 2.0 * (order2 - base_f) + half, -1.0)
    lines = PIECE * PLACES
    chosen = line[:, None, :] == iota((GROUP, lines, 2 * TILE), 1).astype(F32)
    chosen = jnp.where(chosen, 1.0, 0.0).reshape(GROUP * lines, 2 * TILE).astype(BF16)
    held = pieces[:, :, 0 : 2 * TILE].astype(F32).reshape(GROUP * MSG, 2 * TILE).astype(BF16)
    packed = jnp.dot(chosen, held, preferred_element_type=F32)
    message[...] = packed.reshape(GROUP, lines, 2 * TILE).astype(BF16)
    most = jnp.max(jnp.where(needed > 0, order + 1.0, 0.0))
    own = iota((GROUP, TILE), 0) == col
    own_order = jnp.sum(jnp.where(own & (needed > 0), order + 1.0, 0.0), axis=0, keepdims=True)
    own_partner = jnp.sum(jnp.where(own, partner, 0.0), axis=0, keepdims=True)
    at = iota((PLACES, TILE), 0).astype(F32) + 1.0 + base_f
    here = own_order == at
    left_slot = jnp.sum(jnp.where(here, own_partner, 0.0), axis=1, keepdims=True)
    block = jnp.sum(jnp.where(here, right_j - 1.0, 0.0), axis=1, keepdims=True)
    live = jnp.sum(jnp.where(here, 1.0, 0.0), axis=1, keepdims=True)
    lane = iota((PLACES, TILE), 1)
    wanted[...] = jnp.where(
        lane == 0, left_slot, jnp.where(lane == 1, block, jnp.where(lane == 2, live, most))
    ).astype(I32)


def product_kernel(place, wanted, left_here, left_there, pieces, start, out, rows, total):
    lines = PIECE * PLACES
    for v in range(2):
        rows[v] = pieces[:, :, v * TILE : (v + 1) * TILE].astype(F32).reshape(GROUP * lines, TILE)
    if start is None:
        total[...] = jnp.zeros_like(total)
    else:
        total[...] = start[...]
    core = place[0] & 1
    for p in range(PLACES):

        @pl.when(wanted[p, 2] > 0)
        def _(p=p):
            tile = jnp.concatenate(
                [rows[u % 2, pl.ds(PIECE * p + u // 2, GROUP, stride=lines), :] for u in range(4)], axis=0
            ).astype(BF16)
            slot = wanted[p, 0]
            source = (slot * 43) >> 7
            a = pl.multiple_of((slot - source * LEFT) * TILE, TILE)
            panel = ((source >> 3) << 2) + ((source >> 1) & 3)
            columns = pl.ds(pl.multiple_of(wanted[p, 1] * TILE, TILE), TILE)

            @pl.when((source & 1) == core)
            def _():
                total[:, columns] += jnp.dot(left_here[panel, pl.ds(a, TILE), :], tile, preferred_element_type=F32)

            @pl.when((source & 1) != core)
            def _():
                total[:, columns] += jnp.dot(left_there[panel, pl.ds(a, TILE), :], tile, preferred_element_type=F32)

    out[...] = total[...].astype(out.dtype)


def kernel_call(body, out_shape, scratch, in_smem, *operands):
    specs = [pl.BlockSpec(memory_space=pltpu.SMEM if i < in_smem else pltpu.VMEM) for i in range(len(operands))]
    many = isinstance(out_shape, tuple)
    vmem = pl.BlockSpec(memory_space=pltpu.VMEM)
    return pl.pallas_call(
        body,
        out_shape=out_shape,
        in_specs=specs,
        out_specs=tuple(vmem for _ in out_shape) if many else vmem,
        scratch_shapes=scratch,
        compiler_params=pltpu.CompilerParams(vmem_limit_bytes=VMEM_LIMIT),
    )(*operands)


def on_device(left_tiles, left_index, right_tiles, right_index, keep_mask):
    row, col = lax.axis_index(ROW), lax.axis_index(COL)
    place = jnp.stack([row, col, 0]).astype(I32)
    lines = PIECE * PLACES

    with jax.named_scope("scatter_right"):
        message = kernel_call(
            scatter_kernel,
            jax.ShapeDtypeStruct((GROUP, MSG, 3 * TILE), BF16),
            [pltpu.VMEM((2, GROUP * MSG, TILE), F32)],
            4,
            place,
            left_index[0, 0],
            right_index[0, 0],
            keep_mask,
            right_tiles[0, 0],
        )
        pieces = lax.all_to_all(message, COL, 0, 0, tiled=True)

    with jax.named_scope("left_zh"):
        zh = lax.axis_size("zh")
        payload = kernel_call(
            left_kernel,
            jax.ShapeDtypeStruct((zh, PANEL + GROUP, TILE), BF16),
            [pltpu.VMEM((GROUP * MSG, TILE), F32)],
            0,
            left_tiles[0, 0],
            pieces,
        )
        slab = lax.all_to_all(payload, "zh", 0, 0, tiled=True)

    with jax.named_scope("left_ids"):
        ids = jnp.sum(slab[:, PANEL:, :].astype(F32), axis=0).astype(BF16)
        near = ("y", "core")
        ids = jnp.broadcast_to(ids[None], (lax.axis_size(near), GROUP, TILE))
        ids = lax.all_to_all(ids, near, 0, 0, tiled=True)

    with jax.named_scope("left_y"):
        left_here = lax.all_gather(slab, "y").reshape(-1, PANEL + GROUP, TILE)
    with jax.named_scope("left_core"):
        left_there = lax.ppermute(left_here, "core", [(0, 1), (1, 0)])

    def select(base):
        return kernel_call(
            select_kernel,
            (
                jax.ShapeDtypeStruct((GROUP, lines, 2 * TILE), BF16),
                jax.ShapeDtypeStruct((PLACES, TILE), I32),
            ),
            [pltpu.VMEM((GROUP * MSG, TILE), F32)],
            1,
            jnp.stack([row, col, base]).astype(I32),
            pieces,
            ids,
        )

    def product(wanted, tiles, start, dtype):
        shape = (TILE, RIGHT * TILE)
        operands = (place, wanted, left_here, left_there, tiles) + (() if start is None else (start,))
        body = product_kernel
        if start is None:
            body = lambda a, b, c, d, e, out, *scratch: product_kernel(a, b, c, d, e, None, out, *scratch)
        return kernel_call(
            body,
            jax.ShapeDtypeStruct(shape, dtype),
            [pltpu.VMEM((2, GROUP * lines, TILE), F32), pltpu.VMEM(shape, F32)],
            2,
            *operands,
        )

    with jax.named_scope("right_needed"):
        packed, wanted = select(jnp.int32(0))
        tiles = lax.all_to_all(packed, COL, 0, 0, tiled=True)
    with jax.named_scope("multiply"):
        first = product(wanted, tiles, None, BF16)

    most = wanted[0, 3]

    def more_rounds(_):
        def one(carry):
            base, total = carry
            packed, wanted = select(base)
            tiles = lax.all_to_all(packed, COL, 0, 0, tiled=True)
            return base + PLACES, product(wanted, tiles, total, F32)

        begin = (jnp.int32(0), jnp.zeros((TILE, RIGHT * TILE), F32))
        return lax.while_loop(lambda carry: carry[0] < most, one, begin)[1].astype(BF16)

    with jax.named_scope("further_rounds"):
        return lax.cond(most > PLACES, more_rounds, lambda done: done, first)


def solution(mesh):
    parts = Mesh(mesh.devices.reshape(4, 4, 2, 8, 4), ROW + COL)
    in_specs = (P(COL, ROW), P(COL, ROW), P(ROW, COL), P(ROW, COL), P(COL, ROW))
    return jax.shard_map(on_device, mesh=parts, in_specs=in_specs, out_specs=P(COL, ROW), check_vma=False)
```

time: 864 us -> 177 us (0.20)
  starting transfers between devices: 468 us -> 24.4 us
  waiting for transfers between devices: 362 us -> 22.9 us
  blocking collectives: 0 us -> 102 us
  matrix products: 18 us -> 0 us
  between operations: 0.16 us -> 14 us
    ppermute x124 -> x1, starting transfers between devices: 468 us -> 2.67 us  [on_device(): left_there = lax.ppermute(left_here, 'core', [(0, 1), (1, 0)])]
    ppermute x124 -> x1, waiting for transfers between devices: 362 us -> 2.4 us  [on_device(): left_there = lax.ppermute(left_here, 'core', [(0, 1), (1, 0)])]
    all_to_all x0 -> x3, blocking collectives: none -> 102 us  [the longest x1 63.1 us: on_device(): slab = lax.all_to_all(payload, 'zh', 0, 0, tiled=True)]
    all_to_all x0 -> x1, starting transfers between devices: none -> 21.7 us  [on_device(): tiles = lax.all_to_all(packed, COL, 0, 0, tiled=True)]
    dot_general x64 -> x0, matrix products: 18 us -> none  [the longest x32 9.09 us: multiply(): jnp.einsum('ab,bj,bxy->axjy', matched, placed, right_block, preferred_ele...]
    all_to_all x0 -> x1, waiting for transfers between devices: none -> 11.4 us  [on_device(): tiles = lax.all_to_all(packed, COL, 0, 0, tiled=True)]
    all_gather x0 -> x1, waiting for transfers between devices: none -> 9.05 us  [on_device(): left_here = lax.all_gather(slab, 'y').reshape(-1, PANEL + GROUP, TILE)]
  transfers between devices with their start and end apart: 124 -> 3, of which waited for: 37 -> 3; matrix products, arithmetic and copies ran while one was open for 1% -> 1% of each run, Pallas kernels for 0% -> 1%
where the time goes in v1:
time: 177 us; the launch traced here: 175 us
  blocking collectives  102 us (58%)
  starting transfers between devices  24.4 us (14%)
  waiting for transfers between devices  22.9 us (13%)
  between operations  14 us (8%)
  Pallas kernels  5.53 us (3%)
  local copies, waits for them, and re-layouts  5.05 us (3%)
    all_to_all x1, blocking collectives, on_device(): slab = lax.all_to_all(payload, 'zh', 0, 0, tiled=True)  63.1 us
    all_to_all x1, blocking collectives, on_device(): pieces = lax.all_to_all(message, COL, 0, 0, tiled=True)  29.3 us
    all_to_all x1, starting transfers between devices, on_device(): tiles = lax.all_to_all(packed, COL, 0, 0, tiled=True)  21.7 us
    all_to_all x1, waiting for transfers between devices, on_device(): tiles = lax.all_to_all(packed, COL, 0, 0, tiled=True)  11.4 us
    all_to_all x1, blocking collectives, on_device(): ids = lax.all_to_all(ids, near, 0, 0, tiled=True)  9.61 us
    all_gather x1, waiting for transfers between devices, on_device(): left_here = lax.all_gather(slab, 'y').reshape(-1, PANEL + GROUP, TILE)  9.05 us
    pallas_call x4, Pallas kernels, kernel_call(): pl.pallas_call(body, out_shape=out_shape, in_specs=specs, out_specs=tuple...  5.53 us
    unnamed x12, local copies, waits for them, and re-layouts  4.46 us
  transfers between devices with their start and end apart: 3, of which 3 were waited for; matrix products, arithmetic and copies ran while one was open for 1% of the time, Pallas kernels for 1%

profile of v1, /device:TPU:1, one launch (start us, length us, event | category | flops | bytes accessed | tf_op | source)
XLA Modules:
  0.0 174.7 jit_solution(11402159087464655435)
XLA Ops:
  6.5 0.0 all-gather.3.cloned.1.call-start
  6.5 0.1 pad_add_fusion.1.place.a
  6.6 0.0 copy-start
  6.6 0.9 copy-done
  7.5 0.0 copy-start.2
  7.5 0.7 copy-done.2
  8.2 0.0 copy-start.3
  8.2 0.7 copy-done.3
  8.9 0.0 copy-start.4
  8.9 0.7 copy-done.4
  9.5 0.7 scatter_right.1
  10.2 29.3 %all_to_all.26.pieces = bf16[32,8,384]{2,1,0:T(8,128)(2,1)S(1)} all-to-all(bf16[32,8,384]{2,1,0:T(8,128)(2,1)S(1)} %scatter_right.1), channel_id=1, replica_groups=mesh['y'=4,'zh'=4,'core'=2,'zl'=8,'x'=4] {'zl','x'}, dimensions={0} | all-to-all | bytes 393216 | tf_op jit(solution)/shard_map/scatter_right/all_to_all | solution.py:174
  39.5 0.0 copy-start.1
  39.5 0.9 copy-done.1
  40.4 0.1 left_zh.1
  40.5 63.1 %all_to_all.27 = bf16[4,416,128]{2,1,0:T(8,128)(2,1)} all-to-all(bf16[4,416,128]{2,1,0:T(8,128)(2,1)S(1)} %left_zh.1), channel_id=1, replica_groups=mesh['y'=4,'zh'=4,'core'=2,'zl'=8,'x'=4] {'zh'}, dimensions={0} | all-to-all | bytes 851968 | tf_op jit(solution)/shard_map/left_zh/all_to_all | solution.py:186
  103.6 0.0 all-gather.3.cloned.1.call-update
  103.6 0.8 slice_reduce_fusion
  104.4 9.6 %all_to_all.28.left_facts = bf16[8,32,128]{2,1,0:T(8,128)(2,1)S(1)} all-to-all(bf16[8,32,128]{2,1,0:T(8,128)(2,1)S(1)} %broadcast_in_dim.2), channel_id=1, replica_groups=mesh['y'=4,'zh'=4,'core'=2,'zl'=8,'x'=4] {'y','core'}, dimensions={0} | all-to-all | bytes 131072 | tf_op jit(solution)/shard_map/left_ids/all_to_all | solution.py:192
  114.0 2.5 %right_needed.1 = (bf16[32,32,256]{2,1,0:T(8,128)(2,1)}, s32[16,128]{1,0:T(8,128)S(1)}) custom-call(s32[3]{0:T(128)S(1)} %pad_add_fusion.1.place.a, bf16[32,8,384]{2,1,0:T(8,128)(2,1)S(1)} %all_to_all.26.pieces, bf16[8,32,128]{2,1,0:T(8,128)(2,1)S(1)} %all_to_all.28.left_facts), custom_call_target="tpu_custom_call" | custom-call | tf_op jit(solution)/shard_map/right_needed/pallas_call | solution.py:147
  116.5 21.7 %all-to-all-start.4 = ((bf16[32,32,256]{2,1,0:T(8,128)(2,1)}), bf16[32,32,256]{2,1,0:T(8,128)(2,1)S(1)}, u32[]{:S(2)}, u32[]{:S(2)}) async-start(bf16[32,32,256]{2,1,0:T(8,128)(2,1)} %get-tuple-element.91), calls=%async_computation.4 | async-start | bytes 1048576 | tf_op jit(solution)/shard_map/right_needed/all_to_all | solution.py:229
  138.2 9.1 %all-gather.3.cloned.1.call-done.c = bf16[16,416,128]{2,1,0:T(8,128)(2,1)} async-done(((bf16[4,416,128]{2,1,0:T(8,128)(2,1)}), bf16[16,416,128]{2,1,0:T(8,128)(2,1)}) %all-gather.3.cloned.1.call-update) | async-done | bytes 1703952 | tf_op jit(solution)/shard_map/left_y/all_gather | solution.py:195
  147.3 2.7 %collective-permute-start = (bf16[16,416,128]{2,1,0:T(8,128)(2,1)}, bf16[16,416,128]{2,1,0:T(8,128)(2,1)}, u32[]{:S(2)}, u32[]{:S(2)}) collective-permute-start(bf16[16,416,128]{2,1,0:T(8,128)(2,1)} %all-gather.3.cloned.1.call-done.c), channel_id=1, source_target_pairs={{0,32},{32,0},{1,33},{33,1},{2,34},{34,2},{3,35},{35,3},{4,36},{36... | collective-permute-start | bytes 5111816 | tf_op jit(solution)/shard_map/left_core/ppermute | solution.py:197
  150.0 0.6 slice.7
  151.1 2.4 %collective-permute-done.d = bf16[16,416,128]{2,1,0:T(8,128)(2,1)} collective-permute-done((bf16[16,416,128]{2,1,0:T(8,128)(2,1)}, bf16[16,416,128]{2,1,0:T(8,128)(2,1)}, u32[]{:S(2)}, u32[]{:S(2)}) %collective-permute-start) | collective-permute-done | bytes 1703968 | tf_op jit(solution)/shard_map/left_core/ppermute | solution.py:197
  153.5 11.4 %all-to-all-done.4.e = bf16[32,32,256]{2,1,0:T(8,128)(2,1)S(1)} async-done(((bf16[32,32,256]{2,1,0:T(8,128)(2,1)}), bf16[32,32,256]{2,1,0:T(8,128)(2,1)S(1)}, u32[]{:S(2)}, u32[]{:S(2)}) %all-to-all-start.4) | async-done | bytes 524320 | tf_op jit(solution)/shard_map/right_needed/all_to_all | solution.py:229
  164.9 2.3 %multiply.1 = bf16[128,512]{1,0:T(8,128)(2,1)S(1)} custom-call(s32[3]{0:T(128)S(1)} %pad_add_fusion.1.place.a, s32[16,128]{1,0:T(8,128)S(1)} %get-tuple-element.90.b, bf16[16,416,128]{2,1,0:T(8,128)(2,1)} %all-gather.3.cloned.1.call-done.c, bf16[16,416,128]{2,1,0:T(8,128)(2,1)} %collective-permute-done.d, bf16[32,32,256]{2,1,0:T(8,128)(2,1)S(1)} %all-to-all-done.4.e), custom_call_target="tpu_custom_call" | custom-call | tf_op jit(solution)/shard_map/multiply/pallas_call | solution.py:147
  167.2 0.0 copy-start.6
  167.2 0.6 copy-done.6
  (2 shorter events, 0.0 us)
Async XLA Ops:
  6.5 140.7 %all-gather.3.cloned.1.call-start = ((), (), s32[]{:S(2)}) async-start(), calls=%async_computation.5 | async-start | bytes 2129920 | tf_op jit(solution)/shard_map/left_y/all_gather | solution.py:195
  6.6 0.9 copy-start
  7.5 0.7 copy-start.2
  8.2 0.7 copy-start.3
  8.9 0.7 copy-start.4
  39.5 0.9 copy-start.1
  116.5 48.4 %all-to-all-start.4 = ((bf16[32,32,256]{2,1,0:T(8,128)(2,1)}), bf16[32,32,256]{2,1,0:T(8,128)(2,1)S(1)}, u32[]{:S(2)}, u32[]{:S(2)}) async-start(bf16[32,32,256]{2,1,0:T(8,128)(2,1)} %get-tuple-element.91), calls=%async_computation.4 | async-start | bytes 1048576 | tf_op jit(solution)/shard_map/right_needed/all_to_all | solution.py:229
  147.3 6.2 %collective-permute-start = (bf16[16,416,128]{2,1,0:T(8,128)(2,1)}, bf16[16,416,128]{2,1,0:T(8,128)(2,1)}, u32[]{:S(2)}, u32[]{:S(2)}) collective-permute-start(bf16[16,416,128]{2,1,0:T(8,128)(2,1)} %all-gather.3.cloned.1.call-done.c), channel_id=1, source_target_pairs={{0,32},{32,0},{1,33},{33,1},{2,34},{34,2},{3,35},{35,3},{4,36},{36... | collective-permute-start | bytes 5111816 | tf_op jit(solution)/shard_map/left_core/ppermute | solution.py:197
  167.2 0.7 copy-start.6
Sparse Core Ops, SparseCore 0:
  103.7 43.5 all-gather.2

commit v2 on v1

v2 whole, which is shorter than its diff:
```python
import functools

import jax
import jax.numpy as jnp
from jax import lax
from jax.experimental import pallas as pl
from jax.experimental.pallas import tpu as pltpu
from jax.sharding import Mesh, PartitionSpec as P

ROW = ("y", "zh", "core")
HALF = ("zl", "x")
COL = ("zb",) + HALF
GROUP = 32
TILE = 128
LEFT = 3
RIGHT = 4
PLACES = 16
SPREAD = 16
WIDE = 4
PIECE = TILE // SPREAD // WIDE
MSG = RIGHT * PIECE
PANEL = LEFT * TILE
IDS = 16
F32, BF16, I32 = jnp.float32, jnp.bfloat16, jnp.int32
VMEM_LIMIT = 48 * 1024 * 1024


def iota(shape, dim):
    return lax.broadcasted_iota(I32, shape, dim)


def scatter_kernel(place, right_ids, keep, right, data, own_facts, rows):
    for b in range(RIGHT):
        for u in range(TILE // SPREAD):
            strip = right[b, SPREAD * u : SPREAD * (u + 1), :].astype(F32)
            rows[u % WIDE, pl.ds(PIECE * b + u // WIDE, SPREAD, stride=MSG), :] = strip
    for v in range(WIDE):
        data[:, :, v * TILE : (v + 1) * TILE] = rows[v].reshape(SPREAD, MSG, TILE).astype(BF16)
    sub, lane = iota((MSG, TILE), 0), iota((MSG, TILE), 1)
    facts = jnp.zeros((MSG, TILE), I32)
    for b in range(RIGHT):
        key, block = right_ids[0, b], right_ids[1, b]
        here = lane == place[1] * RIGHT + b
        facts = jnp.where((sub == 0) & here, jnp.where(key >= 0, lax.shift_right_logical(key, 5) + 1, 0), facts)
        facts = jnp.where((sub == 1) & here, block + 1, facts)
        facts = jnp.where((sub == 3) & (lane == b), keep[0, b], facts)
    own_facts[...] = facts.astype(F32)


def message_kernel(data, own_facts, left_ids, message):
    for half in range(GROUP // SPREAD):
        message[half * SPREAD : (half + 1) * SPREAD, :, 0 : WIDE * TILE] = data[...]
    left_q = jnp.sum(left_ids[:, 0:MSG, :].astype(F32), axis=0)[0:1]
    facts = jnp.where(iota((MSG, TILE), 0) == 2, left_q, own_facts[...])
    message[:, :, WIDE * TILE :] = jnp.broadcast_to(facts[None], (GROUP, MSG, TILE)).astype(BF16)


def left_kernel(place, ids, left, payload):
    for a in range(LEFT):
        payload[a * TILE : (a + 1) * TILE, :] = left[a]
    lane = iota((IDS, TILE), 1)
    facts = jnp.zeros((IDS, TILE), I32)
    for a in range(LEFT):
        key = ids[1, a]
        here = (iota((IDS, TILE), 0) == 0) & (lane == place[0] * LEFT + a)
        facts = jnp.where(here, jnp.where(key >= 0, lax.shift_right_logical(key, 5) + 1, 0), facts)
    payload[PANEL:, :] = facts.astype(F32).astype(BF16)


def select_kernel(place, pieces, below, above, message, wanted, facts):
    row, col, base = place[0], place[1], place[2]
    first = (col // SPREAD) * SPREAD
    facts[...] = pieces[:, :, WIDE * TILE :].astype(F32).reshape(GROUP * MSG, TILE)
    right_q = jnp.sum(facts[pl.ds(0, GROUP, stride=MSG), :], axis=0, keepdims=True)
    right_j = jnp.sum(facts[pl.ds(1, GROUP, stride=MSG), :], axis=0, keepdims=True)
    keep = facts[pl.ds(first * MSG + 3, SPREAD, stride=MSG), :]
    left_q = facts[pl.ds(first * MSG + 2, SPREAD, stride=MSG), :]
    lane = iota((1, TILE), 1)
    right_class = ((lane >> 2) + row) & (GROUP - 1)
    right_key = jnp.where(right_q > 0, (right_q - 1) * GROUP + right_class.astype(F32), -2.0)
    slot = iota((SPREAD, TILE), 1)
    left_class = (first + iota((SPREAD, TILE), 0) + ((slot * 43) >> 7)) & (GROUP - 1)
    left_key = jnp.where(left_q > 0, (left_q - 1) * GROUP + left_class.astype(F32), -1.0)
    partner = jnp.full((SPREAD, TILE), -1.0, F32)
    for t in range(GROUP * LEFT):
        partner = jnp.where(left_key[:, t : t + 1] == right_key, float(t), partner)
    kept = jnp.zeros((SPREAD, TILE), F32)
    for j in range(RIGHT):
        kept = kept + jnp.where(right_j == j + 1, keep[:, j : j + 1], 0.0)
    needed = jnp.where((partner >= 0) & (kept > 0), 1.0, 0.0)
    before = (iota((TILE, TILE), 0) < iota((TILE, TILE), 1)).astype(F32).astype(BF16)
    order = jnp.dot(needed.astype(BF16), before, preferred_element_type=F32)
    spread = (iota((TILE, 2 * TILE), 0) == (iota((TILE, 2 * TILE), 1) >> 1)).astype(F32).astype(BF16)
    needed2 = jnp.dot(needed.astype(BF16), spread, preferred_element_type=F32)
    order2 = jnp.dot(order.astype(BF16), spread, preferred_element_type=F32)
    half = (iota((SPREAD, 2 * TILE), 1) & 1).astype(F32)
    base_f = base.astype(F32)
    line = jnp.where(needed2 > 0, 2.0 * (order2 - base_f) + half, -1.0)
    lines = PIECE * PLACES
    chosen = line[:, None, :] == iota((SPREAD, lines, 2 * TILE), 1).astype(F32)
    chosen = jnp.where(chosen, 1.0, 0.0).reshape(SPREAD * lines, 2 * TILE).astype(BF16)
    held = pieces[:, :, 0 : WIDE * TILE].astype(F32).reshape(GROUP * MSG, WIDE * TILE).astype(BF16)
    packed = jnp.dot(chosen, held, preferred_element_type=F32)
    message[...] = packed.reshape(SPREAD, lines, WIDE * TILE).astype(BF16)
    most = jnp.max(jnp.where(needed > 0, order + 1.0, 0.0))
    own = iota((SPREAD, TILE), 0) == col - first
    own_order = jnp.sum(jnp.where(own & (needed > 0), order + 1.0, 0.0), axis=0, keepdims=True)
    own_partner = jnp.sum(jnp.where(own, partner, 0.0), axis=0, keepdims=True)
    at = iota((PLACES, TILE), 0).astype(F32) + 1.0 + base_f
    here = own_order == at
    left_slot = jnp.sum(jnp.where(here, own_partner, 0.0), axis=1, keepdims=True)
    block = jnp.sum(jnp.where(here, right_j - 1.0, 0.0), axis=1, keepdims=True)
    live = jnp.sum(jnp.where(here, 1.0, 0.0), axis=1, keepdims=True)
    lane = iota((PLACES, TILE), 1)
    wanted[...] = jnp.where(
        lane == 0, left_slot, jnp.where(lane == 1, block, jnp.where(lane == 2, live, most))
    ).astype(I32)


def product_kernel(place, wanted, left_here, left_there, pieces, start, out, rows, total):
    lines = PIECE * PLACES
    for v in range(WIDE):
        rows[v] = pieces[:, :, v * TILE : (v + 1) * TILE].astype(F32).reshape(SPREAD * lines, TILE)
    if start is None:
        total[...] = jnp.zeros_like(total)
    else:
        total[...] = start[...]
    core = place[0] & 1
    for p in range(PLACES):

        @pl.when(wanted[p, 2] > 0)
        def _(p=p):
            tile = jnp.concatenate(
                [rows[u % WIDE, pl.ds(PIECE * p + u // WIDE, SPREAD, stride=lines), :] for u in range(TILE // SPREAD)],
                axis=0,
            ).astype(BF16)
            slot = wanted[p, 0]
            source = (slot * 43) >> 7
            a = pl.multiple_of((slot - source * LEFT) * TILE, TILE)
            panel = ((((place[0] >> 3) - (source >> 3)) & 3) << 2) + ((source >> 1) & 3)
            columns = pl.ds(pl.multiple_of(wanted[p, 1] * TILE, TILE), TILE)

            @pl.when((source & 1) == core)
            def _():
                total[:, columns] += jnp.dot(left_here[panel, pl.ds(a, TILE), :], tile, preferred_element_type=F32)

            @pl.when((source & 1) != core)
            def _():
                total[:, columns] += jnp.dot(left_there[panel, pl.ds(a, TILE), :], tile, preferred_element_type=F32)

    out[...] = total[...].astype(out.dtype)


def kernel_call(body, out_shape, scratch, spaces, *operands):
    kinds = {"s": pltpu.SMEM, "v": pltpu.VMEM, "a": pl.ANY}
    specs = [pl.BlockSpec(memory_space=kinds[space]) for space in spaces]
    many = isinstance(out_shape, tuple)
    vmem = pl.BlockSpec(memory_space=pltpu.VMEM)
    return pl.pallas_call(
        body,
        out_shape=out_shape,
        in_specs=specs,
        out_specs=tuple(vmem for _ in out_shape) if many else vmem,
        scratch_shapes=scratch,
        compiler_params=pltpu.CompilerParams(vmem_limit_bytes=VMEM_LIMIT),
    )(*operands)


def on_device(left_tiles, left_index, right_tiles, right_index, keep_mask):
    row, col = lax.axis_index(ROW), lax.axis_index(COL)
    place = jnp.stack([row, col, 0]).astype(I32)
    lines = PIECE * PLACES

    with jax.named_scope("left_zh"):
        payload = kernel_call(
            left_kernel,
            jax.ShapeDtypeStruct((PANEL + IDS, TILE), BF16),
            [],
            "ssv",
            place,
            left_index[0, 0],
            left_tiles[0, 0],
        )
        slab = lax.all_gather(payload, "zh")

    with jax.named_scope("left_ids"):
        ids = jnp.sum(slab[:, PANEL:, :].astype(F32), axis=0).astype(BF16)
        near = ("y", "core")
        ids = jnp.broadcast_to(ids[None], (lax.axis_size(near), IDS, TILE))
        ids = lax.all_to_all(ids, near, 0, 0, tiled=True)

    with jax.named_scope("scatter_right"):
        data, own_facts = kernel_call(
            scatter_kernel,
            (
                jax.ShapeDtypeStruct((SPREAD, MSG, WIDE * TILE), BF16),
                jax.ShapeDtypeStruct((MSG, TILE), F32),
            ),
            [pltpu.VMEM((WIDE, SPREAD * MSG, TILE), F32)],
            "sssv",
            place,
            right_index[0, 0],
            keep_mask,
            right_tiles[0, 0],
        )
        message = kernel_call(
            message_kernel,
            jax.ShapeDtypeStruct((GROUP, MSG, (WIDE + 1) * TILE), BF16),
            [],
            "vvv",
            data,
            own_facts,
            ids,
        )
        pieces = lax.all_to_all(message, COL, 0, 0, tiled=True)

    with jax.named_scope("left_y"):
        size = lax.axis_size("y")
        up = [(i, (i + 1) % size) for i in range(size)]
        down = [(i, (i - 1) % size) for i in range(size)]
        half = slab.shape[0] // 2
        below = lax.ppermute(slab, "y", up)
        above = lax.ppermute(slab, "y", down)
        far = (lax.ppermute(below[:half], "y", up), lax.ppermute(above[half:], "y", down))
        left_here = jnp.concatenate((slab, below) + far + (above,))

    with jax.named_scope("left_core"):
        left_there = lax.ppermute(left_here, "core", [(0, 1), (1, 0)])

    def select(base):
        return kernel_call(
            select_kernel,
            (
                jax.ShapeDtypeStruct((SPREAD, lines, WIDE * TILE), BF16),
                jax.ShapeDtypeStruct((PLACES, TILE), I32),
            ),
            [pltpu.VMEM((GROUP * MSG, TILE), F32)],
            "svaa",
            jnp.stack([row, col, base]).astype(I32),
            pieces,
            below,
            above,
        )

    def product(wanted, tiles, start, dtype):
        shape = (TILE, RIGHT * TILE)
        operands = (place, wanted, left_here, left_there, tiles) + (() if start is None else (start,))
        body = product_kernel
        if start is None:
            body = lambda a, b, c, d, e, out, *scratch: product_kernel(a, b, c, d, e, None, out, *scratch)
        return kernel_call(
            body,
            jax.ShapeDtypeStruct(shape, dtype),
            [pltpu.VMEM((WIDE, SPREAD * lines, TILE), F32), pltpu.VMEM(shape, F32)],
            "ssvvvv"[: len(operands)],
            *operands,
        )

    with jax.named_scope("right_needed"):
        packed, wanted = select(jnp.int32(0))
        tiles = lax.all_to_all(packed, HALF, 0, 0, tiled=True)
    with jax.named_scope("multiply"):
        first = product(wanted, tiles, None, BF16)

    most = wanted[0, 3]

    def more_rounds(_):
        def one(carry):
            base, total = carry
            packed, wanted = select(base)
            tiles = lax.all_to_all(packed, HALF, 0, 0, tiled=True)
            return base + PLACES, product(wanted, tiles, total, F32)

        begin = (jnp.int32(0), jnp.zeros((TILE, RIGHT * TILE), F32))
        return lax.while_loop(lambda carry: carry[0] < most, one, begin)[1].astype(BF16)

    with jax.named_scope("further_rounds"):
        return lax.cond(most > PLACES, more_rounds, lambda done: done, first)


def solution(mesh):
    parts = Mesh(mesh.devices.reshape(4, 4, 2, 2, 4, 4), ROW + COL)
    in_specs = (P(COL, ROW), P(COL, ROW), P(ROW, COL), P(ROW, COL), P(COL, ROW))
    return jax.shard_map(on_device, mesh=parts, in_specs=in_specs, out_specs=P(COL, ROW), check_vma=False)
```

time: 177 us -> 129 us (0.73); the launches traced: 175 us -> 129 us
  blocking collectives: 102 us -> 52.2 us
  starting transfers between devices: 24.4 us -> 42.5 us
  between operations: 14 us -> 0.81 us
  waiting for transfers between devices: 22.9 us -> 19.4 us
  Pallas kernels: 5.53 us -> 7.67 us
    all_to_all x3 -> x0, blocking collectives: 102 us -> none  [the longest x1 63.1 us: on_device(): slab = lax.all_to_all(payload, 'zh', 0, 0, tiled=True)]
    all_gather x0 -> x1, blocking collectives: none -> 52.2 us  [on_device(): slab = lax.all_gather(payload, 'zh')]
    ppermute x0 -> x4, waiting for transfers between devices: none -> 13 us  [the longest x1 6.65 us: on_device(): above = lax.ppermute(slab, 'y', down)]
    ppermute x0 -> x4, starting transfers between devices: none -> 11.8 us  [the longest x1 4.3 us: on_device(): lax.ppermute(above[half:], 'y', down)]
    all_gather x1 -> x0, waiting for transfers between devices: 9.05 us -> none  [on_device(): left_here = lax.all_gather(slab, 'y').reshape(-1, PANEL + GROUP, TILE)]
    all_to_all x1 -> x3, waiting for transfers between devices: 11.4 us -> 4.43 us  [the longest x1 2.6 us: on_device(): pieces = lax.all_to_all(message, COL, 0, 0, tiled=True)]
    ppermute x1, starting transfers between devices: 2.67 us -> 5.89 us  [on_device(): left_there = lax.ppermute(left_here, 'core', [(0, 1), (1, 0)])]
    all_to_all x1 -> x3, starting transfers between devices: 21.7 us -> 24.8 us  [the longest x1 11.2 us: on_device(): ids = lax.all_to_all(ids, near, 0, 0, tiled=True)]
  transfers between devices with their start and end apart: 3 -> 8, of which waited for: 3 -> 7; matrix products, arithmetic and copies ran while one was open for 1% -> 1% of each run, Pallas kernels for 1% -> 0%
where the time goes in v2:
time: 129 us
  blocking collectives  52.2 us (40%)
  starting transfers between devices  42.5 us (33%)
  waiting for transfers between devices  19.4 us (15%)
  Pallas kernels  7.67 us (6%)
  local copies, waits for them, and re-layouts  5.89 us (5%)
    all_gather x1, blocking collectives, on_device(): slab = lax.all_gather(payload, 'zh')  52.2 us
    all_to_all x1, starting transfers between devices, on_device(): ids = lax.all_to_all(ids, near, 0, 0, tiled=True)  11.2 us
    all_to_all x1, starting transfers between devices, on_device(): pieces = lax.all_to_all(message, COL, 0, 0, tiled=True)  8.47 us
    pallas_call x5, Pallas kernels, kernel_call(): pl.pallas_call(body, out_shape=out_shape, in_specs=specs, out_specs=tuple...  7.67 us
    ppermute x1, waiting for transfers between devices, on_device(): above = lax.ppermute(slab, 'y', down)  6.65 us
    ppermute x1, starting transfers between devices, on_device(): left_there = lax.ppermute(left_here, 'core', [(0, 1), (1, 0)])  5.89 us
    all_to_all x1, starting transfers between devices, on_device(): tiles = lax.all_to_all(packed, HALF, 0, 0, tiled=True)  5.16 us
    unnamed x16, local copies, waits for them, and re-layouts  4.6 us
  transfers between devices with their start and end apart: 8, of which 7 were waited for; matrix products, arithmetic and copies ran while one was open for 1% of the time, Pallas kernels for 0%

profile of v2, /device:TPU:1, one launch (start us, length us, event | category | flops | bytes accessed | tf_op | source)
XLA Modules:
  0.0 128.6 jit_solution(11103428565064000790)
XLA Ops:
  0.0 0.1 pad_add_fusion.1.place.a
  0.1 0.0 copy-start.1
  0.1 0.9 copy-done.1
  1.0 0.0 copy-start.2
  1.0 0.7 copy-done.2
  1.7 0.6 left_zh.1
  2.2 52.2 %all-gather = bf16[1600,128]{1,0:T(8,128)(2,1)S(1)} all-gather(bf16[400,128]{1,0:T(8,128)(2,1)S(1)} %left_zh.1), channel_id=2, replica_groups=mesh['y'=4,'zh'=4,'core'=2,'zb'=2,'zl'=4,'x'=4] {'zh'}, dimensions={0}, use_global_device_ids=true | all-gather | bytes 512000 | tf_op jit(solution)/shard_map/left_zh/all_gather | solution.py:184
  54.4 0.6 broadcast_in_dim.2
  55.0 11.2 %all-to-all-start.1 = ((bf16[8,16,128]{2,1,0:T(8,128)(2,1)}), bf16[8,16,128]{2,1,0:T(8,128)(2,1)S(1)}, u32[]{:S(2)}, u32[]{:S(2)}) async-start(bf16[8,16,128]{2,1,0:T(8,128)(2,1)} %broadcast_in_dim.2), calls=%async_computation.1 | async-start | bytes 65536 | tf_op jit(solution)/shard_map/left_ids/all_to_all | solution.py:190
  66.3 0.0 copy-start
  66.3 0.9 copy-done
  67.2 0.0 copy-start.3
  67.2 0.7 copy-done.3
  67.8 0.0 copy-start.4
  67.9 0.7 copy-done.4
  68.5 0.6 scatter_right.2
  69.1 1.8 %all-to-all-done.1.left_ids = bf16[8,16,128]{2,1,0:T(8,128)(2,1)S(1)} async-done(((bf16[8,16,128]{2,1,0:T(8,128)(2,1)}), bf16[8,16,128]{2,1,0:T(8,128)(2,1)S(1)}, u32[]{:S(2)}, u32[]{:S(2)}) %all-to-all-start.1) | async-done | bytes 32800 | tf_op jit(solution)/shard_map/left_ids/all_to_all | solution.py:190
  71.0 0.8 scatter_right.3
  71.7 8.5 %all-to-all-start.2 = ((bf16[32,8,640]{2,1,0:T(8,128)(2,1)}), bf16[32,8,640]{2,1,0:T(8,128)(2,1)}, u32[]{:S(2)}, u32[]{:S(2)}) async-start(bf16[32,8,640]{2,1,0:T(8,128)(2,1)} %scatter_right.3), calls=%async_computation.2 | async-start | bytes 655360 | tf_op jit(solution)/shard_map/scatter_right/all_to_all | solution.py:215
  80.2 2.8 %collective-permute-start.1 = (bf16[4,400,128]{2,1,0:T(8,128)(2,1)S(1)}, bf16[4,400,128]{2,1,0:T(8,128)(2,1)S(1)}, u32[]{:S(2)}, u32[]{:S(2)}) collective-permute-start(bf16[4,400,128]{2,1,0:T(8,128)(2,1)S(1)} %bitcast.22), channel_id=1, source_target_pairs={{0,768},{256,0},{512,256},{768,512},{1,769},{257,1},{513,257},{769... | collective-permute-start | bytes 1228808 | tf_op jit(solution)/shard_map/left_y/ppermute | solution.py:223
  83.0 2.5 %collective-permute-start = (bf16[4,400,128]{2,1,0:T(8,128)(2,1)S(1)}, bf16[4,400,128]{2,1,0:T(8,128)(2,1)S(1)}, u32[]{:S(2)}, u32[]{:S(2)}) collective-permute-start(bf16[4,400,128]{2,1,0:T(8,128)(2,1)S(1)} %bitcast.23), channel_id=1, source_target_pairs={{0,256},{256,512},{512,768},{768,0},{1,257},{257,513},{513,769},{7... | collective-permute-start | bytes 1228808 | tf_op jit(solution)/shard_map/left_y/ppermute | solution.py:222
  85.5 6.6 %collective-permute-done.1.above = bf16[4,400,128]{2,1,0:T(8,128)(2,1)S(1)} collective-permute-done((bf16[4,400,128]{2,1,0:T(8,128)(2,1)S(1)}, bf16[4,400,128]{2,1,0:T(8,128)(2,1)S(1)}, u32[]{:S(2)}, u32[]{:S(2)}) %collective-permute-start.1) | collective-permute-done | bytes 409632 | tf_op jit(solution)/shard_map/left_y/ppermute | solution.py:223
  92.2 3.7 %collective-permute-done.below = bf16[4,400,128]{2,1,0:T(8,128)(2,1)S(1)} collective-permute-done((bf16[4,400,128]{2,1,0:T(8,128)(2,1)S(1)}, bf16[4,400,128]{2,1,0:T(8,128)(2,1)S(1)}, u32[]{:S(2)}, u32[]{:S(2)}) %collective-permute-start) | collective-permute-done | bytes 409632 | tf_op jit(solution)/shard_map/left_y/ppermute | solution.py:222
  95.9 2.6 %all-to-all-done.2.pieces = bf16[32,8,640]{2,1,0:T(8,128)(2,1)} async-done(((bf16[32,8,640]{2,1,0:T(8,128)(2,1)}), bf16[32,8,640]{2,1,0:T(8,128)(2,1)}, u32[]{:S(2)}, u32[]{:S(2)}) %all-to-all-start.2) | async-done | bytes 327712 | tf_op jit(solution)/shard_map/scatter_right/all_to_all | solution.py:215
  98.5 2.7 %right_needed.1 = (bf16[16,32,512]{2,1,0:T(8,128)(2,1)}, s32[16,128]{1,0:T(8,128)S(1)}) custom-call(s32[3]{0:T(128)S(1)} %pad_add_fusion.1.place.a, bf16[32,8,640]{2,1,0:T(8,128)(2,1)} %all-to-all-done.2.pieces, bf16[4,400,128]{2,1,0:T(8,128)(2,1)S(1)} %collective-permute-done.below, bf16[4,400,128]{2,1,0:T(8,128)(2,1)S(1)} %collective-permute-done.1.above), custom_call_target="tpu_custom_call" | custom-call | tf_op jit(solution)/shard_map/right_needed/pallas_call | solution.py:159
  101.2 5.2 %all-to-all-start.3 = ((bf16[16,32,512]{2,1,0:T(8,128)(2,1)}), bf16[16,32,512]{2,1,0:T(8,128)(2,1)S(1)}, u32[]{:S(2)}, u32[]{:S(2)}) async-start(bf16[16,32,512]{2,1,0:T(8,128)(2,1)} %get-tuple-element.103), calls=%async_computation.3 | async-start | bytes 1048576 | tf_op jit(solution)/shard_map/right_needed/all_to_all | solution.py:261
  106.4 2.2 %collective-permute-start.2 = (bf16[2,400,128]{2,1,0:T(8,128)(2,1)S(1)}, bf16[2,400,128]{2,1,0:T(8,128)(2,1)S(1)}, u32[]{:S(2)}, u32[]{:S(2)}) collective-permute-start(bf16[2,400,128]{2,1,0:T(8,128)(2,1)S(1)} %slice.17), channel_id=1, source_target_pairs={{0,256},{256,512},{512,768},{768,0},{1,257},{257,513},{513,769},{7... | collective-permute-start | bytes 614408 | tf_op jit(solution)/shard_map/left_y/ppermute | solution.py:224
  108.7 4.3 %collective-permute-start.3 = (bf16[2,400,128]{2,1,0:T(8,128)(2,1)S(1)}, bf16[2,400,128]{2,1,0:T(8,128)(2,1)S(1)}, u32[]{:S(2)}, u32[]{:S(2)}) collective-permute-start(bf16[2,400,128]{2,1,0:T(8,128)(2,1)S(1)} %slice.18), channel_id=1, source_target_pairs={{0,768},{256,0},{512,256},{768,512},{1,769},{257,1},{513,257},{769... | collective-permute-start | bytes 614408 | tf_op jit(solution)/shard_map/left_y/ppermute | solution.py:224
  113.0 0.1 constant_dynamic-update-slice_fusion.3
  113.0 1.4 %collective-permute-done.2 = bf16[2,400,128]{2,1,0:T(8,128)(2,1)S(1)} collective-permute-done((bf16[2,400,128]{2,1,0:T(8,128)(2,1)S(1)}, bf16[2,400,128]{2,1,0:T(8,128)(2,1)S(1)}, u32[]{:S(2)}, u32[]{:S(2)}) %collective-permute-start.2) | collective-permute-done | bytes 204832 | tf_op jit(solution)/shard_map/left_y/ppermute | solution.py:224
  114.4 1.2 collective-permute-done.3
  115.7 0.1 constant_dynamic-update-slice_fusion.c
  115.7 5.9 %collective-permute-start.4 = (bf16[16,400,128]{2,1,0:T(8,128)(2,1)S(1)}, bf16[16,400,128]{2,1,0:T(8,128)(2,1)}, u32[]{:S(2)}, u32[]{:S(2)}) collective-permute-start(bf16[16,400,128]{2,1,0:T(8,128)(2,1)S(1)} %constant_dynamic-update-slice_fusion.c), channel_id=1, source_target_pairs={{0,32},{32,0},{1,33},{33,1},{2,34},{34,2},{3,35},{35,3},{4,36},{36... | collective-permute-start | bytes 4915208 | tf_op jit(solution)/shard_map/left_core/ppermute | solution.py:228
  121.6 0.6 slice.13
  122.9 2.0 %collective-permute-done.4.d = bf16[16,400,128]{2,1,0:T(8,128)(2,1)} collective-permute-done((bf16[16,400,128]{2,1,0:T(8,128)(2,1)S(1)}, bf16[16,400,128]{2,1,0:T(8,128)(2,1)}, u32[]{:S(2)}, u32[]{:S(2)}) %collective-permute-start.4) | collective-permute-done | bytes 1638432 | tf_op jit(solution)/shard_map/left_core/ppermute | solution.py:228
  124.9 0.0 all-to-all-done.3.e
  124.9 3.0 %multiply.1 = bf16[128,512]{1,0:T(8,128)(2,1)S(1)} custom-call(s32[3]{0:T(128)S(1)} %pad_add_fusion.1.place.a, s32[16,128]{1,0:T(8,128)S(1)} %get-tuple-element.102.b, bf16[16,400,128]{2,1,0:T(8,128)(2,1)S(1)} %constant_dynamic-update-slice_fusion.c, bf16[16,400,128]{2,1,0:T(8,128)(2,1)} %collective-permute-done.4.d, bf16[16,32,512]{2,1,0:T(8,128)(2,1)S(1)} %all-to-all-done.3.e), custom_call_target="tpu_custom_call" | custom-call | tf_op jit(solution)/shard_map/multiply/pallas_call | solution.py:159
  127.9 0.0 copy-start.5
  127.9 0.6 copy-done.5
  (7 shorter events, 0.1 us)
Async XLA Ops:
  0.1 0.9 copy-start.1
  1.0 0.7 copy-start.2
  55.0 15.9 %all-to-all-start.1 = ((bf16[8,16,128]{2,1,0:T(8,128)(2,1)}), bf16[8,16,128]{2,1,0:T(8,128)(2,1)S(1)}, u32[]{:S(2)}, u32[]{:S(2)}) async-start(bf16[8,16,128]{2,1,0:T(8,128)(2,1)} %broadcast_in_dim.2), calls=%async_computation.1 | async-start | bytes 65536 | tf_op jit(solution)/shard_map/left_ids/all_to_all | solution.py:190
  66.3 0.9 copy-start
  67.2 0.7 copy-start.3
  67.8 0.7 copy-start.4
  71.7 26.8 %all-to-all-start.2 = ((bf16[32,8,640]{2,1,0:T(8,128)(2,1)}), bf16[32,8,640]{2,1,0:T(8,128)(2,1)}, u32[]{:S(2)}, u32[]{:S(2)}) async-start(bf16[32,8,640]{2,1,0:T(8,128)(2,1)} %scatter_right.3), calls=%async_computation.2 | async-start | bytes 655360 | tf_op jit(solution)/shard_map/scatter_right/all_to_all | solution.py:215
  80.2 11.9 %collective-permute-start.1 = (bf16[4,400,128]{2,1,0:T(8,128)(2,1)S(1)}, bf16[4,400,128]{2,1,0:T(8,128)(2,1)S(1)}, u32[]{:S(2)}, u32[]{:S(2)}) collective-permute-start(bf16[4,400,128]{2,1,0:T(8,128)(2,1)S(1)} %bitcast.22), channel_id=1, source_target_pairs={{0,768},{256,0},{512,256},{768,512},{1,769},{257,1},{513,257},{769... | collective-permute-start | bytes 1228808 | tf_op jit(solution)/shard_map/left_y/ppermute | solution.py:223
  83.0 12.9 %collective-permute-start = (bf16[4,400,128]{2,1,0:T(8,128)(2,1)S(1)}, bf16[4,400,128]{2,1,0:T(8,128)(2,1)S(1)}, u32[]{:S(2)}, u32[]{:S(2)}) collective-permute-start(bf16[4,400,128]{2,1,0:T(8,128)(2,1)S(1)} %bitcast.23), channel_id=1, source_target_pairs={{0,256},{256,512},{512,768},{768,0},{1,257},{257,513},{513,769},{7... | collective-permute-start | bytes 1228808 | tf_op jit(solution)/shard_map/left_y/ppermute | solution.py:222
  101.2 23.7 %all-to-all-start.3 = ((bf16[16,32,512]{2,1,0:T(8,128)(2,1)}), bf16[16,32,512]{2,1,0:T(8,128)(2,1)S(1)}, u32[]{:S(2)}, u32[]{:S(2)}) async-start(bf16[16,32,512]{2,1,0:T(8,128)(2,1)} %get-tuple-element.103), calls=%async_computation.3 | async-start | bytes 1048576 | tf_op jit(solution)/shard_map/right_needed/all_to_all | solution.py:261
  106.4 8.0 %collective-permute-start.2 = (bf16[2,400,128]{2,1,0:T(8,128)(2,1)S(1)}, bf16[2,400,128]{2,1,0:T(8,128)(2,1)S(1)}, u32[]{:S(2)}, u32[]{:S(2)}) collective-permute-start(bf16[2,400,128]{2,1,0:T(8,128)(2,1)S(1)} %slice.17), channel_id=1, source_target_pairs={{0,256},{256,512},{512,768},{768,0},{1,257},{257,513},{513,769},{7... | collective-permute-start | bytes 614408 | tf_op jit(solution)/shard_map/left_y/ppermute | solution.py:224
  108.7 7.0 %collective-permute-start.3 = (bf16[2,400,128]{2,1,0:T(8,128)(2,1)S(1)}, bf16[2,400,128]{2,1,0:T(8,128)(2,1)S(1)}, u32[]{:S(2)}, u32[]{:S(2)}) collective-permute-start(bf16[2,400,128]{2,1,0:T(8,128)(2,1)S(1)} %slice.18), channel_id=1, source_target_pairs={{0,768},{256,0},{512,256},{768,512},{1,769},{257,1},{513,257},{769... | collective-permute-start | bytes 614408 | tf_op jit(solution)/shard_map/left_y/ppermute | solution.py:224
  115.7 9.1 %collective-permute-start.4 = (bf16[16,400,128]{2,1,0:T(8,128)(2,1)S(1)}, bf16[16,400,128]{2,1,0:T(8,128)(2,1)}, u32[]{:S(2)}, u32[]{:S(2)}) collective-permute-start(bf16[16,400,128]{2,1,0:T(8,128)(2,1)S(1)} %constant_dynamic-update-slice_fusion.c), channel_id=1, source_target_pairs={{0,32},{32,0},{1,33},{33,1},{2,34},{34,2},{3,35},{35,3},{4,36},{36... | collective-permute-start | bytes 4915208 | tf_op jit(solution)/shard_map/left_core/ppermute | solution.py:228
  127.9 0.7 copy-start.5

commit v3 on v2

--- a/solution.py
+++ b/solution.py
@@ -55,16 +55,10 @@
     message[:, :, WIDE * TILE :] = jnp.broadcast_to(facts[None], (GROUP, MSG, TILE)).astype(BF16)
 
 
-def left_kernel(place, ids, left, payload):
+def left_kernel(near_ids, left, facts, payload):
     for a in range(LEFT):
         payload[a * TILE : (a + 1) * TILE, :] = left[a]
-    lane = iota((IDS, TILE), 1)
-    facts = jnp.zeros((IDS, TILE), I32)
-    for a in range(LEFT):
-        key = ids[1, a]
-        here = (iota((IDS, TILE), 0) == 0) & (lane == place[0] * LEFT + a)
-        facts = jnp.where(here, jnp.where(key >= 0, lax.shift_right_logical(key, 5) + 1, 0), facts)
-    payload[PANEL:, :] = facts.astype(F32).astype(BF16)
+    payload[PANEL:, :] = jnp.sum(near_ids[...].astype(F32), axis=0).astype(BF16)
 
 
 def select_kernel(place, pieces, below, above, message, wanted, facts):
@@ -171,23 +165,14 @@
     place = jnp.stack([row, col, 0]).astype(I32)
     lines = PIECE * PLACES
 
-    with jax.named_scope("left_zh"):
-        payload = kernel_call(
-            left_kernel,
-            jax.ShapeDtypeStruct((PANEL + IDS, TILE), BF16),
-            [],
-            "ssv",
-            place,
-            left_index[0, 0],
-            left_tiles[0, 0],
-        )
-        slab = lax.all_gather(payload, "zh")
-
     with jax.named_scope("left_ids"):
-        ids = jnp.sum(slab[:, PANEL:, :].astype(F32), axis=0).astype(BF16)
+        key = left_index[0, 0, 1]
+        values = jnp.where(key >= 0, lax.shift_right_logical(key, 5) + 1, 0)
+        here = iota((LEFT, TILE), 1) == row * LEFT + iota((LEFT, TILE), 0)
+        ids = jnp.sum(jnp.where(here, values[:, None], 0), axis=0).astype(F32).astype(BF16)
         near = ("y", "core")
-        ids = jnp.broadcast_to(ids[None], (lax.axis_size(near), IDS, TILE))
-        ids = lax.all_to_all(ids, near, 0, 0, tiled=True)
+        near_ids = jnp.broadcast_to(ids[None, None], (lax.axis_size(near), IDS, TILE))
+        near_ids = lax.all_to_all(near_ids, near, 0, 0, tiled=True)
 
     with jax.named_scope("scatter_right"):
         data, own_facts = kernel_call(
@@ -203,6 +188,19 @@
             keep_mask,
             right_tiles[0, 0],
         )
+    with jax.named_scope("left_zh"):
+        payload = kernel_call(
+            left_kernel,
+            jax.ShapeDtypeStruct((PANEL + IDS, TILE), BF16),
+            [],
+            "vva",
+            near_ids,
+            left_tiles[0, 0],
+            own_facts,
+        )
+        slab = lax.all_gather(payload, "zh")
+
+    with jax.named_scope("right_message"):
         message = kernel_call(
             message_kernel,
             jax.ShapeDtypeStruct((GROUP, MSG, (WIDE + 1) * TILE), BF16),
@@ -210,7 +208,7 @@
             "vvv",
             data,
             own_facts,
-            ids,
+            slab[:, PANEL:, :],
         )
         pieces = lax.all_to_all(message, COL, 0, 0, tiled=True)
 

time: 129 us -> 124 us (0.961)
  blocking collectives: 52.2 us -> 42.9 us
  starting transfers between devices: 42.5 us -> 48.6 us
  Pallas kernels: 7.67 us -> 6.21 us
    all_gather x1, blocking collectives: 52.2 us -> 42.9 us  [on_device(): slab = lax.all_gather(payload, 'zh')]
    all_to_all x1, starting transfers between devices: 11.2 us -> 17.4 us  [on_device(): near_ids = lax.all_to_all(near_ids, near, 0, 0, tiled=True)]
    ppermute x1, waiting for transfers between devices: 6.65 us -> 3.4 us  [on_device(): above = lax.ppermute(slab, 'y', down)]
    ppermute x1, waiting for transfers between devices: 1.21 us -> 4.26 us  [on_device(): lax.ppermute(above[half:], 'y', down)]
    all_to_all x1, starting transfers between devices: 8.47 us -> 5.64 us  [on_device(): pieces = lax.all_to_all(message, COL, 0, 0, tiled=True)]
    ppermute x1, starting transfers between devices: 5.89 us -> 8.69 us  [on_device(): left_there = lax.ppermute(left_here, 'core', [(0, 1), (1, 0)])]
    pallas_call x5, Pallas kernels: 7.67 us -> 6.21 us  [kernel_call(): pl.pallas_call(body, out_shape=out_shape, in_specs=specs, out_specs=tuple...]
    unnamed x16 -> x14, local copies, waits for them, and re-layouts: 4.6 us -> 3.92 us
  transfers between devices with their start and end apart: 8 -> 8, of which waited for: 7 -> 7; matrix products, arithmetic and copies ran while one was open for 1% -> 1% of each run, Pallas kernels for 0% -> 1%
where the time goes in v3:
time: 124 us; the launch traced here: 123 us
  starting transfers between devices  48.6 us (39%)
  blocking collectives  42.9 us (35%)
  waiting for transfers between devices  18.6 us (15%)
  Pallas kernels  6.21 us (5%)
  local copies, waits for them, and re-layouts  5.21 us (4%)
    all_gather x1, blocking collectives, on_device(): slab = lax.all_gather(payload, 'zh')  42.9 us
    all_to_all x1, starting transfers between devices, on_device(): near_ids = lax.all_to_all(near_ids, near, 0, 0, tiled=True)  17.4 us
    ppermute x1, starting transfers between devices, on_device(): left_there = lax.ppermute(left_here, 'core', [(0, 1), (1, 0)])  8.69 us
    pallas_call x5, Pallas kernels, kernel_call(): pl.pallas_call(body, out_shape=out_shape, in_specs=specs, out_specs=tuple...  6.21 us
    all_to_all x1, starting transfers between devices, on_device(): pieces = lax.all_to_all(message, COL, 0, 0, tiled=True)  5.64 us
    all_to_all x1, starting transfers between devices, on_device(): tiles = lax.all_to_all(packed, HALF, 0, 0, tiled=True)  5.1 us
    ppermute x1, starting transfers between devices, on_device(): lax.ppermute(above[half:], 'y', down)  4.57 us
    ppermute x1, waiting for transfers between devices, on_device(): below = lax.ppermute(slab, 'y', up)  4.41 us
  transfers between devices with their start and end apart: 8, of which 7 were waited for; matrix products, arithmetic and copies ran while one was open for 1% of the time, Pallas kernels for 1%

profile of v3, /device:TPU:1, one launch (start us, length us, event | category | flops | bytes accessed | tf_op | source)
XLA Modules:
  0.0 123.2 jit_solution(2398411937662734454)
XLA Ops:
  0.0 0.7 fusion
  0.7 0.1 select_reduce_fusion
  0.8 0.6 broadcast_in_dim.23
  1.4 17.4 %all-to-all-start.1 = ((bf16[8,16,128]{2,1,0:T(8,128)(2,1)}), bf16[8,16,128]{2,1,0:T(8,128)(2,1)S(1)}, u32[]{:S(2)}, u32[]{:S(2)}) async-start(bf16[8,16,128]{2,1,0:T(8,128)(2,1)} %broadcast_in_dim.23), calls=%async_computation.1 | async-start | bytes 65536 | tf_op jit(solution)/shard_map/left_ids/all_to_all | solution.py:175
  18.8 0.1 pad_add_fusion.1.place.a
  18.9 0.0 copy-start
  18.9 0.9 copy-done
  19.8 0.0 copy-start.2
  19.8 0.7 copy-done.2
  20.5 0.0 copy-start.3
  20.5 0.7 copy-done.3
  21.1 0.6 scatter_right.1
  21.8 1.8 %all-to-all-done.1.near_ids = bf16[8,16,128]{2,1,0:T(8,128)(2,1)S(1)} async-done(((bf16[8,16,128]{2,1,0:T(8,128)(2,1)}), bf16[8,16,128]{2,1,0:T(8,128)(2,1)S(1)}, u32[]{:S(2)}, u32[]{:S(2)}) %all-to-all-start.1) | async-done | bytes 32800 | tf_op jit(solution)/shard_map/left_ids/all_to_all | solution.py:175
  23.5 0.0 copy-start.1
  23.5 0.9 copy-done.1
  24.5 42.9 %all-gather = bf16[1600,128]{1,0:T(8,128)(2,1)S(1)} all-gather(bf16[400,128]{1,0:T(8,128)(2,1)S(1)} %left_zh.1), channel_id=2, replica_groups=mesh['y'=4,'zh'=4,'core'=2,'zb'=2,'zl'=4,'x'=4] {'zh'}, dimensions={0}, use_global_device_ids=true | all-gather | bytes 512000 | tf_op jit(solution)/shard_map/left_zh/all_gather | solution.py:201
  67.4 0.8 right_message.1
  68.1 5.6 %all-to-all-start.2 = ((bf16[32,8,640]{2,1,0:T(8,128)(2,1)}), bf16[32,8,640]{2,1,0:T(8,128)(2,1)}, u32[]{:S(2)}, u32[]{:S(2)}) async-start(bf16[32,8,640]{2,1,0:T(8,128)(2,1)} %right_message.1), calls=%async_computation.2 | async-start | bytes 655360 | tf_op jit(solution)/shard_map/right_message/all_to_all | solution.py:213
  73.8 2.8 %collective-permute-start.1 = (bf16[4,400,128]{2,1,0:T(8,128)(2,1)S(1)}, bf16[4,400,128]{2,1,0:T(8,128)(2,1)S(1)}, u32[]{:S(2)}, u32[]{:S(2)}) collective-permute-start(bf16[4,400,128]{2,1,0:T(8,128)(2,1)S(1)} %bitcast.22), channel_id=1, source_target_pairs={{0,768},{256,0},{512,256},{768,512},{1,769},{257,1},{513,257},{769... | collective-permute-start | bytes 1228808 | tf_op jit(solution)/shard_map/left_y/ppermute | solution.py:221
  76.6 2.5 %collective-permute-start = (bf16[4,400,128]{2,1,0:T(8,128)(2,1)S(1)}, bf16[4,400,128]{2,1,0:T(8,128)(2,1)S(1)}, u32[]{:S(2)}, u32[]{:S(2)}) collective-permute-start(bf16[4,400,128]{2,1,0:T(8,128)(2,1)S(1)} %bitcast.23), channel_id=1, source_target_pairs={{0,256},{256,512},{512,768},{768,0},{1,257},{257,513},{513,769},{7... | collective-permute-start | bytes 1228808 | tf_op jit(solution)/shard_map/left_y/ppermute | solution.py:220
  79.1 3.4 %collective-permute-done.1.above = bf16[4,400,128]{2,1,0:T(8,128)(2,1)S(1)} collective-permute-done((bf16[4,400,128]{2,1,0:T(8,128)(2,1)S(1)}, bf16[4,400,128]{2,1,0:T(8,128)(2,1)S(1)}, u32[]{:S(2)}, u32[]{:S(2)}) %collective-permute-start.1) | collective-permute-done | bytes 409632 | tf_op jit(solution)/shard_map/left_y/ppermute | solution.py:221
  82.5 4.4 %collective-permute-done.below = bf16[4,400,128]{2,1,0:T(8,128)(2,1)S(1)} collective-permute-done((bf16[4,400,128]{2,1,0:T(8,128)(2,1)S(1)}, bf16[4,400,128]{2,1,0:T(8,128)(2,1)S(1)}, u32[]{:S(2)}, u32[]{:S(2)}) %collective-permute-start) | collective-permute-done | bytes 409632 | tf_op jit(solution)/shard_map/left_y/ppermute | solution.py:220
  86.9 1.7 %all-to-all-done.2.pieces = bf16[32,8,640]{2,1,0:T(8,128)(2,1)} async-done(((bf16[32,8,640]{2,1,0:T(8,128)(2,1)}), bf16[32,8,640]{2,1,0:T(8,128)(2,1)}, u32[]{:S(2)}, u32[]{:S(2)}) %all-to-all-start.2) | async-done | bytes 327712 | tf_op jit(solution)/shard_map/right_message/all_to_all | solution.py:213
  88.5 2.7 %right_needed.1 = (bf16[16,32,512]{2,1,0:T(8,128)(2,1)}, s32[16,128]{1,0:T(8,128)S(1)}) custom-call(s32[3]{0:T(128)S(1)} %pad_add_fusion.1.place.a, bf16[32,8,640]{2,1,0:T(8,128)(2,1)} %all-to-all-done.2.pieces, bf16[4,400,128]{2,1,0:T(8,128)(2,1)S(1)} %collective-permute-done.below, bf16[4,400,128]{2,1,0:T(8,128)(2,1)S(1)} %collective-permute-done.1.above), custom_call_target="tpu_custom_call" | custom-call | tf_op jit(solution)/shard_map/right_needed/pallas_call | solution.py:153
  91.2 5.1 %all-to-all-start.3 = ((bf16[16,32,512]{2,1,0:T(8,128)(2,1)}), bf16[16,32,512]{2,1,0:T(8,128)(2,1)S(1)}, u32[]{:S(2)}, u32[]{:S(2)}) async-start(bf16[16,32,512]{2,1,0:T(8,128)(2,1)} %get-tuple-element.103), calls=%async_computation.3 | async-start | bytes 1048576 | tf_op jit(solution)/shard_map/right_needed/all_to_all | solution.py:259
  96.4 1.9 %collective-permute-start.2 = (bf16[2,400,128]{2,1,0:T(8,128)(2,1)S(1)}, bf16[2,400,128]{2,1,0:T(8,128)(2,1)S(1)}, u32[]{:S(2)}, u32[]{:S(2)}) collective-permute-start(bf16[2,400,128]{2,1,0:T(8,128)(2,1)S(1)} %slice.21), channel_id=1, source_target_pairs={{0,256},{256,512},{512,768},{768,0},{1,257},{257,513},{513,769},{7... | collective-permute-start | bytes 614408 | tf_op jit(solution)/shard_map/left_y/ppermute | solution.py:222
  98.4 4.6 %collective-permute-start.3 = (bf16[2,400,128]{2,1,0:T(8,128)(2,1)S(1)}, bf16[2,400,128]{2,1,0:T(8,128)(2,1)S(1)}, u32[]{:S(2)}, u32[]{:S(2)}) collective-permute-start(bf16[2,400,128]{2,1,0:T(8,128)(2,1)S(1)} %slice.22), channel_id=1, source_target_pairs={{0,768},{256,0},{512,256},{768,512},{1,769},{257,1},{513,257},{769... | collective-permute-start | bytes 614408 | tf_op jit(solution)/shard_map/left_y/ppermute | solution.py:222
  102.9 0.1 constant_dynamic-update-slice_fusion.3
  103.0 1.1 collective-permute-done.2
  104.1 4.3 %collective-permute-done.3 = bf16[2,400,128]{2,1,0:T(8,128)(2,1)S(1)} collective-permute-done((bf16[2,400,128]{2,1,0:T(8,128)(2,1)S(1)}, bf16[2,400,128]{2,1,0:T(8,128)(2,1)S(1)}, u32[]{:S(2)}, u32[]{:S(2)}) %collective-permute-start.3) | collective-permute-done | bytes 204832 | tf_op jit(solution)/shard_map/left_y/ppermute | solution.py:222
  108.4 0.1 constant_dynamic-update-slice_fusion.c
  108.5 8.7 %collective-permute-start.4 = (bf16[16,400,128]{2,1,0:T(8,128)(2,1)S(1)}, bf16[16,400,128]{2,1,0:T(8,128)(2,1)}, u32[]{:S(2)}, u32[]{:S(2)}) collective-permute-start(bf16[16,400,128]{2,1,0:T(8,128)(2,1)S(1)} %constant_dynamic-update-slice_fusion.c), channel_id=1, source_target_pairs={{0,32},{32,0},{1,33},{33,1},{2,34},{34,2},{3,35},{35,3},{4,36},{36... | collective-permute-start | bytes 4915208 | tf_op jit(solution)/shard_map/left_core/ppermute | solution.py:226
  117.2 0.6 slice.17
  118.4 2.0 %collective-permute-done.4.d = bf16[16,400,128]{2,1,0:T(8,128)(2,1)} collective-permute-done((bf16[16,400,128]{2,1,0:T(8,128)(2,1)S(1)}, bf16[16,400,128]{2,1,0:T(8,128)(2,1)}, u32[]{:S(2)}, u32[]{:S(2)}) %collective-permute-start.4) | collective-permute-done | bytes 1638432 | tf_op jit(solution)/shard_map/left_core/ppermute | solution.py:226
  120.4 0.0 all-to-all-done.3.e
  120.4 2.1 %multiply.1 = bf16[128,512]{1,0:T(8,128)(2,1)S(1)} custom-call(s32[3]{0:T(128)S(1)} %pad_add_fusion.1.place.a, s32[16,128]{1,0:T(8,128)S(1)} %get-tuple-element.102.b, bf16[16,400,128]{2,1,0:T(8,128)(2,1)S(1)} %constant_dynamic-update-slice_fusion.c, bf16[16,400,128]{2,1,0:T(8,128)(2,1)} %collective-permute-done.4.d, bf16[16,32,512]{2,1,0:T(8,128)(2,1)S(1)} %all-to-all-done.3.e), custom_call_target="tpu_custom_call" | custom-call | tf_op jit(solution)/shard_map/multiply/pallas_call | solution.py:153
  122.5 0.0 copy-start.4
  122.5 0.6 copy-done.4
  (10 shorter events, 0.2 us)
Async XLA Ops:
  1.4 22.1 %all-to-all-start.1 = ((bf16[8,16,128]{2,1,0:T(8,128)(2,1)}), bf16[8,16,128]{2,1,0:T(8,128)(2,1)S(1)}, u32[]{:S(2)}, u32[]{:S(2)}) async-start(bf16[8,16,128]{2,1,0:T(8,128)(2,1)} %broadcast_in_dim.23), calls=%async_computation.1 | async-start | bytes 65536 | tf_op jit(solution)/shard_map/left_ids/all_to_all | solution.py:175
  18.9 0.9 copy-start
  19.8 0.7 copy-start.2
  20.5 0.7 copy-start.3
  23.5 0.9 copy-start.1
  68.1 20.4 %all-to-all-start.2 = ((bf16[32,8,640]{2,1,0:T(8,128)(2,1)}), bf16[32,8,640]{2,1,0:T(8,128)(2,1)}, u32[]{:S(2)}, u32[]{:S(2)}) async-start(bf16[32,8,640]{2,1,0:T(8,128)(2,1)} %right_message.1), calls=%async_computation.2 | async-start | bytes 655360 | tf_op jit(solution)/shard_map/right_message/all_to_all | solution.py:213
  73.8 8.7 %collective-permute-start.1 = (bf16[4,400,128]{2,1,0:T(8,128)(2,1)S(1)}, bf16[4,400,128]{2,1,0:T(8,128)(2,1)S(1)}, u32[]{:S(2)}, u32[]{:S(2)}) collective-permute-start(bf16[4,400,128]{2,1,0:T(8,128)(2,1)S(1)} %bitcast.22), channel_id=1, source_target_pairs={{0,768},{256,0},{512,256},{768,512},{1,769},{257,1},{513,257},{769... | collective-permute-start | bytes 1228808 | tf_op jit(solution)/shard_map/left_y/ppermute | solution.py:221
  76.6 10.3 %collective-permute-start = (bf16[4,400,128]{2,1,0:T(8,128)(2,1)S(1)}, bf16[4,400,128]{2,1,0:T(8,128)(2,1)S(1)}, u32[]{:S(2)}, u32[]{:S(2)}) collective-permute-start(bf16[4,400,128]{2,1,0:T(8,128)(2,1)S(1)} %bitcast.23), channel_id=1, source_target_pairs={{0,256},{256,512},{512,768},{768,0},{1,257},{257,513},{513,769},{7... | collective-permute-start | bytes 1228808 | tf_op jit(solution)/shard_map/left_y/ppermute | solution.py:220
  91.2 29.2 %all-to-all-start.3 = ((bf16[16,32,512]{2,1,0:T(8,128)(2,1)}), bf16[16,32,512]{2,1,0:T(8,128)(2,1)S(1)}, u32[]{:S(2)}, u32[]{:S(2)}) async-start(bf16[16,32,512]{2,1,0:T(8,128)(2,1)} %get-tuple-element.103), calls=%async_computation.3 | async-start | bytes 1048576 | tf_op jit(solution)/shard_map/right_needed/all_to_all | solution.py:259
  96.4 7.7 %collective-permute-start.2 = (bf16[2,400,128]{2,1,0:T(8,128)(2,1)S(1)}, bf16[2,400,128]{2,1,0:T(8,128)(2,1)S(1)}, u32[]{:S(2)}, u32[]{:S(2)}) collective-permute-start(bf16[2,400,128]{2,1,0:T(8,128)(2,1)S(1)} %slice.21), channel_id=1, source_target_pairs={{0,256},{256,512},{512,768},{768,0},{1,257},{257,513},{513,769},{7... | collective-permute-start | bytes 614408 | tf_op jit(solution)/shard_map/left_y/ppermute | solution.py:222
  98.4 10.0 %collective-permute-start.3 = (bf16[2,400,128]{2,1,0:T(8,128)(2,1)S(1)}, bf16[2,400,128]{2,1,0:T(8,128)(2,1)S(1)}, u32[]{:S(2)}, u32[]{:S(2)}) collective-permute-start(bf16[2,400,128]{2,1,0:T(8,128)(2,1)S(1)} %slice.22), channel_id=1, source_target_pairs={{0,768},{256,0},{512,256},{768,512},{1,769},{257,1},{513,257},{769... | collective-permute-start | bytes 614408 | tf_op jit(solution)/shard_map/left_y/ppermute | solution.py:222
  108.5 11.9 %collective-permute-start.4 = (bf16[16,400,128]{2,1,0:T(8,128)(2,1)S(1)}, bf16[16,400,128]{2,1,0:T(8,128)(2,1)}, u32[]{:S(2)}, u32[]{:S(2)}) collective-permute-start(bf16[16,400,128]{2,1,0:T(8,128)(2,1)S(1)} %constant_dynamic-update-slice_fusion.c), channel_id=1, source_target_pairs={{0,32},{32,0},{1,33},{33,1},{2,34},{34,2},{3,35},{35,3},{4,36},{36... | collective-permute-start | bytes 4915208 | tf_op jit(solution)/shard_map/left_core/ppermute | solution.py:226
  122.5 0.7 copy-start.4

commit v4 on v3

--- a/solution.py
+++ b/solution.py
@@ -216,11 +216,12 @@
         size = lax.axis_size("y")
         up = [(i, (i + 1) % size) for i in range(size)]
         down = [(i, (i - 1) % size) for i in range(size)]
-        half = slab.shape[0] // 2
+        ring = [(2 * y + core, (y + 1 - 2 * core) % size * 2 + core) for y in range(size) for core in range(2)]
         below = lax.ppermute(slab, "y", up)
         above = lax.ppermute(slab, "y", down)
-        far = (lax.ppermute(below[:half], "y", up), lax.ppermute(above[half:], "y", down))
-        left_here = jnp.concatenate((slab, below) + far + (above,))
+        onward = jnp.where(lax.axis_index("core") == 0, below, above)
+        far = lax.ppermute(onward, ("y", "core"), ring)
+        left_here = jnp.concatenate((slab, below, far, above))
 
     with jax.named_scope("left_core"):
         left_there = lax.ppermute(left_here, "core", [(0, 1), (1, 0)])

time: 124 us -> 126 us (1.016)
    ppermute x1, starting transfers between devices: 8.69 us -> 12.7 us  [on_device(): left_there = lax.ppermute(left_here, 'core', [(0, 1), (1, 0)])]
    ppermute x2 -> x1, starting transfers between devices: 6.49 us -> 3.09 us  [on_device(): far = lax.ppermute(onward, ('y', 'core'), ring)]
    ppermute x2 -> x1, waiting for transfers between devices: 5.34 us -> 5.6 us  [on_device(): far = lax.ppermute(onward, ('y', 'core'), ring)]
    unnamed x14 -> x10, local copies, waits for them, and re-layouts: 3.92 us -> 3.78 us
  transfers between devices with their start and end apart: 8 -> 7, of which waited for: 7 -> 6; matrix products, arithmetic and copies ran while one was open for 1% -> 1% of each run, Pallas kernels for 1% -> 1%
where the time goes in v4:
time: 126 us; the launch traced here: 125 us
  starting transfers between devices  49.2 us (39%)
  blocking collectives  42.9 us (34%)
  waiting for transfers between devices  18.8 us (15%)
  Pallas kernels  6.96 us (6%)
  local copies, waits for them, and re-layouts  4.99 us (4%)
    all_gather x1, blocking collectives, on_device(): slab = lax.all_gather(payload, 'zh')  42.9 us
    all_to_all x1, starting transfers between devices, on_device(): near_ids = lax.all_to_all(near_ids, near, 0, 0, tiled=True)  17.4 us
    ppermute x1, starting transfers between devices, on_device(): left_there = lax.ppermute(left_here, 'core', [(0, 1), (1, 0)])  12.7 us
    pallas_call x5, Pallas kernels, kernel_call(): pl.pallas_call(body, out_shape=out_shape, in_specs=specs, out_specs=tuple...  6.96 us
    all_to_all x1, starting transfers between devices, on_device(): pieces = lax.all_to_all(message, COL, 0, 0, tiled=True)  5.64 us
    ppermute x1, waiting for transfers between devices, on_device(): far = lax.ppermute(onward, ('y', 'core'), ring)  5.6 us
    all_to_all x1, starting transfers between devices, on_device(): tiles = lax.all_to_all(packed, HALF, 0, 0, tiled=True)  5.11 us
    ppermute x1, waiting for transfers between devices, on_device(): below = lax.ppermute(slab, 'y', up)  4.41 us
  transfers between devices with their start and end apart: 7, of which 6 were waited for; matrix products, arithmetic and copies ran while one was open for 1% of the time, Pallas kernels for 1%

profile of v4, /device:TPU:1, one launch (start us, length us, event | category | flops | bytes accessed | tf_op | source)
XLA Modules:
  0.0 124.8 jit_solution(7762245467508247137)
XLA Ops:
  0.0 0.7 fusion
  0.7 0.1 select_reduce_fusion
  0.8 0.6 broadcast_in_dim.23
  1.4 17.4 %all-to-all-start.1 = ((bf16[8,16,128]{2,1,0:T(8,128)(2,1)}), bf16[8,16,128]{2,1,0:T(8,128)(2,1)S(1)}, u32[]{:S(2)}, u32[]{:S(2)}) async-start(bf16[8,16,128]{2,1,0:T(8,128)(2,1)} %broadcast_in_dim.23), calls=%async_computation.1 | async-start | bytes 65536 | tf_op jit(solution)/shard_map/left_ids/all_to_all | solution.py:175
  18.8 0.1 pad_add_fusion.1.place.a
  18.9 0.0 copy-start
  18.9 0.9 copy-done
  19.8 0.0 copy-start.2
  19.8 0.7 copy-done.2
  20.5 0.0 copy-start.3
  20.5 0.7 copy-done.3
  21.1 0.6 scatter_right.1
  21.8 1.8 %all-to-all-done.1.near_ids = bf16[8,16,128]{2,1,0:T(8,128)(2,1)S(1)} async-done(((bf16[8,16,128]{2,1,0:T(8,128)(2,1)}), bf16[8,16,128]{2,1,0:T(8,128)(2,1)S(1)}, u32[]{:S(2)}, u32[]{:S(2)}) %all-to-all-start.1) | async-done | bytes 32800 | tf_op jit(solution)/shard_map/left_ids/all_to_all | solution.py:175
  23.5 0.0 copy-start.1
  23.5 0.9 copy-done.1
  24.5 42.9 %all-gather = bf16[1600,128]{1,0:T(8,128)(2,1)S(1)} all-gather(bf16[400,128]{1,0:T(8,128)(2,1)S(1)} %left_zh.1), channel_id=2, replica_groups=mesh['y'=4,'zh'=4,'core'=2,'zb'=2,'zl'=4,'x'=4] {'zh'}, dimensions={0}, use_global_device_ids=true | all-gather | bytes 512000 | tf_op jit(solution)/shard_map/left_zh/all_gather | solution.py:201
  67.4 0.8 right_message.1
  68.1 5.6 %all-to-all-start.2 = ((bf16[32,8,640]{2,1,0:T(8,128)(2,1)}), bf16[32,8,640]{2,1,0:T(8,128)(2,1)}, u32[]{:S(2)}, u32[]{:S(2)}) async-start(bf16[32,8,640]{2,1,0:T(8,128)(2,1)} %right_message.1), calls=%async_computation.2 | async-start | bytes 655360 | tf_op jit(solution)/shard_map/right_message/all_to_all | solution.py:213
  73.8 2.8 %collective-permute-start.1 = (bf16[4,400,128]{2,1,0:T(8,128)(2,1)S(1)}, bf16[4,400,128]{2,1,0:T(8,128)(2,1)S(1)}, u32[]{:S(2)}, u32[]{:S(2)}) collective-permute-start(bf16[4,400,128]{2,1,0:T(8,128)(2,1)S(1)} %bitcast.22), channel_id=1, source_target_pairs={{0,768},{256,0},{512,256},{768,512},{1,769},{257,1},{513,257},{769... | collective-permute-start | bytes 1228808 | tf_op jit(solution)/shard_map/left_y/ppermute | solution.py:221
  76.6 2.5 %collective-permute-start = (bf16[4,400,128]{2,1,0:T(8,128)(2,1)S(1)}, bf16[4,400,128]{2,1,0:T(8,128)(2,1)S(1)}, u32[]{:S(2)}, u32[]{:S(2)}) collective-permute-start(bf16[4,400,128]{2,1,0:T(8,128)(2,1)S(1)} %bitcast.23), channel_id=1, source_target_pairs={{0,256},{256,512},{512,768},{768,0},{1,257},{257,513},{513,769},{7... | collective-permute-start | bytes 1228808 | tf_op jit(solution)/shard_map/left_y/ppermute | solution.py:220
  79.1 3.4 %collective-permute-done.1.above = bf16[4,400,128]{2,1,0:T(8,128)(2,1)S(1)} collective-permute-done((bf16[4,400,128]{2,1,0:T(8,128)(2,1)S(1)}, bf16[4,400,128]{2,1,0:T(8,128)(2,1)S(1)}, u32[]{:S(2)}, u32[]{:S(2)}) %collective-permute-start.1) | collective-permute-done | bytes 409632 | tf_op jit(solution)/shard_map/left_y/ppermute | solution.py:221
  82.5 4.4 %collective-permute-done.below = bf16[4,400,128]{2,1,0:T(8,128)(2,1)S(1)} collective-permute-done((bf16[4,400,128]{2,1,0:T(8,128)(2,1)S(1)}, bf16[4,400,128]{2,1,0:T(8,128)(2,1)S(1)}, u32[]{:S(2)}, u32[]{:S(2)}) %collective-permute-start) | collective-permute-done | bytes 409632 | tf_op jit(solution)/shard_map/left_y/ppermute | solution.py:220
  86.9 1.7 %all-to-all-done.2.pieces = bf16[32,8,640]{2,1,0:T(8,128)(2,1)} async-done(((bf16[32,8,640]{2,1,0:T(8,128)(2,1)}), bf16[32,8,640]{2,1,0:T(8,128)(2,1)}, u32[]{:S(2)}, u32[]{:S(2)}) %all-to-all-start.2) | async-done | bytes 327712 | tf_op jit(solution)/shard_map/right_message/all_to_all | solution.py:213
  88.5 2.7 %right_needed.1 = (bf16[16,32,512]{2,1,0:T(8,128)(2,1)}, s32[16,128]{1,0:T(8,128)S(1)}) custom-call(s32[3]{0:T(128)S(1)} %pad_add_fusion.1.place.a, bf16[32,8,640]{2,1,0:T(8,128)(2,1)} %all-to-all-done.2.pieces, bf16[4,400,128]{2,1,0:T(8,128)(2,1)S(1)} %collective-permute-done.below, bf16[4,400,128]{2,1,0:T(8,128)(2,1)S(1)} %collective-permute-done.1.above), custom_call_target="tpu_custom_call" | custom-call | tf_op jit(solution)/shard_map/right_needed/pallas_call | solution.py:153
  91.2 5.1 %all-to-all-start.3 = ((bf16[16,32,512]{2,1,0:T(8,128)(2,1)}), bf16[16,32,512]{2,1,0:T(8,128)(2,1)S(1)}, u32[]{:S(2)}, u32[]{:S(2)}) async-start(bf16[16,32,512]{2,1,0:T(8,128)(2,1)} %get-tuple-element.103), calls=%async_computation.3 | async-start | bytes 1048576 | tf_op jit(solution)/shard_map/right_needed/all_to_all | solution.py:260
  96.4 3.1 %collective-permute-start.2 = (bf16[4,400,128]{2,1,0:T(8,128)(2,1)S(1)}, bf16[4,400,128]{2,1,0:T(8,128)(2,1)S(1)}, u32[]{:S(2)}, u32[]{:S(2)}) collective-permute-start(bf16[4,400,128]{2,1,0:T(8,128)(2,1)S(1)} %broadcast_select_fusion), channel_id=1, source_target_pairs={{0,256},{32,800},{256,512},{288,32},{512,768},{544,288},{768,0},{8... | collective-permute-start | bytes 1228808 | tf_op jit(solution)/shard_map/left_y/ppermute | solution.py:223
  99.5 5.6 %collective-permute-done.2 = bf16[4,400,128]{2,1,0:T(8,128)(2,1)S(1)} collective-permute-done((bf16[4,400,128]{2,1,0:T(8,128)(2,1)S(1)}, bf16[4,400,128]{2,1,0:T(8,128)(2,1)S(1)}, u32[]{:S(2)}, u32[]{:S(2)}) %collective-permute-start.2) | collective-permute-done | bytes 409632 | tf_op jit(solution)/shard_map/left_y/ppermute | solution.py:223
  105.1 0.2 pad_maximum_fusion.c
  105.3 12.7 %collective-permute-start.3 = (bf16[16,400,128]{2,1,0:T(8,128)(2,1)S(1)}, bf16[16,400,128]{2,1,0:T(8,128)(2,1)}, u32[]{:S(2)}, u32[]{:S(2)}) collective-permute-start(bf16[16,400,128]{2,1,0:T(8,128)(2,1)S(1)} %pad_maximum_fusion.c), channel_id=1, source_target_pairs={{0,32},{32,0},{1,33},{33,1},{2,34},{34,2},{3,35},{35,3},{4,36},{36... | collective-permute-start | bytes 4915208 | tf_op jit(solution)/shard_map/left_core/ppermute | solution.py:227
  118.0 0.6 slice.11
  119.2 2.0 %collective-permute-done.3.d = bf16[16,400,128]{2,1,0:T(8,128)(2,1)} collective-permute-done((bf16[16,400,128]{2,1,0:T(8,128)(2,1)S(1)}, bf16[16,400,128]{2,1,0:T(8,128)(2,1)}, u32[]{:S(2)}, u32[]{:S(2)}) %collective-permute-start.3) | collective-permute-done | bytes 1638432 | tf_op jit(solution)/shard_map/left_core/ppermute | solution.py:227
  121.2 0.0 all-to-all-done.3.e
  121.2 2.8 %multiply.1 = bf16[128,512]{1,0:T(8,128)(2,1)S(1)} custom-call(s32[3]{0:T(128)S(1)} %pad_add_fusion.1.place.a, s32[16,128]{1,0:T(8,128)S(1)} %get-tuple-element.102.b, bf16[16,400,128]{2,1,0:T(8,128)(2,1)S(1)} %pad_maximum_fusion.c, bf16[16,400,128]{2,1,0:T(8,128)(2,1)} %collective-permute-done.3.d, bf16[16,32,512]{2,1,0:T(8,128)(2,1)S(1)} %all-to-all-done.3.e), custom_call_target="tpu_custom_call" | custom-call | tf_op jit(solution)/shard_map/multiply/pallas_call | solution.py:153
  124.1 0.0 copy-start.4
  124.1 0.6 copy-done.4
  (6 shorter events, 0.1 us)
Async XLA Ops:
  1.4 22.1 %all-to-all-start.1 = ((bf16[8,16,128]{2,1,0:T(8,128)(2,1)}), bf16[8,16,128]{2,1,0:T(8,128)(2,1)S(1)}, u32[]{:S(2)}, u32[]{:S(2)}) async-start(bf16[8,16,128]{2,1,0:T(8,128)(2,1)} %broadcast_in_dim.23), calls=%async_computation.1 | async-start | bytes 65536 | tf_op jit(solution)/shard_map/left_ids/all_to_all | solution.py:175
  18.9 0.9 copy-start
  19.8 0.7 copy-start.2
  20.5 0.7 copy-start.3
  23.5 0.9 copy-start.1
  68.1 20.4 %all-to-all-start.2 = ((bf16[32,8,640]{2,1,0:T(8,128)(2,1)}), bf16[32,8,640]{2,1,0:T(8,128)(2,1)}, u32[]{:S(2)}, u32[]{:S(2)}) async-start(bf16[32,8,640]{2,1,0:T(8,128)(2,1)} %right_message.1), calls=%async_computation.2 | async-start | bytes 655360 | tf_op jit(solution)/shard_map/right_message/all_to_all | solution.py:213
  73.8 8.7 %collective-permute-start.1 = (bf16[4,400,128]{2,1,0:T(8,128)(2,1)S(1)}, bf16[4,400,128]{2,1,0:T(8,128)(2,1)S(1)}, u32[]{:S(2)}, u32[]{:S(2)}) collective-permute-start(bf16[4,400,128]{2,1,0:T(8,128)(2,1)S(1)} %bitcast.22), channel_id=1, source_target_pairs={{0,768},{256,0},{512,256},{768,512},{1,769},{257,1},{513,257},{769... | collective-permute-start | bytes 1228808 | tf_op jit(solution)/shard_map/left_y/ppermute | solution.py:221
  76.6 10.3 %collective-permute-start = (bf16[4,400,128]{2,1,0:T(8,128)(2,1)S(1)}, bf16[4,400,128]{2,1,0:T(8,128)(2,1)S(1)}, u32[]{:S(2)}, u32[]{:S(2)}) collective-permute-start(bf16[4,400,128]{2,1,0:T(8,128)(2,1)S(1)} %bitcast.23), channel_id=1, source_target_pairs={{0,256},{256,512},{512,768},{768,0},{1,257},{257,513},{513,769},{7... | collective-permute-start | bytes 1228808 | tf_op jit(solution)/shard_map/left_y/ppermute | solution.py:220
  91.2 30.0 %all-to-all-start.3 = ((bf16[16,32,512]{2,1,0:T(8,128)(2,1)}), bf16[16,32,512]{2,1,0:T(8,128)(2,1)S(1)}, u32[]{:S(2)}, u32[]{:S(2)}) async-start(bf16[16,32,512]{2,1,0:T(8,128)(2,1)} %get-tuple-element.103), calls=%async_computation.3 | async-start | bytes 1048576 | tf_op jit(solution)/shard_map/right_needed/all_to_all | solution.py:260
  96.4 8.7 %collective-permute-start.2 = (bf16[4,400,128]{2,1,0:T(8,128)(2,1)S(1)}, bf16[4,400,128]{2,1,0:T(8,128)(2,1)S(1)}, u32[]{:S(2)}, u32[]{:S(2)}) collective-permute-start(bf16[4,400,128]{2,1,0:T(8,128)(2,1)S(1)} %broadcast_select_fusion), channel_id=1, source_target_pairs={{0,256},{32,800},{256,512},{288,32},{512,768},{544,288},{768,0},{8... | collective-permute-start | bytes 1228808 | tf_op jit(solution)/shard_map/left_y/ppermute | solution.py:223
  105.3 15.9 %collective-permute-start.3 = (bf16[16,400,128]{2,1,0:T(8,128)(2,1)S(1)}, bf16[16,400,128]{2,1,0:T(8,128)(2,1)}, u32[]{:S(2)}, u32[]{:S(2)}) collective-permute-start(bf16[16,400,128]{2,1,0:T(8,128)(2,1)S(1)} %pad_maximum_fusion.c), channel_id=1, source_target_pairs={{0,32},{32,0},{1,33},{33,1},{2,34},{34,2},{3,35},{35,3},{4,36},{36... | collective-permute-start | bytes 4915208 | tf_op jit(solution)/shard_map/left_core/ppermute | solution.py:227
  124.1 0.7 copy-start.4

commit v5 on v4

--- a/solution.py
+++ b/solution.py
@@ -35,7 +35,7 @@
             strip = right[b, SPREAD * u : SPREAD * (u + 1), :].astype(F32)
             rows[u % WIDE, pl.ds(PIECE * b + u // WIDE, SPREAD, stride=MSG), :] = strip
     for v in range(WIDE):
-        data[:, :, v * TILE : (v + 1) * TILE] = rows[v].reshape(SPREAD, MSG, TILE).astype(BF16)
+        data[:, :, v * TILE : (v + 1) * TILE] = rows[v, 0 : SPREAD * MSG, :].reshape(SPREAD, MSG, TILE).astype(BF16)
     sub, lane = iota((MSG, TILE), 0), iota((MSG, TILE), 1)
     facts = jnp.zeros((MSG, TILE), I32)
     for b in range(RIGHT):
@@ -64,7 +64,7 @@
 def select_kernel(place, pieces, below, above, message, wanted, facts):
     row, col, base = place[0], place[1], place[2]
     first = (col // SPREAD) * SPREAD
-    facts[...] = pieces[:, :, WIDE * TILE :].astype(F32).reshape(GROUP * MSG, TILE)
+    facts[0 : GROUP * MSG, :] = pieces[:, :, WIDE * TILE :].astype(F32).reshape(GROUP * MSG, TILE)
     right_q = jnp.sum(facts[pl.ds(0, GROUP, stride=MSG), :], axis=0, keepdims=True)
     right_j = jnp.sum(facts[pl.ds(1, GROUP, stride=MSG), :], axis=0, keepdims=True)
     keep = facts[pl.ds(first * MSG + 3, SPREAD, stride=MSG), :]
@@ -114,7 +114,7 @@
 def product_kernel(place, wanted, left_here, left_there, pieces, start, out, rows, total):
     lines = PIECE * PLACES
     for v in range(WIDE):
-        rows[v] = pieces[:, :, v * TILE : (v + 1) * TILE].astype(F32).reshape(SPREAD * lines, TILE)
+        rows[v, 0 : SPREAD * lines, :] = pieces[:, :, v * TILE : (v + 1) * TILE].astype(F32).reshape(SPREAD * lines, TILE)
     if start is None:
         total[...] = jnp.zeros_like(total)
     else:
@@ -181,7 +181,7 @@
                 jax.ShapeDtypeStruct((SPREAD, MSG, WIDE * TILE), BF16),
                 jax.ShapeDtypeStruct((MSG, TILE), F32),
             ),
-            [pltpu.VMEM((WIDE, SPREAD * MSG, TILE), F32)],
+            [pltpu.VMEM((WIDE, (SPREAD + 1) * MSG, TILE), F32)],
             "sssv",
             place,
             right_index[0, 0],
@@ -233,7 +233,7 @@
                 jax.ShapeDtypeStruct((SPREAD, lines, WIDE * TILE), BF16),
                 jax.ShapeDtypeStruct((PLACES, TILE), I32),
             ),
-            [pltpu.VMEM((GROUP * MSG, TILE), F32)],
+            [pltpu.VMEM(((GROUP + 1) * MSG, TILE), F32)],
             "svaa",
             jnp.stack([row, col, base]).astype(I32),
             pieces,
@@ -250,7 +250,7 @@
         return kernel_call(
             body,
             jax.ShapeDtypeStruct(shape, dtype),
-            [pltpu.VMEM((WIDE, SPREAD * lines, TILE), F32), pltpu.VMEM(shape, F32)],
+            [pltpu.VMEM((WIDE, (SPREAD + 1) * lines, TILE), F32), pltpu.VMEM(shape, F32)],
             "ssvvvv"[: len(operands)],
             *operands,
         )

time: 126 us -> 125 us (level)
  no operation moved by 1% of the time
where the time goes in v5:
time: 125 us; the launch traced here: 124 us
  starting transfers between devices  49.2 us (39%)
  blocking collectives  42.9 us (34%)
  waiting for transfers between devices  18.8 us (15%)
  Pallas kernels  6.05 us (5%)
  local copies, waits for them, and re-layouts  4.99 us (4%)
    all_gather x1, blocking collectives, on_device(): slab = lax.all_gather(payload, 'zh')  42.9 us
    all_to_all x1, starting transfers between devices, on_device(): near_ids = lax.all_to_all(near_ids, near, 0, 0, tiled=True)  17.4 us
    ppermute x1, starting transfers between devices, on_device(): left_there = lax.ppermute(left_here, 'core', [(0, 1), (1, 0)])  12.7 us
    pallas_call x5, Pallas kernels, kernel_call(): pl.pallas_call(body, out_shape=out_shape, in_specs=specs, out_specs=tuple...  6.05 us
    all_to_all x1, starting transfers between devices, on_device(): pieces = lax.all_to_all(message, COL, 0, 0, tiled=True)  5.64 us
    ppermute x1, waiting for transfers between devices, on_device(): far = lax.ppermute(onward, ('y', 'core'), ring)  5.6 us
    all_to_all x1, starting transfers between devices, on_device(): tiles = lax.all_to_all(packed, HALF, 0, 0, tiled=True)  5.11 us
    ppermute x1, waiting for transfers between devices, on_device(): below = lax.ppermute(slab, 'y', up)  4.41 us
  transfers between devices with their start and end apart: 7, of which 6 were waited for; matrix products, arithmetic and copies ran while one was open for 1% of the time, Pallas kernels for 1%

profile of v5, /device:TPU:1, one launch (start us, length us, event | category | flops | bytes accessed | tf_op | source)
XLA Modules:
  0.0 123.8 jit_solution(4485051030510495125)
XLA Ops:
  0.0 0.7 fusion
  0.7 0.1 select_reduce_fusion
  0.8 0.6 broadcast_in_dim.23
  1.4 17.4 %all-to-all-start.1 = ((bf16[8,16,128]{2,1,0:T(8,128)(2,1)}), bf16[8,16,128]{2,1,0:T(8,128)(2,1)S(1)}, u32[]{:S(2)}, u32[]{:S(2)}) async-start(bf16[8,16,128]{2,1,0:T(8,128)(2,1)} %broadcast_in_dim.23), calls=%async_computation.1 | async-start | bytes 65536 | tf_op jit(solution)/shard_map/left_ids/all_to_all | solution.py:175
  18.8 0.1 pad_add_fusion.1.place.a
  18.9 0.0 copy-start
  18.9 0.9 copy-done
  19.8 0.0 copy-start.2
  19.8 0.7 copy-done.2
  20.5 0.0 copy-start.3
  20.5 0.7 copy-done.3
  21.1 0.6 scatter_right.1
  21.8 1.8 %all-to-all-done.1.near_ids = bf16[8,16,128]{2,1,0:T(8,128)(2,1)S(1)} async-done(((bf16[8,16,128]{2,1,0:T(8,128)(2,1)}), bf16[8,16,128]{2,1,0:T(8,128)(2,1)S(1)}, u32[]{:S(2)}, u32[]{:S(2)}) %all-to-all-start.1) | async-done | bytes 32800 | tf_op jit(solution)/shard_map/left_ids/all_to_all | solution.py:175
  23.5 0.0 copy-start.1
  23.5 0.9 copy-done.1
  24.5 42.9 %all-gather = bf16[1600,128]{1,0:T(8,128)(2,1)S(1)} all-gather(bf16[400,128]{1,0:T(8,128)(2,1)S(1)} %left_zh.1), channel_id=2, replica_groups=mesh['y'=4,'zh'=4,'core'=2,'zb'=2,'zl'=4,'x'=4] {'zh'}, dimensions={0}, use_global_device_ids=true | all-gather | bytes 512000 | tf_op jit(solution)/shard_map/left_zh/all_gather | solution.py:201
  67.4 0.8 right_message.1
  68.1 5.6 %all-to-all-start.2 = ((bf16[32,8,640]{2,1,0:T(8,128)(2,1)}), bf16[32,8,640]{2,1,0:T(8,128)(2,1)}, u32[]{:S(2)}, u32[]{:S(2)}) async-start(bf16[32,8,640]{2,1,0:T(8,128)(2,1)} %right_message.1), calls=%async_computation.2 | async-start | bytes 655360 | tf_op jit(solution)/shard_map/right_message/all_to_all | solution.py:213
  73.8 2.8 %collective-permute-start.1 = (bf16[4,400,128]{2,1,0:T(8,128)(2,1)S(1)}, bf16[4,400,128]{2,1,0:T(8,128)(2,1)S(1)}, u32[]{:S(2)}, u32[]{:S(2)}) collective-permute-start(bf16[4,400,128]{2,1,0:T(8,128)(2,1)S(1)} %bitcast.22), channel_id=1, source_target_pairs={{0,768},{256,0},{512,256},{768,512},{1,769},{257,1},{513,257},{769... | collective-permute-start | bytes 1228808 | tf_op jit(solution)/shard_map/left_y/ppermute | solution.py:221
  76.6 2.5 %collective-permute-start = (bf16[4,400,128]{2,1,0:T(8,128)(2,1)S(1)}, bf16[4,400,128]{2,1,0:T(8,128)(2,1)S(1)}, u32[]{:S(2)}, u32[]{:S(2)}) collective-permute-start(bf16[4,400,128]{2,1,0:T(8,128)(2,1)S(1)} %bitcast.23), channel_id=1, source_target_pairs={{0,256},{256,512},{512,768},{768,0},{1,257},{257,513},{513,769},{7... | collective-permute-start | bytes 1228808 | tf_op jit(solution)/shard_map/left_y/ppermute | solution.py:220
  79.1 3.4 %collective-permute-done.1.above = bf16[4,400,128]{2,1,0:T(8,128)(2,1)S(1)} collective-permute-done((bf16[4,400,128]{2,1,0:T(8,128)(2,1)S(1)}, bf16[4,400,128]{2,1,0:T(8,128)(2,1)S(1)}, u32[]{:S(2)}, u32[]{:S(2)}) %collective-permute-start.1) | collective-permute-done | bytes 409632 | tf_op jit(solution)/shard_map/left_y/ppermute | solution.py:221
  82.5 4.4 %collective-permute-done.below = bf16[4,400,128]{2,1,0:T(8,128)(2,1)S(1)} collective-permute-done((bf16[4,400,128]{2,1,0:T(8,128)(2,1)S(1)}, bf16[4,400,128]{2,1,0:T(8,128)(2,1)S(1)}, u32[]{:S(2)}, u32[]{:S(2)}) %collective-permute-start) | collective-permute-done | bytes 409632 | tf_op jit(solution)/shard_map/left_y/ppermute | solution.py:220
  86.9 1.7 %all-to-all-done.2.pieces = bf16[32,8,640]{2,1,0:T(8,128)(2,1)} async-done(((bf16[32,8,640]{2,1,0:T(8,128)(2,1)}), bf16[32,8,640]{2,1,0:T(8,128)(2,1)}, u32[]{:S(2)}, u32[]{:S(2)}) %all-to-all-start.2) | async-done | bytes 327712 | tf_op jit(solution)/shard_map/right_message/all_to_all | solution.py:213
  88.5 2.7 %right_needed.1 = (bf16[16,32,512]{2,1,0:T(8,128)(2,1)}, s32[16,128]{1,0:T(8,128)S(1)}) custom-call(s32[3]{0:T(128)S(1)} %pad_add_fusion.1.place.a, bf16[32,8,640]{2,1,0:T(8,128)(2,1)} %all-to-all-done.2.pieces, bf16[4,400,128]{2,1,0:T(8,128)(2,1)S(1)} %collective-permute-done.below, bf16[4,400,128]{2,1,0:T(8,128)(2,1)S(1)} %collective-permute-done.1.above), custom_call_target="tpu_custom_call" | custom-call | tf_op jit(solution)/shard_map/right_needed/pallas_call | solution.py:153
  91.2 5.1 %all-to-all-start.3 = ((bf16[16,32,512]{2,1,0:T(8,128)(2,1)}), bf16[16,32,512]{2,1,0:T(8,128)(2,1)S(1)}, u32[]{:S(2)}, u32[]{:S(2)}) async-start(bf16[16,32,512]{2,1,0:T(8,128)(2,1)} %get-tuple-element.103), calls=%async_computation.3 | async-start | bytes 1048576 | tf_op jit(solution)/shard_map/right_needed/all_to_all | solution.py:260
  96.4 3.1 %collective-permute-start.2 = (bf16[4,400,128]{2,1,0:T(8,128)(2,1)S(1)}, bf16[4,400,128]{2,1,0:T(8,128)(2,1)S(1)}, u32[]{:S(2)}, u32[]{:S(2)}) collective-permute-start(bf16[4,400,128]{2,1,0:T(8,128)(2,1)S(1)} %broadcast_select_fusion), channel_id=1, source_target_pairs={{0,256},{32,800},{256,512},{288,32},{512,768},{544,288},{768,0},{8... | collective-permute-start | bytes 1228808 | tf_op jit(solution)/shard_map/left_y/ppermute | solution.py:223
  99.5 5.6 %collective-permute-done.2 = bf16[4,400,128]{2,1,0:T(8,128)(2,1)S(1)} collective-permute-done((bf16[4,400,128]{2,1,0:T(8,128)(2,1)S(1)}, bf16[4,400,128]{2,1,0:T(8,128)(2,1)S(1)}, u32[]{:S(2)}, u32[]{:S(2)}) %collective-permute-start.2) | collective-permute-done | bytes 409632 | tf_op jit(solution)/shard_map/left_y/ppermute | solution.py:223
  105.1 0.2 pad_maximum_fusion.c
  105.3 12.7 %collective-permute-start.3 = (bf16[16,400,128]{2,1,0:T(8,128)(2,1)S(1)}, bf16[16,400,128]{2,1,0:T(8,128)(2,1)}, u32[]{:S(2)}, u32[]{:S(2)}) collective-permute-start(bf16[16,400,128]{2,1,0:T(8,128)(2,1)S(1)} %pad_maximum_fusion.c), channel_id=1, source_target_pairs={{0,32},{32,0},{1,33},{33,1},{2,34},{34,2},{3,35},{35,3},{4,36},{36... | collective-permute-start | bytes 4915208 | tf_op jit(solution)/shard_map/left_core/ppermute | solution.py:227
  118.0 0.6 slice.11
  119.2 2.0 %collective-permute-done.3.d = bf16[16,400,128]{2,1,0:T(8,128)(2,1)} collective-permute-done((bf16[16,400,128]{2,1,0:T(8,128)(2,1)S(1)}, bf16[16,400,128]{2,1,0:T(8,128)(2,1)}, u32[]{:S(2)}, u32[]{:S(2)}) %collective-permute-start.3) | collective-permute-done | bytes 1638432 | tf_op jit(solution)/shard_map/left_core/ppermute | solution.py:227
  121.2 0.0 all-to-all-done.3.e
  121.2 1.9 %multiply.1 = bf16[128,512]{1,0:T(8,128)(2,1)S(1)} custom-call(s32[3]{0:T(128)S(1)} %pad_add_fusion.1.place.a, s32[16,128]{1,0:T(8,128)S(1)} %get-tuple-element.102.b, bf16[16,400,128]{2,1,0:T(8,128)(2,1)S(1)} %pad_maximum_fusion.c, bf16[16,400,128]{2,1,0:T(8,128)(2,1)} %collective-permute-done.3.d, bf16[16,32,512]{2,1,0:T(8,128)(2,1)S(1)} %all-to-all-done.3.e), custom_call_target="tpu_custom_call" | custom-call | tf_op jit(solution)/shard_map/multiply/pallas_call | solution.py:153
  123.2 0.0 copy-start.4
  123.2 0.6 copy-done.4
  (6 shorter events, 0.1 us)
Async XLA Ops:
  1.4 22.1 %all-to-all-start.1 = ((bf16[8,16,128]{2,1,0:T(8,128)(2,1)}), bf16[8,16,128]{2,1,0:T(8,128)(2,1)S(1)}, u32[]{:S(2)}, u32[]{:S(2)}) async-start(bf16[8,16,128]{2,1,0:T(8,128)(2,1)} %broadcast_in_dim.23), calls=%async_computation.1 | async-start | bytes 65536 | tf_op jit(solution)/shard_map/left_ids/all_to_all | solution.py:175
  18.9 0.9 copy-start
  19.8 0.7 copy-start.2
  20.5 0.7 copy-start.3
  23.5 0.9 copy-start.1
  68.1 20.4 %all-to-all-start.2 = ((bf16[32,8,640]{2,1,0:T(8,128)(2,1)}), bf16[32,8,640]{2,1,0:T(8,128)(2,1)}, u32[]{:S(2)}, u32[]{:S(2)}) async-start(bf16[32,8,640]{2,1,0:T(8,128)(2,1)} %right_message.1), calls=%async_computation.2 | async-start | bytes 655360 | tf_op jit(solution)/shard_map/right_message/all_to_all | solution.py:213
  73.8 8.7 %collective-permute-start.1 = (bf16[4,400,128]{2,1,0:T(8,128)(2,1)S(1)}, bf16[4,400,128]{2,1,0:T(8,128)(2,1)S(1)}, u32[]{:S(2)}, u32[]{:S(2)}) collective-permute-start(bf16[4,400,128]{2,1,0:T(8,128)(2,1)S(1)} %bitcast.22), channel_id=1, source_target_pairs={{0,768},{256,0},{512,256},{768,512},{1,769},{257,1},{513,257},{769... | collective-permute-start | bytes 1228808 | tf_op jit(solution)/shard_map/left_y/ppermute | solution.py:221
  76.6 10.3 %collective-permute-start = (bf16[4,400,128]{2,1,0:T(8,128)(2,1)S(1)}, bf16[4,400,128]{2,1,0:T(8,128)(2,1)S(1)}, u32[]{:S(2)}, u32[]{:S(2)}) collective-permute-start(bf16[4,400,128]{2,1,0:T(8,128)(2,1)S(1)} %bitcast.23), channel_id=1, source_target_pairs={{0,256},{256,512},{512,768},{768,0},{1,257},{257,513},{513,769},{7... | collective-permute-start | bytes 1228808 | tf_op jit(solution)/shard_map/left_y/ppermute | solution.py:220
  91.2 30.0 %all-to-all-start.3 = ((bf16[16,32,512]{2,1,0:T(8,128)(2,1)}), bf16[16,32,512]{2,1,0:T(8,128)(2,1)S(1)}, u32[]{:S(2)}, u32[]{:S(2)}) async-start(bf16[16,32,512]{2,1,0:T(8,128)(2,1)} %get-tuple-element.103), calls=%async_computation.3 | async-start | bytes 1048576 | tf_op jit(solution)/shard_map/right_needed/all_to_all | solution.py:260
  96.4 8.7 %collective-permute-start.2 = (bf16[4,400,128]{2,1,0:T(8,128)(2,1)S(1)}, bf16[4,400,128]{2,1,0:T(8,128)(2,1)S(1)}, u32[]{:S(2)}, u32[]{:S(2)}) collective-permute-start(bf16[4,400,128]{2,1,0:T(8,128)(2,1)S(1)} %broadcast_select_fusion), channel_id=1, source_target_pairs={{0,256},{32,800},{256,512},{288,32},{512,768},{544,288},{768,0},{8... | collective-permute-start | bytes 1228808 | tf_op jit(solution)/shard_map/left_y/ppermute | solution.py:223
  105.3 15.9 %collective-permute-start.3 = (bf16[16,400,128]{2,1,0:T(8,128)(2,1)S(1)}, bf16[16,400,128]{2,1,0:T(8,128)(2,1)}, u32[]{:S(2)}, u32[]{:S(2)}) collective-permute-start(bf16[16,400,128]{2,1,0:T(8,128)(2,1)S(1)} %pad_maximum_fusion.c), channel_id=1, source_target_pairs={{0,32},{32,0},{1,33},{33,1},{2,34},{34,2},{3,35},{35,3},{4,36},{36... | collective-permute-start | bytes 4915208 | tf_op jit(solution)/shard_map/left_core/ppermute | solution.py:227
  123.2 0.7 copy-start.4

commit v6 on v5

--- a/solution.py
+++ b/solution.py
@@ -20,7 +20,7 @@
 PIECE = TILE // SPREAD // WIDE
 MSG = RIGHT * PIECE
 PANEL = LEFT * TILE
-IDS = 16
+IDS = 8
 F32, BF16, I32 = jnp.float32, jnp.bfloat16, jnp.int32
 VMEM_LIMIT = 48 * 1024 * 1024
 

time: 125 us -> 125 us (level)
  starting transfers between devices: 49.2 us -> 47.8 us
    ppermute x1, starting transfers between devices: 12.7 us -> 11 us  [on_device(): left_there = lax.ppermute(left_here, 'core', [(0, 1), (1, 0)])]
    unnamed x10 -> x12, local copies, waits for them, and re-layouts: 3.78 us -> 3.78 us
  transfers between devices with their start and end apart: 7 -> 7, of which waited for: 6 -> 6; matrix products, arithmetic and copies ran while one was open for 1% -> 2% of each run, Pallas kernels for 1% -> 1%
where the time goes in v6:
time: 125 us; the launch traced here: 123 us
  starting transfers between devices  47.8 us (38%)
  blocking collectives  43 us (34%)
  waiting for transfers between devices  19 us (15%)
  Pallas kernels  5.66 us (5%)
  local copies, waits for them, and re-layouts  4.98 us (4%)
  other arithmetic  2.11 us (2%)
    all_gather x1, blocking collectives, on_device(): slab = lax.all_gather(payload, 'zh')  43 us
    all_to_all x1, starting transfers between devices, on_device(): near_ids = lax.all_to_all(near_ids, near, 0, 0, tiled=True)  17.4 us
    ppermute x1, starting transfers between devices, on_device(): left_there = lax.ppermute(left_here, 'core', [(0, 1), (1, 0)])  11 us
    all_to_all x1, starting transfers between devices, on_device(): pieces = lax.all_to_all(message, COL, 0, 0, tiled=True)  5.97 us
    ppermute x1, waiting for transfers between devices, on_device(): far = lax.ppermute(onward, ('y', 'core'), ring)  5.9 us
    pallas_call x5, Pallas kernels, kernel_call(): pl.pallas_call(body, out_shape=out_shape, in_specs=specs, out_specs=tuple...  5.66 us
    all_to_all x1, starting transfers between devices, on_device(): tiles = lax.all_to_all(packed, HALF, 0, 0, tiled=True)  5.42 us
    ppermute x1, waiting for transfers between devices, on_device(): below = lax.ppermute(slab, 'y', up)  3.93 us
  transfers between devices with their start and end apart: 7, of which 6 were waited for; matrix products, arithmetic and copies ran while one was open for 2% of the time, Pallas kernels for 1%

profile of v6, /device:TPU:1, one launch (start us, length us, event | category | flops | bytes accessed | tf_op | source)
XLA Modules:
  0.0 123.3 jit_solution(3644916050402967157)
XLA Ops:
  0.0 0.7 fusion
  0.7 0.1 select_reduce_fusion
  0.8 0.6 broadcast_in_dim.23
  1.4 17.4 %all-to-all-start.1 = ((bf16[8,8,128]{2,1,0:T(8,128)(2,1)}), bf16[8,8,128]{2,1,0:T(8,128)(2,1)S(1)}, u32[]{:S(2)}, u32[]{:S(2)}) async-start(bf16[8,8,128]{2,1,0:T(8,128)(2,1)} %broadcast_in_dim.23), calls=%async_computation.1 | async-start | bytes 32768 | tf_op jit(solution)/shard_map/left_ids/all_to_all | solution.py:175
  18.8 0.1 pad_add_fusion.1.place.a
  18.9 0.0 copy-start
  18.9 0.9 copy-done
  19.8 0.0 copy-start.2
  19.8 0.7 copy-done.2
  20.5 0.0 copy-start.3
  20.5 0.7 copy-done.3
  21.1 0.6 scatter_right.1
  21.7 1.7 %all-to-all-done.1.near_ids = bf16[8,8,128]{2,1,0:T(8,128)(2,1)S(1)} async-done(((bf16[8,8,128]{2,1,0:T(8,128)(2,1)}), bf16[8,8,128]{2,1,0:T(8,128)(2,1)S(1)}, u32[]{:S(2)}, u32[]{:S(2)}) %all-to-all-start.1) | async-done | bytes 16416 | tf_op jit(solution)/shard_map/left_ids/all_to_all | solution.py:175
  23.5 0.0 copy-start.1
  23.5 0.9 copy-done.1
  24.4 43.0 %all-gather = bf16[1568,128]{1,0:T(8,128)(2,1)S(1)} all-gather(bf16[392,128]{1,0:T(8,128)(2,1)S(1)} %left_zh.1), channel_id=2, replica_groups=mesh['y'=4,'zh'=4,'core'=2,'zb'=2,'zl'=4,'x'=4] {'zh'}, dimensions={0}, use_global_device_ids=true | all-gather | bytes 501760 | tf_op jit(solution)/shard_map/left_zh/all_gather | solution.py:201
  67.4 0.0 copy-start.4
  67.4 0.8 right_message.1
  68.2 6.0 %all-to-all-start.2 = ((bf16[32,8,640]{2,1,0:T(8,128)(2,1)}), bf16[32,8,640]{2,1,0:T(8,128)(2,1)S(1)}, u32[]{:S(2)}, u32[]{:S(2)}) async-start(bf16[32,8,640]{2,1,0:T(8,128)(2,1)} %right_message.1), calls=%async_computation.2 | async-start | bytes 655360 | tf_op jit(solution)/shard_map/right_message/all_to_all | solution.py:213
  74.2 2.7 %collective-permute-start.1 = (bf16[4,392,128]{2,1,0:T(8,128)(2,1)S(1)}, bf16[4,392,128]{2,1,0:T(8,128)(2,1)S(1)}, u32[]{:S(2)}, u32[]{:S(2)}) collective-permute-start(bf16[4,392,128]{2,1,0:T(8,128)(2,1)S(1)} %bitcast.22), channel_id=1, source_target_pairs={{0,768},{256,0},{512,256},{768,512},{1,769},{257,1},{513,257},{769... | collective-permute-start | bytes 1204232 | tf_op jit(solution)/shard_map/left_y/ppermute | solution.py:221
  76.9 2.6 %collective-permute-start = (bf16[4,392,128]{2,1,0:T(8,128)(2,1)S(1)}, bf16[4,392,128]{2,1,0:T(8,128)(2,1)S(1)}, u32[]{:S(2)}, u32[]{:S(2)}) collective-permute-start(bf16[4,392,128]{2,1,0:T(8,128)(2,1)S(1)} %bitcast.23), channel_id=1, source_target_pairs={{0,256},{256,512},{512,768},{768,0},{1,257},{257,513},{513,769},{7... | collective-permute-start | bytes 1204232 | tf_op jit(solution)/shard_map/left_y/ppermute | solution.py:220
  79.5 3.6 %collective-permute-done.1.above = bf16[4,392,128]{2,1,0:T(8,128)(2,1)S(1)} collective-permute-done((bf16[4,392,128]{2,1,0:T(8,128)(2,1)S(1)}, bf16[4,392,128]{2,1,0:T(8,128)(2,1)S(1)}, u32[]{:S(2)}, u32[]{:S(2)}) %collective-permute-start.1) | collective-permute-done | bytes 401440 | tf_op jit(solution)/shard_map/left_y/ppermute | solution.py:221
  83.1 3.9 %collective-permute-done.below = bf16[4,392,128]{2,1,0:T(8,128)(2,1)S(1)} collective-permute-done((bf16[4,392,128]{2,1,0:T(8,128)(2,1)S(1)}, bf16[4,392,128]{2,1,0:T(8,128)(2,1)S(1)}, u32[]{:S(2)}, u32[]{:S(2)}) %collective-permute-start) | collective-permute-done | bytes 401440 | tf_op jit(solution)/shard_map/left_y/ppermute | solution.py:220
  87.0 0.0 copy-done.4
  87.0 1.9 %all-to-all-done.2.pieces = bf16[32,8,640]{2,1,0:T(8,128)(2,1)S(1)} async-done(((bf16[32,8,640]{2,1,0:T(8,128)(2,1)}), bf16[32,8,640]{2,1,0:T(8,128)(2,1)S(1)}, u32[]{:S(2)}, u32[]{:S(2)}) %all-to-all-start.2) | async-done | bytes 327712 | tf_op jit(solution)/shard_map/right_message/all_to_all | solution.py:213
  89.0 2.3 %right_needed.1 = (bf16[16,32,512]{2,1,0:T(8,128)(2,1)}, s32[16,128]{1,0:T(8,128)S(1)}) custom-call(s32[3]{0:T(128)S(1)} %pad_add_fusion.1.place.a, bf16[32,8,640]{2,1,0:T(8,128)(2,1)S(1)} %all-to-all-done.2.pieces, bf16[4,392,128]{2,1,0:T(8,128)(2,1)S(1)} %collective-permute-done.below, bf16[4,392,128]{2,1,0:T(8,128)(2,1)S(1)} %collective-permute-done.1.above), custom_call_target="tpu_custom_call" | custom-call | tf_op jit(solution)/shard_map/right_needed/pallas_call | solution.py:153
  91.2 5.4 %all-to-all-start.3 = ((bf16[16,32,512]{2,1,0:T(8,128)(2,1)}), bf16[16,32,512]{2,1,0:T(8,128)(2,1)S(1)}, u32[]{:S(2)}, u32[]{:S(2)}) async-start(bf16[16,32,512]{2,1,0:T(8,128)(2,1)} %get-tuple-element.103), calls=%async_computation.3 | async-start | bytes 1048576 | tf_op jit(solution)/shard_map/right_needed/all_to_all | solution.py:260
  96.7 0.1 broadcast_select_fusion
  96.7 2.7 %collective-permute-start.2 = (bf16[4,392,128]{2,1,0:T(8,128)(2,1)S(1)}, bf16[4,392,128]{2,1,0:T(8,128)(2,1)S(1)}, u32[]{:S(2)}, u32[]{:S(2)}) collective-permute-start(bf16[4,392,128]{2,1,0:T(8,128)(2,1)S(1)} %broadcast_select_fusion), channel_id=1, source_target_pairs={{0,256},{32,800},{256,512},{288,32},{512,768},{544,288},{768,0},{8... | collective-permute-start | bytes 1204232 | tf_op jit(solution)/shard_map/left_y/ppermute | solution.py:223
  99.4 5.9 %collective-permute-done.2 = bf16[4,392,128]{2,1,0:T(8,128)(2,1)S(1)} collective-permute-done((bf16[4,392,128]{2,1,0:T(8,128)(2,1)S(1)}, bf16[4,392,128]{2,1,0:T(8,128)(2,1)S(1)}, u32[]{:S(2)}, u32[]{:S(2)}) %collective-permute-start.2) | collective-permute-done | bytes 401440 | tf_op jit(solution)/shard_map/left_y/ppermute | solution.py:223
  105.3 1.2 pad_maximum_fusion.c
  106.5 11.0 %collective-permute-start.3 = (bf16[16,392,128]{2,1,0:T(8,128)(2,1)S(1)}, bf16[16,392,128]{2,1,0:T(8,128)(2,1)}, u32[]{:S(2)}, u32[]{:S(2)}) collective-permute-start(bf16[16,392,128]{2,1,0:T(8,128)(2,1)S(1)} %pad_maximum_fusion.c), channel_id=1, source_target_pairs={{0,32},{32,0},{1,33},{33,1},{2,34},{34,2},{3,35},{35,3},{4,36},{36... | collective-permute-start | bytes 4816904 | tf_op jit(solution)/shard_map/left_core/ppermute | solution.py:227
  117.6 0.6 slice.11
  118.8 2.0 %collective-permute-done.3.d = bf16[16,392,128]{2,1,0:T(8,128)(2,1)} collective-permute-done((bf16[16,392,128]{2,1,0:T(8,128)(2,1)S(1)}, bf16[16,392,128]{2,1,0:T(8,128)(2,1)}, u32[]{:S(2)}, u32[]{:S(2)}) %collective-permute-start.3) | collective-permute-done | bytes 1605664 | tf_op jit(solution)/shard_map/left_core/ppermute | solution.py:227
  120.8 0.0 all-to-all-done.3.e
  120.8 1.9 %multiply.1 = bf16[128,512]{1,0:T(8,128)(2,1)S(1)} custom-call(s32[3]{0:T(128)S(1)} %pad_add_fusion.1.place.a, s32[16,128]{1,0:T(8,128)S(1)} %get-tuple-element.102.b, bf16[16,392,128]{2,1,0:T(8,128)(2,1)S(1)} %pad_maximum_fusion.c, bf16[16,392,128]{2,1,0:T(8,128)(2,1)} %collective-permute-done.3.d, bf16[16,32,512]{2,1,0:T(8,128)(2,1)S(1)} %all-to-all-done.3.e), custom_call_target="tpu_custom_call" | custom-call | tf_op jit(solution)/shard_map/multiply/pallas_call | solution.py:153
  122.7 0.0 copy-start.5
  122.7 0.6 copy-done.5
  (5 shorter events, 0.0 us)
Async XLA Ops:
  1.4 22.1 %all-to-all-start.1 = ((bf16[8,8,128]{2,1,0:T(8,128)(2,1)}), bf16[8,8,128]{2,1,0:T(8,128)(2,1)S(1)}, u32[]{:S(2)}, u32[]{:S(2)}) async-start(bf16[8,8,128]{2,1,0:T(8,128)(2,1)} %broadcast_in_dim.23), calls=%async_computation.1 | async-start | bytes 32768 | tf_op jit(solution)/shard_map/left_ids/all_to_all | solution.py:175
  18.9 0.9 copy-start
  19.8 0.7 copy-start.2
  20.5 0.7 copy-start.3
  23.5 0.9 copy-start.1
  67.4 19.7 %copy-start.4 = (bf16[1568,128]{1,0:T(8,128)(2,1)}, bf16[1568,128]{1,0:T(8,128)(2,1)S(1)}, u32[]{:S(2)}) copy-start(bf16[1568,128]{1,0:T(8,128)(2,1)S(1)} %all-gather) | copy-start | bytes 1204228
  68.2 20.7 %all-to-all-start.2 = ((bf16[32,8,640]{2,1,0:T(8,128)(2,1)}), bf16[32,8,640]{2,1,0:T(8,128)(2,1)S(1)}, u32[]{:S(2)}, u32[]{:S(2)}) async-start(bf16[32,8,640]{2,1,0:T(8,128)(2,1)} %right_message.1), calls=%async_computation.2 | async-start | bytes 655360 | tf_op jit(solution)/shard_map/right_message/all_to_all | solution.py:213
  74.2 8.9 %collective-permute-start.1 = (bf16[4,392,128]{2,1,0:T(8,128)(2,1)S(1)}, bf16[4,392,128]{2,1,0:T(8,128)(2,1)S(1)}, u32[]{:S(2)}, u32[]{:S(2)}) collective-permute-start(bf16[4,392,128]{2,1,0:T(8,128)(2,1)S(1)} %bitcast.22), channel_id=1, source_target_pairs={{0,768},{256,0},{512,256},{768,512},{1,769},{257,1},{513,257},{769... | collective-permute-start | bytes 1204232 | tf_op jit(solution)/shard_map/left_y/ppermute | solution.py:221
  76.9 10.1 %collective-permute-start = (bf16[4,392,128]{2,1,0:T(8,128)(2,1)S(1)}, bf16[4,392,128]{2,1,0:T(8,128)(2,1)S(1)}, u32[]{:S(2)}, u32[]{:S(2)}) collective-permute-start(bf16[4,392,128]{2,1,0:T(8,128)(2,1)S(1)} %bitcast.23), channel_id=1, source_target_pairs={{0,256},{256,512},{512,768},{768,0},{1,257},{257,513},{513,769},{7... | collective-permute-start | bytes 1204232 | tf_op jit(solution)/shard_map/left_y/ppermute | solution.py:220
  91.2 29.5 %all-to-all-start.3 = ((bf16[16,32,512]{2,1,0:T(8,128)(2,1)}), bf16[16,32,512]{2,1,0:T(8,128)(2,1)S(1)}, u32[]{:S(2)}, u32[]{:S(2)}) async-start(bf16[16,32,512]{2,1,0:T(8,128)(2,1)} %get-tuple-element.103), calls=%async_computation.3 | async-start | bytes 1048576 | tf_op jit(solution)/shard_map/right_needed/all_to_all | solution.py:260
  96.7 8.6 %collective-permute-start.2 = (bf16[4,392,128]{2,1,0:T(8,128)(2,1)S(1)}, bf16[4,392,128]{2,1,0:T(8,128)(2,1)S(1)}, u32[]{:S(2)}, u32[]{:S(2)}) collective-permute-start(bf16[4,392,128]{2,1,0:T(8,128)(2,1)S(1)} %broadcast_select_fusion), channel_id=1, source_target_pairs={{0,256},{32,800},{256,512},{288,32},{512,768},{544,288},{768,0},{8... | collective-permute-start | bytes 1204232 | tf_op jit(solution)/shard_map/left_y/ppermute | solution.py:223
  106.5 14.2 %collective-permute-start.3 = (bf16[16,392,128]{2,1,0:T(8,128)(2,1)S(1)}, bf16[16,392,128]{2,1,0:T(8,128)(2,1)}, u32[]{:S(2)}, u32[]{:S(2)}) collective-permute-start(bf16[16,392,128]{2,1,0:T(8,128)(2,1)S(1)} %pad_maximum_fusion.c), channel_id=1, source_target_pairs={{0,32},{32,0},{1,33},{33,1},{2,34},{34,2},{3,35},{35,3},{4,36},{36... | collective-permute-start | bytes 4816904 | tf_op jit(solution)/shard_map/left_core/ppermute | solution.py:227
  122.7 0.7 copy-start.5
